TPU v7x, 256 devices: a whole 4x4x8 slice. The times are simulated.
256 devices in a mesh: chan: 32 (over x_lo, z, core), stack: 8 (over x_hi, y).
Axes of the slice: x: 4 (x_hi: 2, x_lo: 2; x = x_hi * 2 + x_lo), y: 4, z: 8, core: 2. Of those that a mesh axis runs over, the one named last changes fastest.
Arguments:
- strain: bfloat16 [16, 256, 1024], P(None, 'chan', 'stack'), may hold values from -6 to 6
- sources: int32 [16, 512], P(None, 'stack'), may hold values from 0 to 255
Outputs:
- correlations: float32 [512, 256, 2048], P('stack', 'chan')
All inputs are finite; a program needn't handle non-finite values.
Results may differ from a plain program's by a relative error of at most 0.0054.
Values may be sent and summed in bfloat16 or wider, within the bound.
No kernel may reach another device: no remote copies, remote signals or barrier semaphores. Data moves between devices by JAX's collectives and lax.ppermute only.
A program may use at most 64 MiB of HBM per device.

v0:
```python
import math

import jax
import jax.numpy as jnp
from jax import lax
from jax.sharding import PartitionSpec as P

NS = 1024


def unpack(packed, half):
    real_part = packed[..., : half + 1]
    edge = jnp.zeros(packed.shape[:-1] + (1,), jnp.float32)
    imag_part = jnp.concatenate([edge, packed[..., half + 1 :], edge], axis=-1)
    return (real_part, imag_part)


def pack(real_part, imag_part, half):
    return jnp.concatenate([real_part, imag_part[..., 1:half]], axis=-1)


def whiten(spectra, half):
    real_part, imag_part = unpack(spectra, half)
    power = real_part * real_part + imag_part * imag_part
    level = jnp.mean(power, axis=-1, keepdims=True)
    factor = 1.0 / jnp.sqrt(power + 0.05 * level + 1e-06)
    return pack(real_part * factor, imag_part * factor, half)


def forward_table(half):
    width = 2 * half
    times = jnp.arange(half, dtype=jnp.int32)[:, None]
    cols = jnp.arange(width, dtype=jnp.int32)[None, :]
    freq = jnp.where(cols <= half, cols, cols - half)
    phase = jnp.mod(freq * times, width).astype(jnp.float32) * (2.0 * math.pi / width)
    return jnp.where(cols <= half, jnp.cos(phase), -jnp.sin(phase))


def lag_table(half):
    width = 2 * half
    rows = jnp.arange(width, dtype=jnp.int32)[:, None]
    lags = jnp.arange(width, dtype=jnp.int32)[None, :] - half
    freq = jnp.where(rows <= half, rows, rows - half)
    phase = jnp.mod(freq * lags, width).astype(jnp.float32) * (2.0 * math.pi / width)
    weight = jnp.where((freq == 0) | (freq == half), 1.0, 2.0)
    values = jnp.where(rows <= half, weight * jnp.cos(phase), -2.0 * jnp.sin(phase))
    return (values / math.sqrt(width)).astype(jnp.bfloat16)


def stacked_cross(panel, white, half):
    panel_re, panel_im = unpack(panel.astype(jnp.float32), half)
    chan_re, chan_im = unpack(white.astype(jnp.float32), half)
    cross_re = jnp.mean(
        panel_re[:, :, None] * chan_re[:, None] + panel_im[:, :, None] * chan_im[:, None], axis=0
    )
    cross_im = jnp.mean(
        panel_re[:, :, None] * chan_im[:, None] - panel_im[:, :, None] * chan_re[:, None], axis=0
    )
    return pack(cross_re, cross_im, half)


def local(strain, sources):
    windows, chan_rows, local_samples = strain.shape
    half = NS
    width = 2 * NS
    table = forward_table(half)
    empty = jnp.zeros((windows, chan_rows, width), jnp.float32)
    piece = lax.all_gather(strain, "stack", axis=2, tiled=True)
    count = piece.shape[2]
    flat = piece.astype(jnp.float32).reshape(-1, count)
    term = jnp.dot(flat, table, precision=lax.Precision.HIGHEST, preferred_element_type=jnp.float32)
    spectra = term.reshape(empty.shape)
    white = whiten(spectra, half).astype(jnp.bfloat16)
    source_count = sources.shape[1]
    piece = lax.all_gather(white, "chan", axis=1, tiled=True)
    count = piece.shape[1]
    hits = (sources[:, :, None] == jnp.arange(count, dtype=jnp.int32)[None, None, :]).astype(
        jnp.bfloat16
    )
    panel = jnp.einsum("wsc,wcf->wsf", hits, piece, preferred_element_type=jnp.float32)
    panel = panel.astype(jnp.bfloat16)
    cross = stacked_cross(panel, white, half).astype(jnp.bfloat16)
    lags = lag_table(half)
    result = jnp.dot(cross.reshape(-1, width), lags, preferred_element_type=jnp.float32)
    return result.reshape(source_count, chan_rows, width)


def solution(mesh):
    placed = (P(None, "chan", "stack"), P(None, "stack"))
    return jax.shard_map(
        local, mesh=mesh, in_specs=placed, out_specs=P("stack", "chan", None), check_vma=False
    )
```

profile of v0, /device:TPU:1, one launch (start us, length us, event | category | flops | bytes accessed | tf_op | source)
XLA Modules:
  0.0 299.6 jit_solution(8166940422896248831)
XLA Ops:
  6.5 0.0 all-gather.2.cloned.1.call-start
  6.5 0.0 copy-start.2
  6.6 27.4 %all_gather.6 = bf16[16,8,1024]{2,1,0:T(8,128)(2,1)S(1)} all-gather(bf16[16,8,128]{2,1,0:T(8,128)(2,1)} %param.2), channel_id=1, replica_groups=mesh['chan'=32,'stack'=8] {'stack'}, dimensions={2}, use_global_device_ids=true | all-gather | bytes 294912 | tf_op jit(solution)/shard_map/all_gather | solution.py:68
  34.0 0.0 copy-done.2
  34.0 37.7 %fusion.35 = f32[16,8,2048]{2,1,0:T(8,128)S(1)} fusion(s32[2048]{0:T(1024)S(1)} %iota_select_fusion, pred[2048]{0:T(1024)(128)(4,1)S(1)} %iota_compare_fusion.2, bf16[16,8,1024]{2,1,0:T(8,128)(2,1)S(1)} %all_gather.6), kind=kOutput, calls=%fused_computation.44 | convolution fusion | flops 3254779904 | bytes 1320960 | tf_op jit(solution)/shard_map/dot_general | solution.py:71
  71.7 0.0 copy-start
  71.8 0.2 slice.35
  72.0 0.3 concatenate.19
  72.3 0.2 fusion.45
  72.4 0.2 multiply_convert_fusion.2
  72.6 0.3 fusion.42
  73.0 0.9 pad_maximum_fusion
  73.9 0.0 all-gather.2.cloned.1.call-update
  73.9 1.1 slice.41
  75.0 1.0 slice.39
  76.0 0.3 concatenate.22
  76.3 0.6 or_select_fusion
  76.9 102.1 %all-gather.2.cloned.1.call-done = bf16[16,256,2048]{2,1,0:T(8,128)(2,1)} async-done(((bf16[16,8,2048]{2,1,0:T(8,128)(2,1)}), bf16[16,256,2048]{2,1,0:T(8,128)(2,1)}) %all-gather.2.cloned.1.call-update) | async-done | bytes 16777232 | tf_op jit(solution)/shard_map/all_gather | solution.py:75
  179.0 0.0 copy-done
  179.0 7.4 %convert_convert_fusion = f32[16,64,2048]{2,1,0:T(8,128)S(1)} fusion(bf16[16,256,2048]{2,1,0:T(8,128)(2,1)} %all-gather.2.cloned.1.call-done, s32[16,64]{1,0:T(8,128)S(1)} %copy-done), kind=kOutput, calls=%fused_computation.37 | convolution fusion | flops 1078198272 | bytes 25169920 | tf_op jit(solution)/shard_map/wsc,wcf->wsf/dot_general | solution.py:80
  186.4 3.2 %slice.40 = f32[16,64,1023]{2,1,0:T(8,128)} slice(f32[16,64,2048]{2,1,0:T(8,128)S(1)} %convert_convert_fusion), slice={[0:16], [0:64], [1025:2048]} | slice | bytes 8380416 | tf_op jit(solution)/shard_map/slice | solution.py:14
  189.6 2.6 slice.38
  192.2 6.4 %concatenate.21 = f32[16,64,1025]{2,1,0:T(8,128)} concatenate(f32[16,64,1]{2,1,0:T(8,128)S(1)} %broadcast_in_dim.22, f32[16,64,1023]{2,1,0:T(8,128)} %slice.40, f32[16,64,1]{2,1,0:T(8,128)S(1)} %broadcast_in_dim.22), dimensions={2} | concatenate | bytes 8396800 | tf_op jit(solution)/shard_map/concatenate | solution.py:14
  198.6 16.3 %add_reduce_fusion = (f32[64,8,1025]{2,1,0:T(8,128)S(1)}, f32[64,8,1025]{2,1,0:T(8,128)}) fusion(f32[16,8,1025]{2,1,0:T(8,128)S(1)} %concatenate.22, f32[16,64,1025]{2,1,0:T(8,128)} %concatenate.21, f32[16,8,1025]{2,1,0:T(8,128)S(1)} %slice.39, f32[16,64,1025]{2,1,0:T(8,128)} %slice.38), kind=kLoop, calls=%fused_computation.1 | loop fusion | flops 66124800 | bytes 13644800 | tf_op jit(solution)/shard_map/reduce_sum | solution.py:53
  215.0 0.0 copy-start.1
  215.0 0.0 copy-start.3
  215.0 0.1 multiply_convert_fusion.1
  215.1 2.3 fusion.38
  217.4 0.6 fusion.67
  218.1 0.0 copy-done.1
  218.1 0.0 copy-done.3
  218.1 74.7 %fusion.4 = f32[64,8,2048]{2,1,0:T(8,128)} fusion(s32[2048]{0:T(1024)S(1)} %iota_add_fusion, s32[2048]{0:T(1024)S(1)} %iota_select_fusion, f32[2048]{0:T(1024)S(1)} %copy-done.1, pred[2048]{0:T(1024)(128)(4,1)S(1)} %copy-done.3, bf16[64,8,2048]{2,1,0:T(8,128)(2,1)S(1)} %fusion.67), kind=kOutput, calls=%fused_computation.15 | convolution fusion | flops 4374659072 | bytes 6318080 | tf_op jit(solution)/shard_map/dot_general | solution.py:84
  (6 shorter events, 0.1 us)
Async XLA Ops:
  6.5 172.5 %all-gather.2.cloned.1.call-start = ((), (), s32[]{:S(2)}) async-start(), calls=%async_computation | async-start | bytes 17301504 | tf_op jit(solution)/shard_map/all_gather | solution.py:75
  6.5 27.4 %copy-start.2 = (pred[2048]{0:T(1024)(128)(4,1)}, pred[2048]{0:T(1024)(128)(4,1)S(1)}, u32[]{:S(2)}) copy-start(pred[2048]{0:T(1024)(128)(4,1)S(1)} %iota_compare_fusion.2) | copy-start | bytes 6148
  71.7 107.3 %copy-start = (s32[16,64]{1,0:T(8,128)S(1)}, s32[16,64]{1,0:T(8,128)}, u32[]{:S(2)}) copy-start(s32[16,64]{1,0:T(8,128)} %param.3) | copy-start | bytes 12292
  215.0 3.1 %copy-start.1 = (f32[2048]{0:T(1024)S(1)}, f32[2048]{0:T(1024)}, u32[]{:S(2)}) copy-start(f32[2048]{0:T(1024)} %or_select_fusion) | copy-start | bytes 24580
  215.0 3.1 %copy-start.3 = (pred[2048]{0:T(1024)(128)(4,1)S(1)}, pred[2048]{0:T(1024)(128)(4,1)}, u32[]{:S(2)}) copy-start(pred[2048]{0:T(1024)(128)(4,1)} %copy-done.2) | copy-start | bytes 6148
Sparse Core Ops, SparseCore 0:
  74.0 104.9 all-gather.1
where the time goes:
time: 300 us
  matrix products  120 us (40%)
  waiting for transfers between devices  102 us (34%)
  blocking collectives  27.4 us (9%)
  other arithmetic  21.6 us (7%)
  local copies, waits for them, and re-layouts  15.1 us (5%)
  between operations  13.5 us (4%)
    all_gather x1, waiting for transfers between devices, local(): piece = lax.all_gather(white, 'chan', axis=1, tiled=True)  102 us
    dot_general x1, matrix products, local(): jnp.dot(cross.reshape(-1, width), lags, preferred_element_type=jnp.float32)  74.7 us
    dot_general x1, matrix products, local(): jnp.dot(flat, table, precision=lax.Precision.HIGHEST, preferred_element_t...  37.7 us
    all_gather x1, blocking collectives, local(): piece = lax.all_gather(strain, 'stack', axis=2, tiled=True)  27.4 us
    reduce_sum x1, other arithmetic, stacked_cross(): jnp.mean(panel_re[:, :, None] * chan_re[:, None] + panel_im[:, :, None] *...  16.3 us
    dot_general x1, matrix products, local(): jnp.einsum('wsc,wcf->wsf', hits, piece, preferred_element_type=jnp.float32)  7.41 us
    concatenate x3, local copies, waits for them, and re-layouts, unpack(): imag_part = jnp.concatenate([edge, packed[..., half + 1:], edge], axis=-1)  6.95 us
  transfers between devices with their start and end apart: 1, of which 1 were waited for; matrix products, arithmetic and copies ran while one was open for 1% of the time, Pallas kernels for 0%

commit v1 on v0

v1 whole, which is shorter than its diff:
```python
import functools
import math

import jax
import jax.numpy as jnp
import ml_dtypes
import numpy as np
from jax import lax
from jax.experimental import pallas as pl
from jax.experimental.pallas import tpu as pltpu
from jax.sharding import PartitionSpec as P

NS = 1024
BF = jnp.bfloat16
F32 = jnp.float32
MESH_CORES = 2


def pair_order():
    return np.concatenate([np.arange(0, 512, 2), np.arange(1, 512, 2)])


def split_table(values):
    high = values.astype(ml_dtypes.bfloat16)
    low = (values - high.astype(np.float64)).astype(ml_dtypes.bfloat16)
    return high, low


@functools.lru_cache(None)
def forward_tables():
    freq = pair_order()
    tables = []
    for odd in range(2):
        times = np.arange(odd, NS, 2)[:, None]
        phase = (times * freq[None, :] % 2048) * (2.0 * math.pi / 2048)
        cosine, sine = np.cos(phase), np.sin(phase)
        middle = (times[:, 0] * 512 % 2048) * (2.0 * math.pi / 2048)
        sine[:, 0] = -np.sin(middle) if odd else np.cos(middle)
        tables += split_table(np.concatenate([cosine, sine], axis=1))
    return tuple(tables)


@functools.lru_cache(None)
def lag_tables():
    freq = pair_order()
    lags = np.arange(1024)[None, :]
    parts = []
    for side in (freq, 1024 - freq):
        phase = (side[:, None] * lags % 2048) * (2.0 * math.pi / 2048)
        parts.append([2.0 * np.cos(phase), -2.0 * np.sin(phase)])
    middle = (512 * lags[0] % 2048) * (2.0 * math.pi / 2048)
    parts[0][0][0] = 2.0 * np.cos(middle)
    parts[0][1][0] = -2.0 * np.sin(middle)
    parts[1][0][0] = 1.0
    parts[1][1][0] = np.where(lags[0] % 2, -1.0, 1.0)
    tables = []
    for half in range(2):
        rows = slice(256 * half, 256 * half + 256)
        stacked = np.concatenate([part[rows] for pair in parts for part in pair], axis=0)
        tables.append((stacked / math.sqrt(2048)).astype(ml_dtypes.bfloat16))
    return tuple(tables)


@functools.lru_cache(None)
def deinterleave():
    table = np.zeros((256, 256), ml_dtypes.bfloat16)
    time = np.arange(256)
    table[time, (time % 2) * 128 + time // 2] = 1
    return table


def dot(a, b, dims=((1,), (0,))):
    return lax.dot_general(a, b, (dims, ((), ())), preferred_element_type=F32)


def iota(shape, dim):
    return lax.broadcasted_iota(jnp.int32, shape, dim)


VMEM = pl.BlockSpec(memory_space=pltpu.VMEM)
SMEM = pl.BlockSpec(memory_space=pltpu.SMEM)
PARAMS = pltpu.CompilerParams(vmem_limit_bytes=44 * 1024 * 1024)


def own_kernel(place, received, perm, own, sends, even, odd):
    core, group = place[0], place[1]
    for pair in range(4):
        block = jnp.concatenate([received[2 * pair, :128], received[2 * pair + 1, :128]], axis=1)
        apart = dot(block, perm[...]).astype(BF)
        even[:, 128 * pair : 128 * pair + 128] = apart[:, :128]
        odd[:, 128 * pair : 128 * pair + 128] = apart[:, 128:]
    rows, cols = iota((128, 128), 0), iota((128, 128), 1)
    turn = rows // 8
    window = jnp.where(turn < 8, 2 * turn + core, 2 * (turn - 8) + 1 - core)
    order = (cols == window * 8 + rows % 8).astype(BF)
    own[:, :512] = dot(order, even[...]).astype(BF)
    own[:, 512:] = dot(order, odd[...]).astype(BF)
    rows, cols = iota((16, 128), 0), iota((16, 128), 1)
    for half in range(2):
        wanted = cols == (2 * group + half) * 8 + rows % 8
        pick_even = (wanted & (rows < 8)).astype(BF)
        pick_odd = (wanted & (rows >= 8)).astype(BF)
        slab = (dot(pick_even, even[...]) + dot(pick_odd, odd[...])).astype(BF)
        for other in range(16):
            sends[2 * other + half] = slab


def prepare(place, received):
    return pl.pallas_call(
        own_kernel,
        out_shape=(
            jax.ShapeDtypeStruct((128, 1024), BF),
            jax.ShapeDtypeStruct((32, 16, 512), BF),
        ),
        in_specs=[SMEM, VMEM, VMEM],
        out_specs=(VMEM, VMEM),
        scratch_shapes=[pltpu.VMEM((128, 512), BF), pltpu.VMEM((128, 512), BF)],
        compiler_params=PARAMS,
    )(place, received, jnp.asarray(deinterleave()))


def pick_kernel(place, received, window_rows, out):
    core, group = place[0], place[1]
    wanted = 2 * group + core
    picks = received[:, 128:144, :].astype(F32)
    picks = jnp.sum(jnp.where(iota(picks.shape, 1) == wanted, picks, 0.0), axis=1)
    slots = iota((512, 128), 0)
    channel = ((slots // 16) * 8 + slots % 8).astype(F32)
    lower = slots % 16 < 8
    for pair in range(4):
        both = picks[2 * pair : 2 * pair + 1] + picks[2 * pair + 1 : 2 * pair + 2]
        hit = channel == both
        for half in range(2):
            chosen = (hit & (lower if half == 0 else ~lower)).astype(F32).astype(BF)
            rows = dot(chosen, window_rows[...], ((0,), (0,)))
            out[128 * pair : 128 * pair + 128, 512 * half : 512 * half + 512] = rows.astype(BF)


def pick(place, received, window_rows):
    return pl.pallas_call(
        pick_kernel,
        out_shape=jax.ShapeDtypeStruct((512, 1024), BF),
        in_specs=[SMEM, VMEM, VMEM],
        out_specs=VMEM,
        compiler_params=PARAMS,
    )(place, received, window_rows)


def white_kernel(rows_ref, even_hi, even_lo, odd_hi, odd_lo, out, evens, odds):
    count = rows_ref.shape[0]
    even, odd = rows_ref[:, :512], rows_ref[:, 512:]
    evens[...] = dot(even, even_hi[...]) + dot(even, even_lo[...])
    odds[...] = dot(odd, odd_hi[...]) + dot(odd, odd_lo[...])

    def strip(step, carry):
        at = pl.ds(pl.multiple_of(step * 16, 16), 16)
        a, c = evens[at, :512], evens[at, 512:]
        b, d = odds[at, :512], odds[at, 512:]
        first = iota((16, 512), 1) == 0
        re_1 = jnp.where(first, c, a + b)
        im_1 = jnp.where(first, d, -c - d)
        re_2 = jnp.where(first, a + b, a - b)
        im_2 = jnp.where(first, a - b, c - d)
        power_1 = re_1 * re_1 + im_1 * im_1
        square_re, square_im = re_2 * re_2, im_2 * im_2
        power_2 = square_re + square_im
        level = jnp.sum(power_1 + power_2, axis=1, keepdims=True) * (1.0 / 1025.0)
        floor = 0.05 * level + 1e-06
        factor_1 = lax.rsqrt(power_1 + floor)
        factor_re = lax.rsqrt(jnp.where(first, square_re, power_2) + floor)
        factor_im = lax.rsqrt(jnp.where(first, square_im, power_2) + floor)
        parts = (re_1 * factor_1, im_1 * factor_1, re_2 * factor_re, im_2 * factor_im)
        for half in range(2):
            for index, part in enumerate(parts):
                start = 1024 * half + 256 * index
                out[at, start : start + 256] = part[:, 256 * half : 256 * half + 256].astype(BF)
        return carry

    lax.fori_loop(0, count // 16, strip, 0)


def whiten(rows, block):
    count = rows.shape[0]
    whole = pl.BlockSpec((512, 1024), lambda i: (0, 0))
    return pl.pallas_call(
        white_kernel,
        out_shape=jax.ShapeDtypeStruct((count, 2048), BF),
        grid=(count // block,),
        in_specs=[pl.BlockSpec((block, 1024), lambda i: (i, 0))] + [whole] * 4,
        out_specs=pl.BlockSpec((block, 2048), lambda i: (i, 0)),
        scratch_shapes=[pltpu.VMEM((block, 1024), F32), pltpu.VMEM((block, 1024), F32)],
        compiler_params=PARAMS,
    )(rows, *[jnp.asarray(t) for t in forward_tables()])


SOURCES = 16


def cross_kernel(near, far, own, lag_even, lag_odd, out, panel, mine, cross):
    @pl.when(pl.program_id(0) == 0)
    def _():
        for w in range(16):
            if w % 2 == 0:
                mine[w : w + 2] = own[8 * w : 8 * w + 16].astype(F32).reshape(2, 8, 2048)

    for w in range(8):
        for group in range(16):
            lane = slice(128 * group, 128 * group + 128)
            panel[w, group] = near[w, :, lane].astype(F32)
            panel[8 + w, group] = far[w, :, lane].astype(F32)

    def pair_of_sources(step, carry):
        for chunk in range(4):
            groups = [8 * (chunk // 2) + chunk % 2 + 2 * k for k in range(4)]
            lanes = [slice(128 * group, 128 * group + 128) for group in groups]
            sums = [[None] * 5, [None] * 5]
            for w in range(16):
                own_parts = [mine[w, :, lane] for lane in lanes]
                for which in range(2):
                    row = step * 2 + which
                    picked = [
                        panel[w, group, pl.ds(row, 8, stride=0), :] for group in groups
                    ]
                    terms = [
                        picked[0] * own_parts[0] + picked[1] * own_parts[1],
                        picked[0] * own_parts[1] - picked[1] * own_parts[0],
                        picked[2] * own_parts[2],
                        picked[3] * own_parts[3],
                        picked[2] * own_parts[3] - picked[3] * own_parts[2],
                    ]
                    if chunk:
                        terms[2:4] = [terms[2] + terms[3], None]
                    total = sums[which]
                    for k, term in enumerate(terms):
                        if term is not None:
                            total[k] = term if total[k] is None else total[k] + term
            results = []
            for re_1, im_1, re_2, edge, im_2 in sums:
                if chunk == 0:
                    first = iota((8, 128), 1) == 0
                    im_2 = jnp.where(first, edge, im_2)
                    re_2 = jnp.where(first, re_2, re_2 + edge)
                results.append((re_1, im_1, re_2, im_2))
            rows = pl.ds(pl.multiple_of(step * 16, 16), 16)
            for lane, upper, lower in zip(lanes, *results):
                both = jnp.concatenate([upper, lower], axis=0) * (1.0 / 16.0)
                cross[rows, lane] = both.astype(BF)
        return carry

    lax.fori_loop(0, SOURCES // 2, pair_of_sources, 0)
    evens = dot(cross[:, :1024], lag_even[...])
    odds = dot(cross[:, 1024:], lag_odd[...])
    out[:, :, :1024] = (evens - odds).reshape(SOURCES, 8, 1024)
    out[:, :, 1024:] = (evens + odds).reshape(SOURCES, 8, 1024)


def correlate(near, far, own):
    panel = pl.BlockSpec((8, SOURCES, 2048), lambda i: (0, i, 0))
    lag = pl.BlockSpec((1024, 1024), lambda i: (0, 0))
    return pl.pallas_call(
        cross_kernel,
        out_shape=jax.ShapeDtypeStruct((64, 8, 2048), F32),
        grid=(64 // SOURCES,),
        in_specs=[panel, panel, pl.BlockSpec((128, 2048), lambda i: (0, 0)), lag, lag],
        out_specs=pl.BlockSpec((SOURCES, 8, 2048), lambda i: (i, 0, 0)),
        scratch_shapes=[
            pltpu.VMEM((16, 16, SOURCES, 128), F32),
            pltpu.VMEM((16, 8, 2048), F32),
            pltpu.VMEM((SOURCES * 8, 2048), BF),
        ],
        compiler_params=PARAMS,
    )(near, far, own, *[jnp.asarray(t) for t in lag_tables()])


def local(strain, sources):
    chan, group = lax.axis_index("chan"), lax.axis_index("stack")
    place = jnp.stack([chan % 2, group]).astype(jnp.int32)
    picks = sources.astype(BF)
    blank = jnp.zeros_like(picks)
    side = group % 2 == 0
    picks = jnp.concatenate([jnp.where(side, picks, blank), jnp.where(side, blank, picks)], axis=1)
    block = jnp.concatenate([strain.reshape(128, 128), picks], axis=0)
    block = jnp.broadcast_to(block[None], (8, 144, 128))
    received = lax.all_to_all(block, "stack", 0, 0, tiled=True)
    own, sends = prepare(place, received)
    window_rows = lax.all_to_all(sends, "chan", 0, 0, tiled=True)
    picked = pick(place, received, window_rows.reshape(512, 512))
    near = lax.all_to_all(picked.reshape(8, 64, 1024), "stack", 0, 0, tiled=True)
    near = near.reshape(512, 1024)
    far = lax.ppermute(near, "chan", [(i, i ^ 1) for i in range(32)])
    own_white = whiten(own, 128)
    near_white = whiten(near, 512).reshape(8, 64, 2048)
    far_white = whiten(far, 512).reshape(8, 64, 2048)
    return correlate(near_white, far_white, own_white)


def solution(mesh):
    placed = (P(None, "chan", "stack"), P(None, "stack"))
    return jax.shard_map(
        local, mesh=mesh, in_specs=placed, out_specs=P("stack", "chan", None), check_vma=False
    )
```

time: 300 us -> 102 us (0.34)
  matrix products: 120 us -> 0 us
  waiting for transfers between devices: 102 us -> 7.64 us
  Pallas kernels: 0 us -> 34.2 us
  other arithmetic: 21.6 us -> 1.61 us
  blocking collectives: 27.4 us -> 44.5 us
  local copies, waits for them, and re-layouts: 15.1 us -> 1.69 us
  between operations: 13.5 us -> 0.1 us
  starting transfers between devices: 0.01 us -> 11.4 us
    dot_general x3 -> x0, matrix products: 120 us -> none  [the longest x1 74.7 us: local(): jnp.dot(cross.reshape(-1, width), lags, preferred_element_type=jnp.float32)]
    all_gather x1 -> x0, waiting for transfers between devices: 102 us -> none  [local(): piece = lax.all_gather(white, 'chan', axis=1, tiled=True)]
    all_to_all x0 -> x2, blocking collectives: none -> 44.5 us  [the longest x1 27.4 us: local(): window_rows = lax.all_to_all(sends, 'chan', 0, 0, tiled=True)]
    pallas_call x0 -> x6, Pallas kernels: none -> 34.2 us  [the longest x1 18.3 us: correlate(): pl.pallas_call(cross_kernel, out_shape=jax.ShapeDtypeStruct((64, 8, 2048)...]
    all_gather x1 -> x0, blocking collectives: 27.4 us -> none  [local(): piece = lax.all_gather(strain, 'stack', axis=2, tiled=True)]
    reduce_sum x2 -> x0, other arithmetic: 16.5 us -> none  [the longest x1 16.3 us: stacked_cross(): jnp.mean(panel_re[:, :, None] * chan_re[:, None] + panel_im[:, :, None] *...]
    slice x5 -> x0, local copies, waits for them, and re-layouts: 8.08 us -> none  [the longest x3 4.45 us: unpack(): imag_part = jnp.concatenate([edge, packed[..., half + 1:], edge], axis=-1)]
    all_to_all x0 -> x1, waiting for transfers between devices: none -> 7.64 us  [local(): received = lax.all_to_all(block, 'stack', 0, 0, tiled=True)]
  transfers between devices with their start and end apart: 1 -> 2, of which waited for: 1 -> 1; matrix products, arithmetic and copies ran while one was open for 1% -> 0% of each run, Pallas kernels for 0% -> 8%
where the time goes in v1:
time: 102 us; the launch traced here: 101 us
  blocking collectives  44.5 us (44%)
  Pallas kernels  34.2 us (34%)
  starting transfers between devices  11.4 us (11%)
  waiting for transfers between devices  7.64 us (7%)
  local copies, waits for them, and re-layouts  1.69 us (2%)
  other arithmetic  1.61 us (2%)
    all_to_all x1, blocking collectives, local(): window_rows = lax.all_to_all(sends, 'chan', 0, 0, tiled=True)  27.4 us
    pallas_call x1, Pallas kernels, correlate(): pl.pallas_call(cross_kernel, out_shape=jax.ShapeDtypeStruct((64, 8, 2048)...  18.3 us
    all_to_all x1, blocking collectives, local(): lax.all_to_all(picked.reshape(8, 64, 1024), 'stack', 0, 0, tiled=True)  17.1 us
    pallas_call x3, Pallas kernels, whiten(): pl.pallas_call(white_kernel, out_shape=jax.ShapeDtypeStruct((count, 2048)...  13.6 us
    all_to_all x1, waiting for transfers between devices, local(): received = lax.all_to_all(block, 'stack', 0, 0, tiled=True)  7.64 us
    all_to_all x1, starting transfers between devices, local(): received = lax.all_to_all(block, 'stack', 0, 0, tiled=True)  7.48 us
    ppermute x1, starting transfers between devices, local(): far = lax.ppermute(near, 'chan', [(i, i ^ 1) for i in range(32)])  3.96 us
  transfers between devices with their start and end apart: 2, of which 1 were waited for; matrix products, arithmetic and copies ran while one was open for 0% of the time, Pallas kernels for 8%

profile of v1, /device:TPU:1, one launch (start us, length us, event | category | flops | bytes accessed | tf_op | source)
XLA Modules:
  0.0 101.2 jit_solution(6090283774877988472)
XLA Ops:
  0.0 0.7 broadcast_select_fusion.1
  0.7 0.8 maximum_maximum_fusion
  1.5 0.8 broadcast_in_dim.10
  2.3 7.5 %all-to-all-start = ((bf16[8,144,128]{2,1,0:T(8,128)(2,1)}), bf16[8,144,128]{2,1,0:T(8,128)(2,1)S(1)}, u32[]{:S(2)}, u32[]{:S(2)}) async-start(bf16[8,144,128]{2,1,0:T(8,128)(2,1)} %broadcast_in_dim.10), calls=%async_computation | async-start | bytes 589824 | tf_op jit(solution)/shard_map/all_to_all | solution.py:284
  9.8 0.1 pad_add_fusion.place
  9.8 7.6 %all-to-all-done.received = bf16[8,144,128]{2,1,0:T(8,128)(2,1)S(1)} async-done(((bf16[8,144,128]{2,1,0:T(8,128)(2,1)}), bf16[8,144,128]{2,1,0:T(8,128)(2,1)S(1)}, u32[]{:S(2)}, u32[]{:S(2)}) %all-to-all-start) | async-done | bytes 294944 | tf_op jit(solution)/shard_map/all_to_all | solution.py:284
  17.5 0.0 copy-start.6
  17.5 0.9 copy-done.6
  18.4 1.0 %shard_map.91 = (bf16[128,1024]{1,0:T(8,128)(2,1)S(1)}, bf16[32,16,512]{2,1,0:T(8,128)(2,1)S(1)}) custom-call(s32[2]{0:T(128)S(1)} %pad_add_fusion.place, bf16[8,144,128]{2,1,0:T(8,128)(2,1)S(1)} %all-to-all-done.received, bf16[256,256]{1,0:T(8,128)(2,1)S(1)} %copy-done.6), custom_call_target="tpu_custom_call" | custom-call | tf_op jit(solution)/shard_map/pallas_call | solution.py:109
  19.4 0.0 copy-start.3
  19.4 27.4 %all_to_all.15 = bf16[32,16,512]{2,1,0:T(8,128)(2,1)S(1)} all-to-all(bf16[32,16,512]{2,1,0:T(8,128)(2,1)S(1)} %get-tuple-element.7), channel_id=1, replica_groups=mesh['chan'=32,'stack'=8] {'chan'}, dimensions={0} | all-to-all | bytes 1048576 | tf_op jit(solution)/shard_map/all_to_all | solution.py:286
  46.9 0.0 copy-start
  46.9 0.0 copy-start.1
  46.9 0.0 copy-start.2
  46.9 1.3 %shard_map.92 = bf16[512,1024]{1,0:T(8,128)(2,1)S(1)} custom-call(s32[2]{0:T(128)S(1)} %pad_add_fusion.place, bf16[8,144,128]{2,1,0:T(8,128)(2,1)S(1)} %all-to-all-done.received, bf16[512,512]{1,0:T(8,128)(2,1)S(1)} %bitcast.13), custom_call_target="tpu_custom_call" | custom-call | tf_op jit(solution)/shard_map/pallas_call | solution.py:140
  48.2 17.1 %all_to_all.16 = bf16[8,64,1024]{2,1,0:T(8,128)(2,1)S(1)} all-to-all(bf16[8,64,1024]{2,1,0:T(8,128)(2,1)S(1)} %bitcast.12), channel_id=1, replica_groups=mesh['chan'=32,'stack'=8] {'stack'}, dimensions={0} | all-to-all | bytes 2097152 | tf_op jit(solution)/shard_map/all_to_all | solution.py:288
  65.3 4.0 %collective-permute-start = (bf16[512,1024]{1,0:T(8,128)(2,1)S(1)}, bf16[512,1024]{1,0:T(8,128)(2,1)S(1)}, u32[]{:S(2)}, u32[]{:S(2)}) collective-permute-start(bf16[512,1024]{1,0:T(8,128)(2,1)S(1)} %bitcast.10), channel_id=1, source_target_pairs={{0,8},{8,0},{16,24},{24,16},{32,40},{40,32},{48,56},{56,48},{64,72... | collective-permute-start | bytes 3145736 | tf_op jit(solution)/shard_map/ppermute | solution.py:290
  69.2 0.0 copy-done.3
  69.2 0.0 copy-done
  69.2 0.0 copy-done.1
  69.2 0.0 copy-done.2
  69.2 1.6 %shard_map.95.own = bf16[128,2048]{1,0:T(8,128)(2,1)S(1)} custom-call(bf16[128,1024]{1,0:T(8,128)(2,1)S(1)} %get-tuple-element.8.rows_ref, bf16[512,1024]{1,0:T(8,128)(2,1)S(1)} %copy-done.3, bf16[512,1024]{1,0:T(8,128)(2,1)S(1)} %copy-done.2, bf16[512,1024]{1,0:T(8,128)(2,1)S(1)} %copy-done.1, bf16[512,1024]{1,0:T(8,128)(2,1)S(1)} %copy-done), custom_call_target="tpu_custom_call" | custom-call | tf_op jit(solution)/shard_map/pallas_call | solution.py:185
  70.9 6.0 %shard_map.93 = bf16[512,2048]{1,0:T(8,128)(2,1)S(1)} custom-call(bf16[512,1024]{1,0:T(8,128)(2,1)S(1)} %bitcast.11, bf16[512,1024]{1,0:T(8,128)(2,1)S(1)} %copy-done.3, bf16[512,1024]{1,0:T(8,128)(2,1)S(1)} %copy-done.2, bf16[512,1024]{1,0:T(8,128)(2,1)S(1)} %copy-done.1, bf16[512,1024]{1,0:T(8,128)(2,1)S(1)} %copy-done), custom_call_target="tpu_custom_call" | custom-call | tf_op jit(solution)/shard_map/pallas_call | solution.py:185
  76.9 0.0 copy-start.4
  76.9 0.0 copy-start.5
  76.9 0.0 collective-permute-done.rows_ref
  76.9 6.0 %shard_map.94 = bf16[512,2048]{1,0:T(8,128)(2,1)S(1)} custom-call(bf16[512,1024]{1,0:T(8,128)(2,1)S(1)} %collective-permute-done.rows_ref, bf16[512,1024]{1,0:T(8,128)(2,1)S(1)} %copy-done.3, bf16[512,1024]{1,0:T(8,128)(2,1)S(1)} %copy-done.2, bf16[512,1024]{1,0:T(8,128)(2,1)S(1)} %copy-done.1, bf16[512,1024]{1,0:T(8,128)(2,1)S(1)} %copy-done), custom_call_target="tpu_custom_call" | custom-call | tf_op jit(solution)/shard_map/pallas_call | solution.py:185
  82.9 0.0 copy-done.4
  82.9 0.0 copy-done.5
  82.9 18.3 %shard_map.96 = f32[64,8,2048]{2,1,0:T(8,128)} custom-call(bf16[8,64,2048]{2,1,0:T(8,128)(2,1)S(1)} %bitcast.8, bf16[8,64,2048]{2,1,0:T(8,128)(2,1)S(1)} %bitcast.9, bf16[128,2048]{1,0:T(8,128)(2,1)S(1)} %shard_map.95.own, bf16[1024,1024]{1,0:T(8,128)(2,1)S(1)} %copy-done.5, bf16[1024,1024]{1,0:T(8,128)(2,1)S(1)} %copy-done.4), custom_call_target="tpu_custom_call" | custom-call | tf_op jit(solution)/shard_map/pallas_call | solution.py:260
Async XLA Ops:
  2.3 15.2 %all-to-all-start = ((bf16[8,144,128]{2,1,0:T(8,128)(2,1)}), bf16[8,144,128]{2,1,0:T(8,128)(2,1)S(1)}, u32[]{:S(2)}, u32[]{:S(2)}) async-start(bf16[8,144,128]{2,1,0:T(8,128)(2,1)} %broadcast_in_dim.10), calls=%async_computation | async-start | bytes 589824 | tf_op jit(solution)/shard_map/all_to_all | solution.py:284
  17.5 0.9 copy-start.6
  19.4 49.8 %copy-start.3 = (bf16[512,1024]{1,0:T(8,128)(2,1)S(1)}, bf16[512,1024]{1,0:T(8,128)(2,1)}, u32[]{:S(2)}) copy-start(bf16[512,1024]{1,0:T(8,128)(2,1)} %constant.44.clone.even_hi) | copy-start | bytes 3145732
  46.9 22.4 %copy-start = (bf16[512,1024]{1,0:T(8,128)(2,1)S(1)}, bf16[512,1024]{1,0:T(8,128)(2,1)}, u32[]{:S(2)}) copy-start(bf16[512,1024]{1,0:T(8,128)(2,1)} %constant.47.clone.odd_lo) | copy-start | bytes 3145732
  46.9 22.4 %copy-start.1 = (bf16[512,1024]{1,0:T(8,128)(2,1)S(1)}, bf16[512,1024]{1,0:T(8,128)(2,1)}, u32[]{:S(2)}) copy-start(bf16[512,1024]{1,0:T(8,128)(2,1)} %constant.46.clone.odd_hi) | copy-start | bytes 3145732
  46.9 22.4 %copy-start.2 = (bf16[512,1024]{1,0:T(8,128)(2,1)S(1)}, bf16[512,1024]{1,0:T(8,128)(2,1)}, u32[]{:S(2)}) copy-start(bf16[512,1024]{1,0:T(8,128)(2,1)} %constant.45.clone.even_lo) | copy-start | bytes 3145732
  65.3 11.6 %collective-permute-start = (bf16[512,1024]{1,0:T(8,128)(2,1)S(1)}, bf16[512,1024]{1,0:T(8,128)(2,1)S(1)}, u32[]{:S(2)}, u32[]{:S(2)}) collective-permute-start(bf16[512,1024]{1,0:T(8,128)(2,1)S(1)} %bitcast.10), channel_id=1, source_target_pairs={{0,8},{8,0},{16,24},{24,16},{32,40},{40,32},{48,56},{56,48},{64,72... | collective-permute-start | bytes 3145736 | tf_op jit(solution)/shard_map/ppermute | solution.py:290
  76.9 6.0 %copy-start.4 = (bf16[1024,1024]{1,0:T(8,128)(2,1)S(1)}, bf16[1024,1024]{1,0:T(8,128)(2,1)}, u32[]{:S(2)}) copy-start(bf16[1024,1024]{1,0:T(8,128)(2,1)} %constant.49.clone.lag_odd) | copy-start | bytes 6291460
  76.9 6.0 %copy-start.5 = (bf16[1024,1024]{1,0:T(8,128)(2,1)S(1)}, bf16[1024,1024]{1,0:T(8,128)(2,1)}, u32[]{:S(2)}) copy-start(bf16[1024,1024]{1,0:T(8,128)(2,1)} %constant.48.clone.lag_even) | copy-start | bytes 6291460

commit v2 on v1

v2 whole, which is shorter than its diff:
```python
import functools
import math

import jax
import jax.numpy as jnp
import ml_dtypes
import numpy as np
from jax import lax
from jax.experimental import pallas as pl
from jax.experimental.pallas import tpu as pltpu
from jax.sharding import PartitionSpec as P

NS = 1024
BF = jnp.bfloat16
F32 = jnp.float32
MESH_CORES = 2


def pair_order():
    return np.concatenate([np.arange(0, 512, 2), np.arange(1, 512, 2)])


def split_table(values):
    high = values.astype(ml_dtypes.bfloat16)
    low = (values - high.astype(np.float64)).astype(ml_dtypes.bfloat16)
    return high, low


@functools.lru_cache(None)
def forward_tables():
    freq = pair_order()
    tables = []
    for odd in range(2):
        times = np.arange(odd, NS, 2)[:, None]
        phase = (times * freq[None, :] % 2048) * (2.0 * math.pi / 2048)
        cosine, sine = np.cos(phase), np.sin(phase)
        middle = (times[:, 0] * 512 % 2048) * (2.0 * math.pi / 2048)
        sine[:, 0] = -np.sin(middle) if odd else np.cos(middle)
        tables += split_table(np.concatenate([cosine, sine], axis=1))
    return tuple(tables)


@functools.lru_cache(None)
def lag_tables():
    freq = pair_order()
    lags = np.arange(1024)[None, :]
    parts = []
    for side in (freq, 1024 - freq):
        phase = (side[:, None] * lags % 2048) * (2.0 * math.pi / 2048)
        parts.append([2.0 * np.cos(phase), -2.0 * np.sin(phase)])
    middle = (512 * lags[0] % 2048) * (2.0 * math.pi / 2048)
    parts[0][0][0] = 2.0 * np.cos(middle)
    parts[0][1][0] = -2.0 * np.sin(middle)
    parts[1][0][0] = 1.0
    parts[1][1][0] = np.where(lags[0] % 2, -1.0, 1.0)
    tables = []
    for half in range(2):
        rows = slice(256 * half, 256 * half + 256)
        stacked = np.concatenate([part[rows] for pair in parts for part in pair], axis=0)
        tables.append((stacked / math.sqrt(2048)).astype(ml_dtypes.bfloat16))
    return tuple(tables)


@functools.lru_cache(None)
def deinterleave():
    table = np.zeros((256, 256), ml_dtypes.bfloat16)
    time = np.arange(256)
    table[time, (time % 2) * 128 + time // 2] = 1
    return table


def dot(a, b, dims=((1,), (0,))):
    return lax.dot_general(a, b, (dims, ((), ())), preferred_element_type=F32)


def iota(shape, dim):
    return lax.broadcasted_iota(jnp.int32, shape, dim)


VMEM = pl.BlockSpec(memory_space=pltpu.VMEM)
PARAMS = pltpu.CompilerParams(vmem_limit_bytes=44 * 1024 * 1024)


def place():
    return lax.axis_index("chan") % MESH_CORES, lax.axis_index("stack")


def pack_kernel(strain, sources, out):
    _, group = place()
    picks = sources[...].astype(F32)
    both = jnp.concatenate([picks, picks], axis=1)
    both = jnp.where(iota((16, 128), 1) // 64 == group % 2, both, 0.0).astype(BF)
    for other in range(8):
        out[other, :128] = strain[...]
        out[other, 128:] = both


def pack(strain, sources):
    return pl.pallas_call(
        pack_kernel,
        out_shape=jax.ShapeDtypeStruct((8, 144, 128), BF),
        in_specs=[VMEM, VMEM],
        out_specs=VMEM,
        compiler_params=PARAMS,
    )(strain, sources)


def own_kernel(received, perm, own, sends, even, odd):
    core, group = place()
    for pair in range(4):
        block = jnp.concatenate([received[2 * pair, :128], received[2 * pair + 1, :128]], axis=1)
        apart = dot(block, perm[...]).astype(BF)
        even[:, 128 * pair : 128 * pair + 128] = apart[:, :128]
        odd[:, 128 * pair : 128 * pair + 128] = apart[:, 128:]
    rows, cols = iota((16, 128), 0), iota((16, 128), 1)
    for half in range(2):
        wanted = cols == (2 * group + half) * 8 + rows % 8
        pick_even = (wanted & (rows < 8)).astype(F32).astype(BF)
        pick_odd = (wanted & (rows >= 8)).astype(F32).astype(BF)
        slab = (dot(pick_even, even[...]) + dot(pick_odd, odd[...])).astype(BF)
        for other in range(16):
            sends[2 * other + half] = slab
    rows, cols = iota((128, 128), 0), iota((128, 128), 1)
    turn = rows // 8
    window = jnp.where(turn < 8, 2 * turn + core, 2 * (turn - 8) + 1 - core)
    order = (cols == window * 8 + rows % 8).astype(F32).astype(BF)
    own[:, :512] = dot(order, even[...]).astype(BF)
    own[:, 512:] = dot(order, odd[...]).astype(BF)


def prepare(received):
    return pl.pallas_call(
        own_kernel,
        out_shape=(
            jax.ShapeDtypeStruct((128, 1024), BF),
            jax.ShapeDtypeStruct((32, 16, 512), BF),
        ),
        in_specs=[VMEM, VMEM],
        out_specs=(VMEM, VMEM),
        scratch_shapes=[pltpu.VMEM((128, 512), BF), pltpu.VMEM((128, 512), BF)],
        compiler_params=PARAMS,
    )(received, jnp.asarray(deinterleave()))


def pick_kernel(received, window_rows, out):
    core, group = place()
    wanted = 2 * group + core
    picks = received[:, 128:144, :].astype(F32)
    picks = jnp.sum(jnp.where(iota(picks.shape, 1) == wanted, picks, 0.0), axis=1)
    slots = iota((512, 128), 0)
    channel = ((slots // 16) * 8 + slots % 8).astype(F32)
    lower = slots % 16 < 8
    for pair in range(4):
        both = picks[2 * pair : 2 * pair + 1] + picks[2 * pair + 1 : 2 * pair + 2]
        hit = channel == both
        for half in range(2):
            chosen = (hit & (lower if half == 0 else ~lower)).astype(F32).astype(BF)
            rows = dot(chosen, window_rows[...], ((0,), (0,)))
            out[128 * pair : 128 * pair + 128, 512 * half : 512 * half + 512] = rows.astype(BF)


def pick(received, window_rows):
    return pl.pallas_call(
        pick_kernel,
        out_shape=jax.ShapeDtypeStruct((512, 1024), BF),
        in_specs=[VMEM, VMEM],
        out_specs=VMEM,
        compiler_params=PARAMS,
    )(received, window_rows)


def whiten_strips(count, evens, odds, store):
    def strip(step, carry):
        at = pl.ds(pl.multiple_of(step * 16, 16), 16)
        first = iota((16, 128), 1) == 0
        held, total = [], None
        for k in range(4):
            near, far = slice(128 * k, 128 * k + 128), slice(512 + 128 * k, 640 + 128 * k)
            a, c, b, d = evens[at, near], evens[at, far], odds[at, near], odds[at, far]
            re_1, im_1, re_2, im_2 = a + b, c + d, a - b, c - d
            if k == 0:
                re_2, im_2 = jnp.where(first, re_1, re_2), jnp.where(first, re_2, im_2)
                re_1, im_1 = jnp.where(first, c, re_1), jnp.where(first, -d, im_1)
            power_1 = re_1 * re_1 + im_1 * im_1
            square_re, square_im = re_2 * re_2, im_2 * im_2
            power_2 = square_re + square_im
            both = power_1 + power_2
            total = both if total is None else total + both
            held.append((re_1, im_1, re_2, im_2, power_1, square_re, square_im, power_2))
        level = jnp.sum(total, axis=1, keepdims=True) * (1.0 / 1025.0)
        floor = 0.05 * level + 1e-06
        for k, (re_1, im_1, re_2, im_2, power_1, square_re, square_im, power_2) in enumerate(held):
            factor_1 = lax.rsqrt(power_1 + floor)
            if k == 0:
                factor_re = lax.rsqrt(jnp.where(first, square_re, power_2) + floor)
                factor_im = lax.rsqrt(jnp.where(first, square_im, power_2) + floor)
            else:
                factor_re = factor_im = lax.rsqrt(power_2 + floor)
            parts = (re_1 * factor_1, -im_1 * factor_1, re_2 * factor_re, im_2 * factor_im)
            for index, part in enumerate(parts):
                store(step, 8 * (k // 2) + 2 * index + k % 2, part.astype(BF))
        return carry

    lax.fori_loop(0, count // 16, strip, 0, unroll=4)


def transform(rows, tables, evens, odds):
    even_hi, even_lo, odd_hi, odd_lo = tables
    even, odd = rows[:, :512], rows[:, 512:]
    evens[...] = dot(even, even_hi[...]) + dot(even, even_lo[...])
    odds[...] = dot(odd, odd_hi[...]) + dot(odd, odd_lo[...])


def own_white_kernel(rows, even_hi, even_lo, odd_hi, odd_lo, out, evens, odds):
    transform(rows[...], (even_hi, even_lo, odd_hi, odd_lo), evens, odds)

    def store(step, lane_group, part):
        out[pl.ds(2 * step, 2), lane_group] = part.astype(F32).reshape(2, 8, 128)

    whiten_strips(128, evens, odds, store)


def panel_white_kernel(half, rows, even_hi, even_lo, odd_hi, odd_lo, out, evens, odds):
    picked = rows[:, 32 * half : 32 * half + 32, :].reshape(256, 1024)
    transform(picked, (even_hi, even_lo, odd_hi, odd_lo), evens, odds)

    def store(step, lane_group, part):
        at = pl.ds(pl.multiple_of(step % 2 * 16, 16), 16)
        out[step // 2, at, 128 * lane_group : 128 * lane_group + 128] = part

    whiten_strips(256, evens, odds, store)


def white_call(kernel, rows, count, shape, dtype):
    return pl.pallas_call(
        kernel,
        out_shape=jax.ShapeDtypeStruct(shape, dtype),
        in_specs=[VMEM] * 5,
        out_specs=VMEM,
        scratch_shapes=[pltpu.VMEM((count, 1024), F32), pltpu.VMEM((count, 1024), F32)],
        compiler_params=PARAMS,
        cost_estimate=pl.CostEstimate(
            flops=count * 2**22, bytes_accessed=2**22 + count * 2**13, transcendentals=count * 1024
        ),
    )(rows, *[jnp.asarray(t) for t in forward_tables()])


SOURCES = 32
CHANNELS = 4
PIECES = 4


def cross_kernel(half, near, far, own, lag_even, lag_odd, *rest):
    out, raw, cross, stage, sems = rest[-5:]
    turns = 8 // CHANNELS

    def block(step, carry):
        tile, start = step // turns, step % turns * CHANNELS
        rows = pl.ds(pl.multiple_of(tile * 16, 16), 16)
        for chunk in range(4):
            groups = [8 * (chunk // 2) + chunk % 2 + 2 * k for k in range(4)]
            sums = [[None] * 5 for _ in range(2 * CHANNELS)]
            for w in range(16):
                side = near if w < 8 else far
                tall = [side[w % 8, rows, 128 * g : 128 * g + 128].astype(F32) for g in groups]
                for c in range(CHANNELS):
                    mine = [own[w, g, pl.ds(start + c, 8, stride=0), :] for g in groups]
                    for t in range(2):
                        picked = [values[8 * t : 8 * t + 8] for values in tall]
                        terms = [
                            picked[0] * mine[0] + picked[1] * mine[1],
                            picked[0] * mine[1] - picked[1] * mine[0],
                            picked[2] * mine[2],
                            picked[3] * mine[3],
                            picked[2] * mine[3] - picked[3] * mine[2],
                        ]
                        if chunk:
                            terms[2:4] = [terms[2] + terms[3], None]
                        total = sums[2 * c + t]
                        for k, term in enumerate(terms):
                            if term is not None:
                                total[k] = term if total[k] is None else total[k] + term
            for index, (re_1, im_1, re_2, edge, im_2) in enumerate(sums):
                if chunk == 0:
                    first = iota((8, 128), 1) == 0
                    im_2 = jnp.where(first, edge, im_2)
                    re_2 = jnp.where(first, re_2, re_2 + edge)
                lowest = tile * 128 + index % 2 * 64 + start + index // 2
                for g, part in zip(groups, (re_1, im_1, re_2, im_2)):
                    raw[g, pl.ds(lowest, 8, stride=8), :] = part
        return carry

    lax.fori_loop(0, SOURCES // 16 * turns, block, 0)
    for g in range(16):
        cross[:, 128 * g : 128 * g + 128] = (raw[g] * (1.0 / 16.0)).astype(BF)
    width = 1024 // PIECES
    copies = []
    for piece in range(PIECES):
        lower = slice(width * piece, width * piece + width)
        upper = slice(1024 + width * piece, 1024 + width * piece + width)
        evens = dot(cross[:, :1024], lag_even[:, lower])
        odds = dot(cross[:, 1024:], lag_odd[:, lower])
        stage[:, :, lower] = (evens - odds).reshape(SOURCES, 8, width)
        stage[:, :, upper] = (evens + odds).reshape(SOURCES, 8, width)
        for lanes in (lower, upper):
            copy = pltpu.make_async_copy(
                stage.at[:, :, lanes],
                out.at[SOURCES * half : SOURCES * half + SOURCES, :, lanes],
                sems.at[len(copies)],
            )
            copy.start()
            copies.append(copy)
    for copy in copies:
        copy.wait()


def correlate(half, near, far, own, earlier=None):
    anywhere = pl.BlockSpec(memory_space=pl.ANY)
    operands = [near, far, own, *[jnp.asarray(t) for t in lag_tables()]]
    specs = [VMEM] * 5
    aliases = {}
    if earlier is not None:
        aliases = {len(operands): 0}
        operands.append(earlier)
        specs.append(anywhere)
    return pl.pallas_call(
        functools.partial(cross_kernel, half),
        out_shape=jax.ShapeDtypeStruct((64, 8, 2048), F32),
        in_specs=specs,
        out_specs=anywhere,
        input_output_aliases=aliases,
        scratch_shapes=[
            pltpu.VMEM((16, SOURCES * 8, 128), F32),
            pltpu.VMEM((SOURCES * 8, 2048), BF),
            pltpu.VMEM((SOURCES, 8, 2048), F32),
            pltpu.SemaphoreType.DMA((2 * PIECES,)),
        ],
        compiler_params=PARAMS,
        cost_estimate=pl.CostEstimate(
            flops=3 * 2**30, bytes_accessed=9 * 2**20, transcendentals=0
        ),
    )(*operands)


def local(strain, sources):
    block = pack(strain.reshape(128, 128), sources)
    received = lax.all_to_all(block, "stack", 0, 0, tiled=True)
    own, sends = prepare(received)
    window_rows = lax.all_to_all(sends, "chan", 0, 0, tiled=True)
    own_white = white_call(own_white_kernel, own, 128, (16, 16, 8, 128), F32)
    picked = pick(received, window_rows.reshape(512, 512))
    picked, own_white = lax.optimization_barrier((picked, own_white))
    rows = lax.all_to_all(picked.reshape(8, 64, 1024), "stack", 0, 0, tiled=True)
    near, far = [], []
    for half in range(2):
        kernel = functools.partial(panel_white_kernel, half)
        near.append(white_call(kernel, rows, 256, (8, 32, 2048), BF))
        far.append(lax.ppermute(near[half], "chan", [(i, i ^ 1) for i in range(32)]))
    result = correlate(0, near[0], far[0], own_white)
    return correlate(1, near[1], far[1], own_white, result)


def solution(mesh):
    placed = (P(None, "chan", "stack"), P(None, "stack"))
    return jax.shard_map(
        local, mesh=mesh, in_specs=placed, out_specs=P("stack", "chan", None), check_vma=False
    )
```

time: 102 us -> 89.7 us (0.88)
  blocking collectives: 44.5 us -> 32.1 us
  Pallas kernels: 34.2 us -> 22.9 us
  local copies, waits for them, and re-layouts: 1.69 us -> 9.9 us
  starting transfers between devices: 11.4 us -> 15.1 us
  other arithmetic: 1.61 us -> 0 us
  waiting for transfers between devices: 7.64 us -> 8.96 us
    pallas_call x4 -> x6, Pallas kernels: 31.9 us -> 19.8 us  [the longest x2 14.8 us: correlate(): pl.pallas_call(functools.partial(cross_kernel, half), out_shape=jax.Shape...]
    all_to_all x1, blocking collectives: 27.4 us -> 15.3 us  [local(): received = lax.all_to_all(block, 'stack', 0, 0, tiled=True)]
    unnamed x14 -> x34, local copies, waits for them, and re-layouts: 0.94 us -> 9.9 us
    all_to_all x1, starting transfers between devices: 7.48 us -> 11 us  [local(): window_rows = lax.all_to_all(sends, 'chan', 0, 0, tiled=True)]
    all_to_all x1, waiting for transfers between devices: 7.64 us -> 8.7 us  [local(): window_rows = lax.all_to_all(sends, 'chan', 0, 0, tiled=True)]
    ppermute x1 -> x2, starting transfers between devices: 3.96 us -> 4.17 us  [local(): lax.ppermute(near[half], 'chan', [(i, i ^ 1) for i in range(32)])]
  transfers between devices with their start and end apart: 2 -> 3, of which waited for: 1 -> 2; matrix products, arithmetic and copies ran while one was open for 0% -> 0% of each run, Pallas kernels for 8% -> 12%
where the time goes in v2:
time: 89.7 us; the launch traced here: 89.1 us
  blocking collectives  32.1 us (36%)
  Pallas kernels  22.9 us (26%)
  starting transfers between devices  15.1 us (17%)
  local copies, waits for them, and re-layouts  9.9 us (11%)
  waiting for transfers between devices  8.96 us (10%)
    all_to_all x1, blocking collectives, local(): lax.all_to_all(picked.reshape(8, 64, 1024), 'stack', 0, 0, tiled=True)  16.8 us
    all_to_all x1, blocking collectives, local(): received = lax.all_to_all(block, 'stack', 0, 0, tiled=True)  15.3 us
    pallas_call x2, Pallas kernels, correlate(): pl.pallas_call(functools.partial(cross_kernel, half), out_shape=jax.Shape...  14.8 us
    all_to_all x1, starting transfers between devices, local(): window_rows = lax.all_to_all(sends, 'chan', 0, 0, tiled=True)  11 us
    unnamed x34, local copies, waits for them, and re-layouts  9.9 us
    all_to_all x1, waiting for transfers between devices, local(): window_rows = lax.all_to_all(sends, 'chan', 0, 0, tiled=True)  8.7 us
    pallas_call x3, Pallas kernels, white_call(): pl.pallas_call(kernel, out_shape=jax.ShapeDtypeStruct(shape, dtype), in_s...  4.91 us
    ppermute x2, starting transfers between devices, local(): lax.ppermute(near[half], 'chan', [(i, i ^ 1) for i in range(32)])  4.17 us
  transfers between devices with their start and end apart: 3, of which 2 were waited for; matrix products, arithmetic and copies ran while one was open for 0% of the time, Pallas kernels for 12%

profile of v2, /device:TPU:1, one launch (start us, length us, event | category | flops | bytes accessed | tf_op | source)
XLA Modules:
  0.0 89.1 jit_solution(3187776295569356646)
XLA Ops:
  0.0 0.8 copy-done.15
  0.8 0.7 copy-done.16
  1.5 0.1 shard_map.91
  1.5 15.3 %all_to_all.15.received = bf16[8,144,128]{2,1,0:T(8,128)(2,1)S(1)} all-to-all(bf16[8,144,128]{2,1,0:T(8,128)(2,1)S(1)} %shard_map.91), channel_id=1, replica_groups=mesh['chan'=32,'stack'=8] {'stack'}, dimensions={0} | all-to-all | bytes 589824 | tf_op jit(solution)/shard_map/all_to_all | solution.py:347
  16.8 0.9 %copy-done.14 = bf16[256,256]{1,0:T(8,128)(2,1)S(1)} copy-done((bf16[256,256]{1,0:T(8,128)(2,1)S(1)}, bf16[256,256]{1,0:T(8,128)(2,1)}, u32[]{:S(2)}) %copy-start.14) | copy-done | bytes 131096
  17.7 1.2 %shard_map.92 = (bf16[128,1024]{1,0:T(8,128)(2,1)S(1)}, bf16[32,16,512]{2,1,0:T(8,128)(2,1)}) custom-call(bf16[8,144,128]{2,1,0:T(8,128)(2,1)S(1)} %all_to_all.15.received, bf16[256,256]{1,0:T(8,128)(2,1)S(1)} %copy-done.14), custom_call_target="tpu_custom_call" | custom-call | tf_op jit(solution)/shard_map/pallas_call | solution.py:132
  19.0 0.7 copy-done.12
  19.7 11.0 %all-to-all-start.1 = ((bf16[32,16,512]{2,1,0:T(8,128)(2,1)}), bf16[32,16,512]{2,1,0:T(8,128)(2,1)}, u32[]{:S(2)}, u32[]{:S(2)}) async-start(bf16[32,16,512]{2,1,0:T(8,128)(2,1)} %get-tuple-element.9), calls=%async_computation.1 | async-start | bytes 1048576 | tf_op jit(solution)/shard_map/all_to_all | solution.py:349
  30.6 0.0 copy-start
  30.6 1.2 %copy-done = bf16[512,1024]{1,0:T(8,128)(2,1)S(1)} copy-done((bf16[512,1024]{1,0:T(8,128)(2,1)S(1)}, bf16[512,1024]{1,0:T(8,128)(2,1)}, u32[]{:S(2)}) %copy-start) | copy-done | bytes 1048600
  31.9 1.2 %copy-done.2 = bf16[512,1024]{1,0:T(8,128)(2,1)S(1)} copy-done((bf16[512,1024]{1,0:T(8,128)(2,1)S(1)}, bf16[512,1024]{1,0:T(8,128)(2,1)}, u32[]{:S(2)}) %copy-start.2) | copy-done | bytes 1048600
  33.1 1.2 %copy-done.4 = bf16[512,1024]{1,0:T(8,128)(2,1)S(1)} copy-done((bf16[512,1024]{1,0:T(8,128)(2,1)S(1)}, bf16[512,1024]{1,0:T(8,128)(2,1)}, u32[]{:S(2)}) %copy-start.4) | copy-done | bytes 1048600
  34.3 1.2 %copy-done.6 = bf16[512,1024]{1,0:T(8,128)(2,1)S(1)} copy-done((bf16[512,1024]{1,0:T(8,128)(2,1)S(1)}, bf16[512,1024]{1,0:T(8,128)(2,1)}, u32[]{:S(2)}) %copy-start.6) | copy-done | bytes 1048600
  35.5 0.9 %copy-done.13 = bf16[128,1024]{1,0:T(8,128)(2,1)S(1)} copy-done((bf16[128,1024]{1,0:T(8,128)(2,1)S(1)}, bf16[128,1024]{1,0:T(8,128)(2,1)}, u32[]{:S(2)}) %copy-start.13) | copy-done | bytes 262168
  36.5 1.1 %shard_map.94.own = f32[16,16,8,128]{3,2,1,0:T(8,128)S(1)} custom-call(bf16[128,1024]{1,0:T(8,128)(2,1)S(1)} %copy-done.13, bf16[512,1024]{1,0:T(8,128)(2,1)S(1)} %copy-done.6, bf16[512,1024]{1,0:T(8,128)(2,1)S(1)} %copy-done.4, bf16[512,1024]{1,0:T(8,128)(2,1)S(1)} %copy-done.2, bf16[512,1024]{1,0:T(8,128)(2,1)S(1)} %copy-done), custom_call_target="tpu_custom_call" | custom-call | flops 536870912 | bytes 5242880 | tf_op jit(solution)/shard_map/pallas_call | solution.py:235
  37.6 0.0 copy-start.8
  37.6 1.0 %copy-done.8 = f32[16,16,8,128]{3,2,1,0:T(8,128)} copy-done((f32[16,16,8,128]{3,2,1,0:T(8,128)}, f32[16,16,8,128]{3,2,1,0:T(8,128)S(1)}, u32[]{:S(2)}) %copy-start.8) | copy-done | bytes 1048600
  38.6 8.7 %all-to-all-done.1 = bf16[32,16,512]{2,1,0:T(8,128)(2,1)} async-done(((bf16[32,16,512]{2,1,0:T(8,128)(2,1)}), bf16[32,16,512]{2,1,0:T(8,128)(2,1)}, u32[]{:S(2)}, u32[]{:S(2)}) %all-to-all-start.1) | async-done | bytes 524320 | tf_op jit(solution)/shard_map/all_to_all | solution.py:349
  47.3 1.9 %shard_map.93 = bf16[512,1024]{1,0:T(8,128)(2,1)S(1)} custom-call(bf16[8,144,128]{2,1,0:T(8,128)(2,1)S(1)} %all_to_all.15.received, bf16[512,512]{1,0:T(8,128)(2,1)} %bitcast.1.window_rows), custom_call_target="tpu_custom_call" | custom-call | tf_op jit(solution)/shard_map/pallas_call | solution.py:163
  49.2 16.8 %all_to_all.16.rows = bf16[8,64,1024]{2,1,0:T(8,128)(2,1)S(1)} all-to-all(bf16[8,64,1024]{2,1,0:T(8,128)(2,1)S(1)} %bitcast.3), channel_id=1, replica_groups=mesh['chan'=32,'stack'=8] {'stack'}, dimensions={0} | all-to-all | bytes 2097152 | tf_op jit(solution)/shard_map/all_to_all | solution.py:353
  65.9 0.0 copy-done.1
  65.9 1.9 %shard_map.96.near = bf16[8,32,2048]{2,1,0:T(8,128)(2,1)S(1)} custom-call(bf16[8,64,1024]{2,1,0:T(8,128)(2,1)S(1)} %all_to_all.16.rows, bf16[512,1024]{1,0:T(8,128)(2,1)S(1)} %copy-done.7, bf16[512,1024]{1,0:T(8,128)(2,1)S(1)} %copy-done.5, bf16[512,1024]{1,0:T(8,128)(2,1)S(1)} %copy-done.3, bf16[512,1024]{1,0:T(8,128)(2,1)S(1)} %copy-done.1), custom_call_target="tpu_custom_call" | custom-call | flops 1073741824 | bytes 6291456 | tf_op jit(solution)/shard_map/pallas_call | solution.py:235
  67.9 0.0 copy-start.9
  67.9 0.0 copy-start.10
  67.9 0.0 copy-start.11
  67.9 4.1 %collective-permute-start.1 = (bf16[8,32,2048]{2,1,0:T(8,128)(2,1)S(1)}, bf16[8,32,2048]{2,1,0:T(8,128)(2,1)S(1)}, u32[]{:S(2)}, u32[]{:S(2)}) collective-permute-start(bf16[8,32,2048]{2,1,0:T(8,128)(2,1)S(1)} %shard_map.96.near), channel_id=1, source_target_pairs={{0,8},{8,0},{16,24},{24,16},{32,40},{40,32},{48,56},{56,48},{64,72... | collective-permute-start | bytes 3145736 | tf_op jit(solution)/shard_map/ppermute | solution.py:358
  72.0 1.9 %shard_map.95.near = bf16[8,32,2048]{2,1,0:T(8,128)(2,1)S(1)} custom-call(bf16[8,64,1024]{2,1,0:T(8,128)(2,1)S(1)} %all_to_all.16.rows, bf16[512,1024]{1,0:T(8,128)(2,1)S(1)} %copy-done.7, bf16[512,1024]{1,0:T(8,128)(2,1)S(1)} %copy-done.5, bf16[512,1024]{1,0:T(8,128)(2,1)S(1)} %copy-done.3, bf16[512,1024]{1,0:T(8,128)(2,1)S(1)} %copy-done.1), custom_call_target="tpu_custom_call" | custom-call | flops 1073741824 | bytes 6291456 | tf_op jit(solution)/shard_map/pallas_call | solution.py:235
  73.9 0.1 collective-permute-start
  74.0 0.3 collective-permute-done.1.far
  74.3 7.4 %shard_map.97.rest_0_ = f32[64,8,2048]{2,1,0:T(8,128)} custom-call(bf16[8,32,2048]{2,1,0:T(8,128)(2,1)S(1)} %shard_map.96.near, bf16[8,32,2048]{2,1,0:T(8,128)(2,1)S(1)} %collective-permute-done.1.far, f32[16,16,8,128]{3,2,1,0:T(8,128)S(1)} %copy-done.9, bf16[1024,1024]{1,0:T(8,128)(2,1)S(1)} %copy-done.11, bf16[1024,1024]{1,0:T(8,128)(2,1)S(1)} %copy-done.10), custom_call_target="tpu_custom_call" | custom-call | flops 3221225472 | bytes 9437184 | tf_op jit(solution)/shard_map/pallas_call | solution.py:326
  81.7 0.0 collective-permute-done.far
  81.7 7.4 %shard_map.98 = f32[64,8,2048]{2,1,0:T(8,128)} custom-call(bf16[8,32,2048]{2,1,0:T(8,128)(2,1)S(1)} %shard_map.95.near, bf16[8,32,2048]{2,1,0:T(8,128)(2,1)S(1)} %collective-permute-done.far, f32[16,16,8,128]{3,2,1,0:T(8,128)S(1)} %copy-done.9, bf16[1024,1024]{1,0:T(8,128)(2,1)S(1)} %copy-done.11, ...), custom_call_target="tpu_custom_call", output_to_operand_aliasing={{}: (5, {})} | custom-call | flops 3221225472 | bytes 9437184 | tf_op jit(solution)/shard_map/pallas_call | solution.py:326
  (18 shorter events, 0.0 us)
Async XLA Ops:
  0.0 0.8 copy-start.15
  0.8 0.7 copy-start.16
  16.8 0.9 %copy-start.14 = (bf16[256,256]{1,0:T(8,128)(2,1)S(1)}, bf16[256,256]{1,0:T(8,128)(2,1)}, u32[]{:S(2)}) copy-start(bf16[256,256]{1,0:T(8,128)(2,1)} %constant.14.clone.perm) | copy-start | bytes 393220
  19.0 0.7 copy-start.12
  19.7 27.6 %all-to-all-start.1 = ((bf16[32,16,512]{2,1,0:T(8,128)(2,1)}), bf16[32,16,512]{2,1,0:T(8,128)(2,1)}, u32[]{:S(2)}, u32[]{:S(2)}) async-start(bf16[32,16,512]{2,1,0:T(8,128)(2,1)} %get-tuple-element.9), calls=%async_computation.1 | async-start | bytes 1048576 | tf_op jit(solution)/shard_map/all_to_all | solution.py:349
  30.6 1.2 %copy-start = (bf16[512,1024]{1,0:T(8,128)(2,1)S(1)}, bf16[512,1024]{1,0:T(8,128)(2,1)}, u32[]{:S(2)}) copy-start(bf16[512,1024]{1,0:T(8,128)(2,1)} %constant.18.clone.odd_lo) | copy-start | bytes 3145732
  31.9 1.2 %copy-start.2 = (bf16[512,1024]{1,0:T(8,128)(2,1)S(1)}, bf16[512,1024]{1,0:T(8,128)(2,1)}, u32[]{:S(2)}) copy-start(bf16[512,1024]{1,0:T(8,128)(2,1)} %constant.17.clone.odd_hi) | copy-start | bytes 3145732
  33.1 1.2 %copy-start.4 = (bf16[512,1024]{1,0:T(8,128)(2,1)S(1)}, bf16[512,1024]{1,0:T(8,128)(2,1)}, u32[]{:S(2)}) copy-start(bf16[512,1024]{1,0:T(8,128)(2,1)} %constant.16.clone.even_lo) | copy-start | bytes 3145732
  34.3 1.2 %copy-start.6 = (bf16[512,1024]{1,0:T(8,128)(2,1)S(1)}, bf16[512,1024]{1,0:T(8,128)(2,1)}, u32[]{:S(2)}) copy-start(bf16[512,1024]{1,0:T(8,128)(2,1)} %constant.15.clone.even_hi) | copy-start | bytes 3145732
  35.5 0.9 %copy-start.13 = (bf16[128,1024]{1,0:T(8,128)(2,1)S(1)}, bf16[128,1024]{1,0:T(8,128)(2,1)}, u32[]{:S(2)}) copy-start(bf16[128,1024]{1,0:T(8,128)(2,1)} %copy-done.12) | copy-start | bytes 786436
  36.5 29.4 %copy-start.1 = (bf16[512,1024]{1,0:T(8,128)(2,1)S(1)}, bf16[512,1024]{1,0:T(8,128)(2,1)}, u32[]{:S(2)}) copy-start(bf16[512,1024]{1,0:T(8,128)(2,1)} %constant.18.clone.odd_lo) | copy-start | bytes 3145732
  36.5 29.4 %copy-start.3 = (bf16[512,1024]{1,0:T(8,128)(2,1)S(1)}, bf16[512,1024]{1,0:T(8,128)(2,1)}, u32[]{:S(2)}) copy-start(bf16[512,1024]{1,0:T(8,128)(2,1)} %constant.17.clone.odd_hi) | copy-start | bytes 3145732
  36.5 29.4 %copy-start.5 = (bf16[512,1024]{1,0:T(8,128)(2,1)S(1)}, bf16[512,1024]{1,0:T(8,128)(2,1)}, u32[]{:S(2)}) copy-start(bf16[512,1024]{1,0:T(8,128)(2,1)} %constant.16.clone.even_lo) | copy-start | bytes 3145732
  37.6 1.0 %copy-start.8 = (f32[16,16,8,128]{3,2,1,0:T(8,128)}, f32[16,16,8,128]{3,2,1,0:T(8,128)S(1)}, u32[]{:S(2)}) copy-start(f32[16,16,8,128]{3,2,1,0:T(8,128)S(1)} %shard_map.94.own) | copy-start | bytes 3145732
  47.3 18.7 %copy-start.7 = (bf16[512,1024]{1,0:T(8,128)(2,1)S(1)}, bf16[512,1024]{1,0:T(8,128)(2,1)}, u32[]{:S(2)}) copy-start(bf16[512,1024]{1,0:T(8,128)(2,1)} %constant.15.clone.even_hi) | copy-start | bytes 3145732
  67.9 6.4 %copy-start.9 = (f32[16,16,8,128]{3,2,1,0:T(8,128)S(1)}, f32[16,16,8,128]{3,2,1,0:T(8,128)}, u32[]{:S(2)}) copy-start(f32[16,16,8,128]{3,2,1,0:T(8,128)} %copy-done.8) | copy-start | bytes 3145732
  67.9 6.4 %copy-start.10 = (bf16[1024,1024]{1,0:T(8,128)(2,1)S(1)}, bf16[1024,1024]{1,0:T(8,128)(2,1)}, u32[]{:S(2)}) copy-start(bf16[1024,1024]{1,0:T(8,128)(2,1)} %constant.20.clone.lag_odd) | copy-start | bytes 6291460
  67.9 6.4 %copy-start.11 = (bf16[1024,1024]{1,0:T(8,128)(2,1)S(1)}, bf16[1024,1024]{1,0:T(8,128)(2,1)}, u32[]{:S(2)}) copy-start(bf16[1024,1024]{1,0:T(8,128)(2,1)} %constant.19.clone.lag_even) | copy-start | bytes 6291460
  67.9 6.4 %collective-permute-start.1 = (bf16[8,32,2048]{2,1,0:T(8,128)(2,1)S(1)}, bf16[8,32,2048]{2,1,0:T(8,128)(2,1)S(1)}, u32[]{:S(2)}, u32[]{:S(2)}) collective-permute-start(bf16[8,32,2048]{2,1,0:T(8,128)(2,1)S(1)} %shard_map.96.near), channel_id=1, source_target_pairs={{0,8},{8,0},{16,24},{24,16},{32,40},{40,32},{48,56},{56,48},{64,72... | collective-permute-start | bytes 3145736 | tf_op jit(solution)/shard_map/ppermute | solution.py:358
  73.9 7.8 %collective-permute-start = (bf16[8,32,2048]{2,1,0:T(8,128)(2,1)S(1)}, bf16[8,32,2048]{2,1,0:T(8,128)(2,1)S(1)}, u32[]{:S(2)}, u32[]{:S(2)}) collective-permute-start(bf16[8,32,2048]{2,1,0:T(8,128)(2,1)S(1)} %shard_map.95.near), channel_id=1, source_target_pairs={{0,8},{8,0},{16,24},{24,16},{32,40},{40,32},{48,56},{56,48},{64,72... | collective-permute-start | bytes 3145736 | tf_op jit(solution)/shard_map/ppermute | solution.py:358

commit v3 on v2

v3 whole, which is shorter than its diff:
```python
import functools
import math

import jax
import jax.numpy as jnp
import ml_dtypes
import numpy as np
from jax import lax
from jax.experimental import pallas as pl
from jax.experimental.pallas import tpu as pltpu
from jax.sharding import PartitionSpec as P

NS = 1024
BF = jnp.bfloat16
F32 = jnp.float32
MESH_CORES = 2
PIECES = 4


def pair_order():
    return np.concatenate([np.arange(0, 512, 2), np.arange(1, 512, 2)])


def split_table(values):
    high = values.astype(ml_dtypes.bfloat16)
    low = (values - high.astype(np.float64)).astype(ml_dtypes.bfloat16)
    return high, low


@functools.lru_cache(None)
def forward_tables():
    freq = pair_order()
    tables = []
    for odd in range(2):
        times = np.arange(odd, NS, 2)[:, None]
        phase = (times * freq[None, :] % 2048) * (2.0 * math.pi / 2048)
        cosine, sine = np.cos(phase), np.sin(phase)
        middle = (times[:, 0] * 512 % 2048) * (2.0 * math.pi / 2048)
        sine[:, 0] = -np.sin(middle) if odd else np.cos(middle)
        tables += split_table(np.concatenate([cosine, sine], axis=1))
    return tuple(tables)


@functools.lru_cache(None)
def lag_tables():
    freq = pair_order()
    lags = np.arange(1024)[None, :]
    parts = []
    for side in (freq, 1024 - freq):
        phase = (side[:, None] * lags % 2048) * (2.0 * math.pi / 2048)
        parts.append([2.0 * np.cos(phase), -2.0 * np.sin(phase)])
    middle = (512 * lags[0] % 2048) * (2.0 * math.pi / 2048)
    parts[0][0][0] = 2.0 * np.cos(middle)
    parts[0][1][0] = -2.0 * np.sin(middle)
    parts[1][0][0] = 1.0
    parts[1][1][0] = np.where(lags[0] % 2, -1.0, 1.0)
    tables = []
    for half in range(2):
        rows = slice(256 * half, 256 * half + 256)
        stacked = np.concatenate([part[rows] for pair in parts for part in pair], axis=0)
        tables.append((stacked / math.sqrt(2048)).astype(ml_dtypes.bfloat16))
    return tuple(tables)


@functools.lru_cache(None)
def deinterleave():
    table = np.zeros((256, 256), ml_dtypes.bfloat16)
    time = np.arange(256)
    table[time, (time % 2) * 128 + time // 2] = 1
    return table


def dot(a, b, dims=((1,), (0,))):
    return lax.dot_general(a, b, (dims, ((), ())), preferred_element_type=F32)


def iota(shape, dim):
    return lax.broadcasted_iota(jnp.int32, shape, dim)


VMEM = pl.BlockSpec(memory_space=pltpu.VMEM)
ANYWHERE = pl.BlockSpec(memory_space=pl.ANY)
PARAMS = pltpu.CompilerParams(vmem_limit_bytes=16 * 1024 * 1024)


def place():
    return lax.axis_index("chan") % MESH_CORES, lax.axis_index("stack")


def cost(flops, moved=2**20, special=0):
    return pl.CostEstimate(flops=flops, bytes_accessed=moved, transcendentals=special)


def spread_kernel(strain, sends, sems):
    copies = []
    for other in range(32):
        windows = strain.at[8 * (other % 2) : 8 * (other % 2) + 8]
        copies.append(pltpu.make_async_copy(windows, sends.at[other], sems.at[other]))
    for copy in copies:
        copy.start()
    for copy in copies:
        copy.wait()


def spread(strain):
    return pl.pallas_call(
        spread_kernel,
        out_shape=jax.ShapeDtypeStruct((32, 8, 8, 128), BF),
        in_specs=[ANYWHERE],
        out_specs=ANYWHERE,
        scratch_shapes=[pltpu.SemaphoreType.DMA((32,))],
        compiler_params=PARAMS,
        cost_estimate=cost(2**32),
    )(strain)


def share_kernel(strain, sources, shared):
    _, group = place()
    picks = sources[...].astype(F32)
    both = jnp.concatenate([picks, picks], axis=1)
    both = jnp.where(iota((16, 128), 1) // 64 == group % 2, both, 0.0)
    shared[:16] = strain[...]
    shared[16:] = both.reshape(2, 8, 128).astype(BF)


def share(strain, sources):
    return pl.pallas_call(
        share_kernel,
        out_shape=jax.ShapeDtypeStruct((18, 8, 128), BF),
        in_specs=[VMEM, VMEM],
        out_specs=VMEM,
        compiler_params=PARAMS,
        cost_estimate=cost(2**28),
    )(strain, sources)


def pick_kernel(window_rows, *rest):
    shared, (out, blocks, picks) = rest[:8], rest[-3:]
    core, group = place()
    for k in range(8):
        picks[group ^ k] = shared[k][16:].astype(F32).reshape(16, 128)
        blocks[group ^ k] = shared[k][:16]
    chosen = iota((16, 8), 0) == 8 * core + iota((16, 8), 1)
    chosen = chosen.astype(F32).astype(BF)
    columns = []
    for pair in range(4):
        both = (picks[2 * pair] + picks[2 * pair + 1]).astype(BF)
        columns.append(dot(both, chosen, ((0,), (0,))))
    column = jnp.concatenate(columns, axis=0)
    channel = iota((512, 256), 1).astype(F32)
    for w in range(8):
        hits = (column[:, w : w + 1] == channel).astype(F32).astype(BF)
        rows = window_rows[:, w].astype(F32).reshape(256, 128).astype(BF)
        found = dot(hits, rows).astype(BF)
        for other in range(8):
            out[other, 64 * w : 64 * w + 64] = found[64 * other : 64 * other + 64]


def pick(window_rows, shared):
    return pl.pallas_call(
        pick_kernel,
        out_shape=(
            jax.ShapeDtypeStruct((8, 512, 128), BF),
            jax.ShapeDtypeStruct((8, 16, 8, 128), BF),
        ),
        in_specs=[VMEM] * 9,
        out_specs=(VMEM, VMEM),
        scratch_shapes=[pltpu.VMEM((8, 16, 128), F32)],
        compiler_params=PARAMS,
        cost_estimate=cost(2**33),
    )(window_rows, *shared)


def whiten_strips(start, count, evens, odds, store):
    def strip(step, carry):
        at = pl.ds(pl.multiple_of(start + step * 16, 16), 16)
        first = iota((16, 128), 1) == 0
        held, total = [], None
        for k in range(4):
            near, far = slice(128 * k, 128 * k + 128), slice(512 + 128 * k, 640 + 128 * k)
            a, c, b, d = evens[at, near], evens[at, far], odds[at, near], odds[at, far]
            re_1, im_1, re_2, im_2 = a + b, c + d, a - b, c - d
            if k == 0:
                re_2, im_2 = jnp.where(first, re_1, re_2), jnp.where(first, re_2, im_2)
                re_1, im_1 = jnp.where(first, c, re_1), jnp.where(first, -d, im_1)
            power_1 = re_1 * re_1 + im_1 * im_1
            square_re, square_im = re_2 * re_2, im_2 * im_2
            power_2 = square_re + square_im
            both = power_1 + power_2
            total = both if total is None else total + both
            held.append((re_1, im_1, re_2, im_2, power_1, square_re, square_im, power_2))
        level = jnp.sum(total, axis=1, keepdims=True) * (1.0 / 1025.0)
        floor = 0.05 * level + 1e-06
        for k, (re_1, im_1, re_2, im_2, power_1, square_re, square_im, power_2) in enumerate(held):
            factor_1 = lax.rsqrt(power_1 + floor)
            if k == 0:
                factor_re = lax.rsqrt(jnp.where(first, square_re, power_2) + floor)
                factor_im = lax.rsqrt(jnp.where(first, square_im, power_2) + floor)
            else:
                factor_re = factor_im = lax.rsqrt(power_2 + floor)
            parts = (re_1 * factor_1, -im_1 * factor_1, re_2 * factor_re, im_2 * factor_im)
            for index, part in enumerate(parts):
                store(step, 8 * (k // 2) + 2 * index + k % 2, part.astype(BF))
        return carry

    lax.fori_loop(0, count // 16, strip, 0, unroll=4)


def transform(blocks, perm, table, evens, odds):
    even, odd = [], []
    for pair in range(4):
        block = jnp.concatenate(blocks[2 * pair : 2 * pair + 2], axis=1)
        apart = dot(block, perm[...]).astype(BF)
        even.append(apart[:, :128])
        odd.append(apart[:, 128:])
    even, odd = jnp.concatenate(even, axis=1), jnp.concatenate(odd, axis=1)
    evens[...] = dot(even, table[0][...]) + dot(even, table[1][...])
    odds[...] = dot(odd, table[2][...]) + dot(odd, table[3][...])


def panel_blocks(rows, half):
    blocks = []
    for k in range(8):
        wanted = rows[k].reshape(8, 64, 128)[:, 32 * half : 32 * half + 32]
        blocks.append(wanted.reshape(256, 128))
    return blocks


def panel_store(out, step, lane_group, part):
    at = pl.ds(pl.multiple_of(step % 2 * 16, 16), 16)
    out[step // 2, at, 128 * lane_group : 128 * lane_group + 128] = part


def first_white_kernel(perm, *refs):
    table, (rows, out, evens, odds) = refs[:4], refs[4:]
    transform(panel_blocks(rows, 0), perm, table, evens, odds)
    whiten_strips(0, 256, evens, odds, functools.partial(panel_store, out))


def second_white_kernel(perm, *refs):
    table, (rows, mine, out, own, evens, odds, held) = refs[:4], refs[4:]
    core, _ = place()
    parts = []
    for k, block in enumerate(panel_blocks(rows, 1)):
        parts.append(jnp.concatenate([block, mine[k].astype(F32).reshape(128, 128).astype(BF)]))
    transform(parts, perm, table, evens, odds)
    whiten_strips(0, 256, evens, odds, functools.partial(panel_store, out))

    def store(step, lane_group, part):
        held[lane_group, pl.ds(pl.multiple_of(step * 16, 16), 16)] = part.astype(F32)

    whiten_strips(256, 128, evens, odds, store)
    first = iota((8, 128), 1) == 0

    def arrange(step, carry):
        window = lax.rem(step + 8 * core, 16)
        at = pl.ds(pl.multiple_of(step * 8, 8), 8)
        for chunk in range(8):
            re = held[real_group(chunk), at]
            im = held[real_group(chunk) + 2, at]
            own[window, 3 * chunk] = re
            own[window, 3 * chunk + 1] = jnp.where(first, im, im - re) if chunk == 1 else im - re
            own[window, 3 * chunk + 2] = im + re
        return carry

    lax.fori_loop(0, 16, arrange, 0, unroll=2)


def real_group(chunk):
    lanes, pair = chunk // 2, chunk % 2
    return 8 * (lanes // 2) + lanes % 2 + 4 * pair


def white_call(kernel, count, shapes, operands, scratch=()):
    return pl.pallas_call(
        kernel,
        out_shape=shapes,
        in_specs=[VMEM] * len(operands),
        out_specs=[VMEM] * len(shapes),
        scratch_shapes=[pltpu.VMEM((count, 1024), F32), pltpu.VMEM((count, 1024), F32), *scratch],
        compiler_params=PARAMS,
        cost_estimate=cost(count * 2**23, 2**22 + count * 2**13, count * 1024),
    )(*operands)


SOURCES = 32
CHANNELS = 4


def cross_kernel(half, near, far, own, lag_even, lag_odd, *rest):
    out, raw, cross, stage, sems = rest[-5:]
    turns = 8 // CHANNELS

    def block(step, carry):
        tile, start = step // turns, step % turns * CHANNELS
        rows = pl.ds(pl.multiple_of(tile * 16, 16), 16)
        first = iota((16, 128), 1) == 0
        for chunk in range(8):
            group = real_group(chunk)
            sums = [[None] * 3 for _ in range(2 * CHANNELS)]
            for w in range(16):
                side = near if w < 8 else far
                re = side[w % 8, rows, 128 * group : 128 * group + 128].astype(F32)
                im = side[w % 8, rows, 128 * group + 256 : 128 * group + 384].astype(F32)
                both = re + (jnp.where(first, 0.0, im) if chunk == 1 else im)
                for c in range(CHANNELS):
                    at = pl.ds(start + c, 8, stride=0)
                    mine = [own[w, 3 * chunk + k, at, :] for k in range(3)]
                    for t in range(2):
                        total = sums[2 * c + t]
                        for k, picked in enumerate((both, im, re)):
                            term = picked[8 * t : 8 * t + 8] * mine[k]
                            total[k] = term if total[k] is None else total[k] + term
            for index, (a, b, c) in enumerate(sums):
                if chunk == 1:
                    edge = first[:8]
                    results = jnp.where(edge, a, a + b), jnp.where(edge, b, c - a)
                else:
                    results = a + b, c - a
                lowest = tile * 128 + index % 2 * 64 + start + index // 2
                for k, part in enumerate(results):
                    raw[group + 2 * k, pl.ds(lowest, 8, stride=8), :] = part
        return carry

    lax.fori_loop(0, SOURCES // 16 * turns, block, 0)
    for g in range(16):
        cross[:, 128 * g : 128 * g + 128] = (raw[g] * (1.0 / 16.0)).astype(BF)
    width = 1024 // PIECES
    copies = []
    for piece in range(PIECES):
        lower = slice(width * piece, width * piece + width)
        upper = slice(1024 + width * piece, 1024 + width * piece + width)
        evens = dot(cross[:, :1024], lag_even[:, lower])
        odds = dot(cross[:, 1024:], lag_odd[:, lower])
        stage[:, :, lower] = (evens - odds).reshape(SOURCES, 8, width)
        stage[:, :, upper] = (evens + odds).reshape(SOURCES, 8, width)
        for lanes in (lower, upper):
            copy = pltpu.make_async_copy(
                stage.at[:, :, lanes],
                out.at[SOURCES * half : SOURCES * half + SOURCES, :, lanes],
                sems.at[len(copies)],
            )
            copy.start()
            copies.append(copy)
    for copy in copies:
        copy.wait()


def correlate(half, near, far, own, lag, earlier=None):
    operands = [near, far, own, *lag]
    specs = [VMEM] * 5
    aliases = {}
    if earlier is not None:
        aliases = {len(operands): 0}
        operands.append(earlier)
        specs.append(ANYWHERE)
    return pl.pallas_call(
        functools.partial(cross_kernel, half),
        out_shape=jax.ShapeDtypeStruct((64, 8, 2048), F32),
        in_specs=specs,
        out_specs=ANYWHERE,
        input_output_aliases=aliases,
        scratch_shapes=[
            pltpu.VMEM((16, SOURCES * 8, 128), F32),
            pltpu.VMEM((SOURCES * 8, 2048), BF),
            pltpu.VMEM((SOURCES, 8, 2048), F32),
            pltpu.SemaphoreType.DMA((2 * PIECES,)),
        ],
        compiler_params=PARAMS,
        cost_estimate=pl.CostEstimate(
            flops=3 * 2**30, bytes_accessed=9 * 2**20, transcendentals=0
        ),
    )(*operands)


def local(strain, sources):
    window_rows = lax.all_to_all(spread(strain), "chan", 0, 0, tiled=True)
    shared = share(strain, sources)
    everyone = [shared]
    for k in range(1, 8):
        everyone.append(lax.ppermute(shared, "stack", [(j, j ^ k) for j in range(8)]))
    picked, blocks = pick(window_rows, everyone)
    rows = lax.all_to_all(picked, "stack", 0, 0, tiled=True)
    tables = [jnp.asarray(t) for t in (deinterleave(), *forward_tables())]
    lag = [jnp.asarray(t) for t in lag_tables()]
    panel = jax.ShapeDtypeStruct((8, 32, 2048), BF)
    mine = jax.ShapeDtypeStruct((16, 24, 8, 128), F32)
    swap = functools.partial(lax.ppermute, axis_name="chan", perm=[(i, i ^ 1) for i in range(32)])
    (near_0,) = white_call(first_white_kernel, 256, [panel], [*tables, rows])
    far_0 = swap(near_0)
    held = [pltpu.VMEM((16, 128, 128), F32)]
    near_1, own = white_call(second_white_kernel, 384, [panel, mine], [*tables, rows, blocks], held)
    far_1 = swap(near_1)
    result = correlate(0, near_0, far_0, own, lag)
    return correlate(1, near_1, far_1, own, lag, result)


def solution(mesh):
    placed = (P(None, "chan", "stack"), P(None, "stack"))
    return jax.shard_map(
        local, mesh=mesh, in_specs=placed, out_specs=P("stack", "chan", None), check_vma=False
    )
```

time: 89.7 us -> 75.1 us (0.84)
  starting transfers between devices: 15.1 us -> 26.9 us
  blocking collectives: 32.1 us -> 20.4 us
  local copies, waits for them, and re-layouts: 9.9 us -> 0.8 us
  waiting for transfers between devices: 8.96 us -> 5 us
  Pallas kernels: 22.9 us -> 21.4 us
    ppermute x2 -> x9, starting transfers between devices: 4.17 us -> 15.8 us  [the longest x7 11.5 us: local(): lax.ppermute(shared, 'stack', [(j, j ^ k) for j in range(8)])]
    all_to_all x2 -> x1, blocking collectives: 32.1 us -> 20.4 us  [local(): rows = lax.all_to_all(picked, 'stack', 0, 0, tiled=True)]
    unnamed x34 -> x20, local copies, waits for them, and re-layouts: 9.9 us -> 0.8 us
    all_to_all x1, waiting for transfers between devices: 8.7 us -> 0.76 us  [local(): window_rows = lax.all_to_all(spread(strain), 'chan', 0, 0, tiled=True)]
    ppermute x2 -> x9, waiting for transfers between devices: 0.26 us -> 4.24 us  [the longest x7 4.24 us: local(): lax.ppermute(shared, 'stack', [(j, j ^ k) for j in range(8)])]
    pallas_call x6 -> x5, Pallas kernels: 8.11 us -> 7.45 us  [the longest x2 5.22 us: white_call(): pl.pallas_call(kernel, out_shape=shapes, in_specs=[VMEM] * len(operands),...]
  transfers between devices with their start and end apart: 3 -> 10, of which waited for: 2 -> 4; matrix products, arithmetic and copies ran while one was open for 0% -> 0% of each run, Pallas kernels for 12% -> 14%
where the time goes in v3:
time: 75.1 us; the launch traced here: 74.8 us
  starting transfers between devices  26.9 us (36%)
  Pallas kernels  21.4 us (28%)
  blocking collectives  20.4 us (27%)
  waiting for transfers between devices  5 us (7%)
  local copies, waits for them, and re-layouts  0.8 us (1%)
    all_to_all x1, blocking collectives, local(): rows = lax.all_to_all(picked, 'stack', 0, 0, tiled=True)  20.4 us
    pallas_call x2, Pallas kernels, correlate(): pl.pallas_call(functools.partial(cross_kernel, half), out_shape=jax.Shape...  14 us
    ppermute x7, starting transfers between devices, local(): lax.ppermute(shared, 'stack', [(j, j ^ k) for j in range(8)])  11.5 us
    all_to_all x1, starting transfers between devices, local(): window_rows = lax.all_to_all(spread(strain), 'chan', 0, 0, tiled=True)  11.1 us
    pallas_call x2, Pallas kernels, white_call(): pl.pallas_call(kernel, out_shape=shapes, in_specs=[VMEM] * len(operands),...  5.22 us
    ppermute x7, waiting for transfers between devices, local(): lax.ppermute(shared, 'stack', [(j, j ^ k) for j in range(8)])  4.24 us
    ppermute x1, starting transfers between devices, local(): far_0 = swap(near_0)  4.04 us
  transfers between devices with their start and end apart: 10, of which 4 were waited for; matrix products, arithmetic and copies ran while one was open for 0% of the time, Pallas kernels for 14%

profile of v3, /device:TPU:1, one launch (start us, length us, event | category | flops | bytes accessed | tf_op | source)
XLA Modules:
  0.0 74.8 jit_solution(18350059188593408426)
XLA Ops:
  0.0 0.8 %copy-done.2 = bf16[16,8,128]{2,1,0:T(8,128)(2,1)S(1)} copy-done((bf16[16,8,128]{2,1,0:T(8,128)(2,1)S(1)}, bf16[16,8,128]{2,1,0:T(8,128)(2,1)}, u32[]{:S(2)}) %copy-start.2) | copy-done | bytes 32792
  0.8 1.1 %shard_map.91 = bf16[32,8,8,128]{3,2,1,0:T(8,128)(2,1)} custom-call(bf16[16,8,128]{2,1,0:T(8,128)(2,1)S(1)} %copy-done.2), custom_call_target="tpu_custom_call" | custom-call | flops 4294967296 | bytes 1048576 | tf_op jit(solution)/shard_map/pallas_call | solution.py:106
  1.8 11.1 %all-to-all-start = ((bf16[32,8,8,128]{3,2,1,0:T(8,128)(2,1)}), bf16[32,8,8,128]{3,2,1,0:T(8,128)(2,1)S(1)}, u32[]{:S(2)}, u32[]{:S(2)}) async-start(bf16[32,8,8,128]{3,2,1,0:T(8,128)(2,1)} %shard_map.91), calls=%async_computation | async-start | bytes 1048576 | tf_op jit(solution)/shard_map/all_to_all | solution.py:377
  12.9 0.1 shard_map.92.rest_0_
  13.0 4.9 %collective-permute-start.6 = (bf16[18,8,128]{2,1,0:T(8,128)(2,1)S(1)}, bf16[18,8,128]{2,1,0:T(8,128)(2,1)S(1)}, u32[]{:S(2)}, u32[]{:S(2)}) collective-permute-start(bf16[18,8,128]{2,1,0:T(8,128)(2,1)S(1)} %shard_map.92.rest_0_), channel_id=1, source_target_pairs={{0,7},{1,6},{2,5},{3,4},{4,3},{5,2},{6,1},{7,0},{8,15},{9,14},{10,... | collective-permute-start | bytes 110600 | tf_op jit(solution)/shard_map/ppermute | solution.py:381
  17.9 0.6 collective-permute-start.5
  18.5 2.3 %collective-permute-start.4 = (bf16[18,8,128]{2,1,0:T(8,128)(2,1)S(1)}, bf16[18,8,128]{2,1,0:T(8,128)(2,1)S(1)}, u32[]{:S(2)}, u32[]{:S(2)}) collective-permute-start(bf16[18,8,128]{2,1,0:T(8,128)(2,1)S(1)} %shard_map.92.rest_0_), channel_id=1, source_target_pairs={{0,5},{1,4},{2,7},{3,6},{4,1},{5,0},{6,3},{7,2},{8,13},{9,12},{10,... | collective-permute-start | bytes 110600 | tf_op jit(solution)/shard_map/ppermute | solution.py:381
  20.9 0.5 collective-permute-start.3
  21.4 2.7 %collective-permute-start.2 = (bf16[18,8,128]{2,1,0:T(8,128)(2,1)S(1)}, bf16[18,8,128]{2,1,0:T(8,128)(2,1)S(1)}, u32[]{:S(2)}, u32[]{:S(2)}) collective-permute-start(bf16[18,8,128]{2,1,0:T(8,128)(2,1)S(1)} %shard_map.92.rest_0_), channel_id=1, source_target_pairs={{0,3},{1,2},{2,1},{3,0},{4,7},{5,6},{6,5},{7,4},{8,11},{9,10},{10,... | collective-permute-start | bytes 110600 | tf_op jit(solution)/shard_map/ppermute | solution.py:381
  24.1 0.0 collective-permute-done.6.rest_7_
  24.1 0.3 collective-permute-start.1
  24.5 0.6 collective-permute-done.5.rest_6_
  25.1 0.0 collective-permute-start
  25.1 0.0 collective-permute-done.4.rest_5_
  25.1 1.4 %collective-permute-done.3.rest_4_ = bf16[18,8,128]{2,1,0:T(8,128)(2,1)S(1)} collective-permute-done((bf16[18,8,128]{2,1,0:T(8,128)(2,1)S(1)}, bf16[18,8,128]{2,1,0:T(8,128)(2,1)S(1)}, u32[]{:S(2)}, u32[]{:S(2)}) %collective-permute-start.3) | collective-permute-done | bytes 36896 | tf_op jit(solution)/shard_map/ppermute | solution.py:381
  26.5 0.0 collective-permute-done.2.rest_3_
  26.5 2.2 %collective-permute-done.1.rest_2_ = bf16[18,8,128]{2,1,0:T(8,128)(2,1)S(1)} collective-permute-done((bf16[18,8,128]{2,1,0:T(8,128)(2,1)S(1)}, bf16[18,8,128]{2,1,0:T(8,128)(2,1)S(1)}, u32[]{:S(2)}, u32[]{:S(2)}) %collective-permute-start.1) | collective-permute-done | bytes 36896 | tf_op jit(solution)/shard_map/ppermute | solution.py:381
  28.7 0.0 collective-permute-done.rest_1_
  28.7 0.8 %all-to-all-done.window_rows = bf16[32,8,8,128]{3,2,1,0:T(8,128)(2,1)S(1)} async-done(((bf16[32,8,8,128]{3,2,1,0:T(8,128)(2,1)}), bf16[32,8,8,128]{3,2,1,0:T(8,128)(2,1)S(1)}, u32[]{:S(2)}, u32[]{:S(2)}) %all-to-all-start) | async-done | bytes 524320 | tf_op jit(solution)/shard_map/all_to_all | solution.py:377
  29.5 1.1 %shard_map.93 = (bf16[8,512,128]{2,1,0:T(8,128)(2,1)S(1)}, bf16[8,16,8,128]{3,2,1,0:T(8,128)(2,1)S(1)}) custom-call(bf16[32,8,8,128]{3,2,1,0:T(8,128)(2,1)S(1)} %all-to-all-done.window_rows, bf16[18,8,128]{2,1,0:T(8,128)(2,1)S(1)} %shard_map.92.rest_0_, bf16[18,8,128]{2,1,0:T(8,128)(2,1)S(1)} %collective-permute-done.rest_1_, ...), custom_call_target="tpu_custom_call" | custom-call | flops 8589934592 | bytes 1048576 | tf_op jit(solution)/shard_map/pallas_call | solution.py:160
  30.6 0.0 copy-start.5
  30.6 0.0 copy-start.6
  30.6 20.4 %all_to_all.10.refs_4_ = bf16[8,512,128]{2,1,0:T(8,128)(2,1)S(1)} all-to-all(bf16[8,512,128]{2,1,0:T(8,128)(2,1)S(1)} %get-tuple-element.9), channel_id=1, replica_groups=mesh['chan'=32,'stack'=8] {'stack'}, dimensions={0} | all-to-all | bytes 2097152 | tf_op jit(solution)/shard_map/all_to_all | solution.py:383
  51.1 2.1 %shard_map.95.near = bf16[8,32,2048]{2,1,0:T(8,128)(2,1)S(1)} custom-call(bf16[256,256]{1,0:T(8,128)(2,1)S(1)} %copy-done.9, bf16[512,1024]{1,0:T(8,128)(2,1)S(1)} %copy-done.8, bf16[512,1024]{1,0:T(8,128)(2,1)S(1)} %copy-done.7, bf16[512,1024]{1,0:T(8,128)(2,1)S(1)} %copy-done.6, bf16[512,1024]{1,0:T(8,128)(2,1)S(1)} %copy-done.5, ...), custom_call_target="tpu_custom_call" | custom-call | flops 2147483648 | bytes 6291456 | tf_op jit(solution)/shard_map/pallas_call | solution.py:275
  53.1 4.0 %collective-permute-start.8 = (bf16[8,32,2048]{2,1,0:T(8,128)(2,1)S(1)}, bf16[8,32,2048]{2,1,0:T(8,128)(2,1)S(1)}, u32[]{:S(2)}, u32[]{:S(2)}) collective-permute-start(bf16[8,32,2048]{2,1,0:T(8,128)(2,1)S(1)} %shard_map.95.near), channel_id=1, source_target_pairs={{0,8},{8,0},{16,24},{24,16},{32,40},{40,32},{48,56},{56,48},{64,72... | collective-permute-start | bytes 3145736 | tf_op jit(solution)/shard_map/ppermute | solution.py:390
  57.2 3.2 %shard_map.94 = (bf16[8,32,2048]{2,1,0:T(8,128)(2,1)S(1)}, f32[16,24,8,128]{3,2,1,0:T(8,128)S(1)}) custom-call(bf16[256,256]{1,0:T(8,128)(2,1)S(1)} %copy-done.9, bf16[512,1024]{1,0:T(8,128)(2,1)S(1)} %copy-done.8, bf16[512,1024]{1,0:T(8,128)(2,1)S(1)} %copy-done.7, bf16[512,1024]{1,0:T(8,128)(2,1)S(1)} %copy-done.6, bf16[512,1024]{1,0:T(8,128)(2,1)S(1)} %copy-done.5, ...), custom_call_target="tpu_custom_call" | custom-call | flops 3221225472 | bytes 7340032 | tf_op jit(solution)/shard_map/pallas_call | solution.py:275
  60.4 0.3 collective-permute-start.7
  60.7 0.0 collective-permute-done.8.far
  60.7 0.0 copy-done
  60.7 7.0 %shard_map.96.rest_0_ = f32[64,8,2048]{2,1,0:T(8,128)} custom-call(bf16[8,32,2048]{2,1,0:T(8,128)(2,1)S(1)} %shard_map.95.near, bf16[8,32,2048]{2,1,0:T(8,128)(2,1)S(1)} %collective-permute-done.8.far, f32[16,24,8,128]{3,2,1,0:T(8,128)S(1)} %get-tuple-element.12.own, bf16[1024,1024]{1,0:T(8,128)(2,1)S(1)} %copy-done.1, bf16[1024,1024]{1,0:T(8,128)(2,1)S(1)} %copy-done), custom_call_target="tpu_custom_call" | custom-call | flops 3221225472 | bytes 9437184 | tf_op jit(solution)/shard_map/pallas_call | solution.py:357
  67.7 0.0 collective-permute-done.7.far
  67.7 7.0 %shard_map.97 = f32[64,8,2048]{2,1,0:T(8,128)} custom-call(bf16[8,32,2048]{2,1,0:T(8,128)(2,1)S(1)} %get-tuple-element.11.near, bf16[8,32,2048]{2,1,0:T(8,128)(2,1)S(1)} %collective-permute-done.7.far, f32[16,24,8,128]{3,2,1,0:T(8,128)S(1)} %get-tuple-element.12.own, bf16[1024,1024]{1,0:T(8,128)(2,1)S(1)} %copy-done.1, ...), custom_call_target="tpu_custom_call", output_to_operand_aliasing={{}: (5, {})} | custom-call | flops 3221225472 | bytes 9437184 | tf_op jit(solution)/shard_map/pallas_call | solution.py:357
  (16 shorter events, 0.0 us)
Async XLA Ops:
  0.0 0.8 %copy-start.2 = (bf16[16,8,128]{2,1,0:T(8,128)(2,1)S(1)}, bf16[16,8,128]{2,1,0:T(8,128)(2,1)}, u32[]{:S(2)}) copy-start(bf16[16,8,128]{2,1,0:T(8,128)(2,1)} %strain.3) | copy-start | bytes 98308
  0.8 12.1 %copy-start.3 = (bf16[16,8,128]{2,1,0:T(8,128)(2,1)S(1)}, bf16[16,8,128]{2,1,0:T(8,128)(2,1)}, u32[]{:S(2)}) copy-start(bf16[16,8,128]{2,1,0:T(8,128)(2,1)} %strain.3) | copy-start | bytes 98308
  0.8 12.1 %copy-start.4 = (s32[16,64]{1,0:T(8,128)S(1)}, s32[16,64]{1,0:T(8,128)}, u32[]{:S(2)}) copy-start(s32[16,64]{1,0:T(8,128)} %sources.1) | copy-start | bytes 12292
  1.8 27.6 %all-to-all-start = ((bf16[32,8,8,128]{3,2,1,0:T(8,128)(2,1)}), bf16[32,8,8,128]{3,2,1,0:T(8,128)(2,1)S(1)}, u32[]{:S(2)}, u32[]{:S(2)}) async-start(bf16[32,8,8,128]{3,2,1,0:T(8,128)(2,1)} %shard_map.91), calls=%async_computation | async-start | bytes 1048576 | tf_op jit(solution)/shard_map/all_to_all | solution.py:377
  13.0 11.1 %collective-permute-start.6 = (bf16[18,8,128]{2,1,0:T(8,128)(2,1)S(1)}, bf16[18,8,128]{2,1,0:T(8,128)(2,1)S(1)}, u32[]{:S(2)}, u32[]{:S(2)}) collective-permute-start(bf16[18,8,128]{2,1,0:T(8,128)(2,1)S(1)} %shard_map.92.rest_0_), channel_id=1, source_target_pairs={{0,7},{1,6},{2,5},{3,4},{4,3},{5,2},{6,1},{7,0},{8,15},{9,14},{10,... | collective-permute-start | bytes 110600 | tf_op jit(solution)/shard_map/ppermute | solution.py:381
  17.9 7.1 %collective-permute-start.5 = (bf16[18,8,128]{2,1,0:T(8,128)(2,1)S(1)}, bf16[18,8,128]{2,1,0:T(8,128)(2,1)S(1)}, u32[]{:S(2)}, u32[]{:S(2)}) collective-permute-start(bf16[18,8,128]{2,1,0:T(8,128)(2,1)S(1)} %shard_map.92.rest_0_), channel_id=1, source_target_pairs={{0,6},{1,7},{2,4},{3,5},{4,2},{5,3},{6,0},{7,1},{8,14},{9,15},{10,... | collective-permute-start | bytes 110600 | tf_op jit(solution)/shard_map/ppermute | solution.py:381
  18.5 6.6 %collective-permute-start.4 = (bf16[18,8,128]{2,1,0:T(8,128)(2,1)S(1)}, bf16[18,8,128]{2,1,0:T(8,128)(2,1)S(1)}, u32[]{:S(2)}, u32[]{:S(2)}) collective-permute-start(bf16[18,8,128]{2,1,0:T(8,128)(2,1)S(1)} %shard_map.92.rest_0_), channel_id=1, source_target_pairs={{0,5},{1,4},{2,7},{3,6},{4,1},{5,0},{6,3},{7,2},{8,13},{9,12},{10,... | collective-permute-start | bytes 110600 | tf_op jit(solution)/shard_map/ppermute | solution.py:381
  20.9 5.6 %collective-permute-start.3 = (bf16[18,8,128]{2,1,0:T(8,128)(2,1)S(1)}, bf16[18,8,128]{2,1,0:T(8,128)(2,1)S(1)}, u32[]{:S(2)}, u32[]{:S(2)}) collective-permute-start(bf16[18,8,128]{2,1,0:T(8,128)(2,1)S(1)} %shard_map.92.rest_0_), channel_id=1, source_target_pairs={{0,4},{1,5},{2,6},{3,7},{4,0},{5,1},{6,2},{7,3},{8,12},{9,13},{10,... | collective-permute-start | bytes 110600 | tf_op jit(solution)/shard_map/ppermute | solution.py:381
  21.4 5.1 %collective-permute-start.2 = (bf16[18,8,128]{2,1,0:T(8,128)(2,1)S(1)}, bf16[18,8,128]{2,1,0:T(8,128)(2,1)S(1)}, u32[]{:S(2)}, u32[]{:S(2)}) collective-permute-start(bf16[18,8,128]{2,1,0:T(8,128)(2,1)S(1)} %shard_map.92.rest_0_), channel_id=1, source_target_pairs={{0,3},{1,2},{2,1},{3,0},{4,7},{5,6},{6,5},{7,4},{8,11},{9,10},{10,... | collective-permute-start | bytes 110600 | tf_op jit(solution)/shard_map/ppermute | solution.py:381
  24.1 4.6 %collective-permute-start.1 = (bf16[18,8,128]{2,1,0:T(8,128)(2,1)S(1)}, bf16[18,8,128]{2,1,0:T(8,128)(2,1)S(1)}, u32[]{:S(2)}, u32[]{:S(2)}) collective-permute-start(bf16[18,8,128]{2,1,0:T(8,128)(2,1)S(1)} %shard_map.92.rest_0_), channel_id=1, source_target_pairs={{0,2},{1,3},{2,0},{3,1},{4,6},{5,7},{6,4},{7,5},{8,10},{9,11},{10,... | collective-permute-start | bytes 110600 | tf_op jit(solution)/shard_map/ppermute | solution.py:381
  25.1 3.6 %collective-permute-start = (bf16[18,8,128]{2,1,0:T(8,128)(2,1)S(1)}, bf16[18,8,128]{2,1,0:T(8,128)(2,1)S(1)}, u32[]{:S(2)}, u32[]{:S(2)}) collective-permute-start(bf16[18,8,128]{2,1,0:T(8,128)(2,1)S(1)} %shard_map.92.rest_0_), channel_id=1, source_target_pairs={{0,1},{1,0},{2,3},{3,2},{4,5},{5,4},{6,7},{7,6},{8,9},{9,8},{10,11... | collective-permute-start | bytes 110600 | tf_op jit(solution)/shard_map/ppermute | solution.py:381
  29.5 21.6 %copy-start.7 = (bf16[512,1024]{1,0:T(8,128)(2,1)S(1)}, bf16[512,1024]{1,0:T(8,128)(2,1)}, u32[]{:S(2)}) copy-start(bf16[512,1024]{1,0:T(8,128)(2,1)} %constant.16.clone.refs_1_) | copy-start | bytes 3145732
  29.5 21.6 %copy-start.8 = (bf16[512,1024]{1,0:T(8,128)(2,1)S(1)}, bf16[512,1024]{1,0:T(8,128)(2,1)}, u32[]{:S(2)}) copy-start(bf16[512,1024]{1,0:T(8,128)(2,1)} %constant.15.clone.refs_0_) | copy-start | bytes 3145732
  29.5 21.6 %copy-start.9 = (bf16[256,256]{1,0:T(8,128)(2,1)S(1)}, bf16[256,256]{1,0:T(8,128)(2,1)}, u32[]{:S(2)}) copy-start(bf16[256,256]{1,0:T(8,128)(2,1)} %constant.14.clone.perm) | copy-start | bytes 393220
  30.6 20.5 %copy-start.5 = (bf16[512,1024]{1,0:T(8,128)(2,1)S(1)}, bf16[512,1024]{1,0:T(8,128)(2,1)}, u32[]{:S(2)}) copy-start(bf16[512,1024]{1,0:T(8,128)(2,1)} %constant.18.clone.refs_3_) | copy-start | bytes 3145732
  30.6 20.5 %copy-start.6 = (bf16[512,1024]{1,0:T(8,128)(2,1)S(1)}, bf16[512,1024]{1,0:T(8,128)(2,1)}, u32[]{:S(2)}) copy-start(bf16[512,1024]{1,0:T(8,128)(2,1)} %constant.17.clone.refs_2_) | copy-start | bytes 3145732
  53.1 7.5 %collective-permute-start.8 = (bf16[8,32,2048]{2,1,0:T(8,128)(2,1)S(1)}, bf16[8,32,2048]{2,1,0:T(8,128)(2,1)S(1)}, u32[]{:S(2)}, u32[]{:S(2)}) collective-permute-start(bf16[8,32,2048]{2,1,0:T(8,128)(2,1)S(1)} %shard_map.95.near), channel_id=1, source_target_pairs={{0,8},{8,0},{16,24},{24,16},{32,40},{40,32},{48,56},{56,48},{64,72... | collective-permute-start | bytes 3145736 | tf_op jit(solution)/shard_map/ppermute | solution.py:390
  57.2 3.5 %copy-start = (bf16[1024,1024]{1,0:T(8,128)(2,1)S(1)}, bf16[1024,1024]{1,0:T(8,128)(2,1)}, u32[]{:S(2)}) copy-start(bf16[1024,1024]{1,0:T(8,128)(2,1)} %constant.20.clone.lag_odd) | copy-start | bytes 6291460
  57.2 3.5 %copy-start.1 = (bf16[1024,1024]{1,0:T(8,128)(2,1)S(1)}, bf16[1024,1024]{1,0:T(8,128)(2,1)}, u32[]{:S(2)}) copy-start(bf16[1024,1024]{1,0:T(8,128)(2,1)} %constant.19.clone.lag_even) | copy-start | bytes 6291460
  60.4 7.3 %collective-permute-start.7 = (bf16[8,32,2048]{2,1,0:T(8,128)(2,1)S(1)}, bf16[8,32,2048]{2,1,0:T(8,128)(2,1)S(1)}, u32[]{:S(2)}, u32[]{:S(2)}) collective-permute-start(bf16[8,32,2048]{2,1,0:T(8,128)(2,1)S(1)} %get-tuple-element.11.near), channel_id=1, source_target_pairs={{0,8},{8,0},{16,24},{24,16},{32,40},{40,32},{48,56},{56,48},{64,72... | collective-permute-start | bytes 3145736 | tf_op jit(solution)/shard_map/ppermute | solution.py:393

commit v4 on v3

--- a/solution.py
+++ b/solution.py
@@ -138,8 +138,9 @@
     shared, (out, blocks, picks) = rest[:8], rest[-3:]
     core, group = place()
     for k in range(8):
-        picks[group ^ k] = shared[k][16:].astype(F32).reshape(16, 128)
-        blocks[group ^ k] = shared[k][:16]
+        sender = group ^ (k + core * (8 - 2 * k) if k else 0)
+        picks[sender] = shared[k][16:].astype(F32).reshape(16, 128)
+        blocks[sender] = shared[k][:16]
     chosen = iota((16, 8), 0) == 8 * core + iota((16, 8), 1)
     chosen = chosen.astype(F32).astype(BF)
     columns = []
@@ -256,8 +257,8 @@
         window = lax.rem(step + 8 * core, 16)
         at = pl.ds(pl.multiple_of(step * 8, 8), 8)
         for chunk in range(8):
-            re = held[real_group(chunk), at]
-            im = held[real_group(chunk) + 2, at]
+            re = held[real_group(chunk), at] * (1.0 / 16.0)
+            im = held[real_group(chunk) + 2, at] * (1.0 / 16.0)
             own[window, 3 * chunk] = re
             own[window, 3 * chunk + 1] = jnp.where(first, im, im - re) if chunk == 1 else im - re
             own[window, 3 * chunk + 2] = im + re
@@ -283,94 +284,107 @@
     )(*operands)
 
 
-SOURCES = 32
-CHANNELS = 4
-
-
-def cross_kernel(half, near, far, own, lag_even, lag_odd, *rest):
-    out, raw, cross, stage, sems = rest[-5:]
-    turns = 8 // CHANNELS
-
-    def block(step, carry):
-        tile, start = step // turns, step % turns * CHANNELS
-        rows = pl.ds(pl.multiple_of(tile * 16, 16), 16)
-        first = iota((16, 128), 1) == 0
-        for chunk in range(8):
-            group = real_group(chunk)
-            sums = [[None] * 3 for _ in range(2 * CHANNELS)]
-            for w in range(16):
-                side = near if w < 8 else far
-                re = side[w % 8, rows, 128 * group : 128 * group + 128].astype(F32)
-                im = side[w % 8, rows, 128 * group + 256 : 128 * group + 384].astype(F32)
-                both = re + (jnp.where(first, 0.0, im) if chunk == 1 else im)
-                for c in range(CHANNELS):
-                    at = pl.ds(start + c, 8, stride=0)
-                    mine = [own[w, 3 * chunk + k, at, :] for k in range(3)]
-                    for t in range(2):
-                        total = sums[2 * c + t]
-                        for k, picked in enumerate((both, im, re)):
-                            term = picked[8 * t : 8 * t + 8] * mine[k]
-                            total[k] = term if total[k] is None else total[k] + term
-            for index, (a, b, c) in enumerate(sums):
-                if chunk == 1:
-                    edge = first[:8]
-                    results = jnp.where(edge, a, a + b), jnp.where(edge, b, c - a)
-                else:
-                    results = a + b, c - a
-                lowest = tile * 128 + index % 2 * 64 + start + index // 2
-                for k, part in enumerate(results):
-                    raw[group + 2 * k, pl.ds(lowest, 8, stride=8), :] = part
-        return carry
-
-    lax.fori_loop(0, SOURCES // 16 * turns, block, 0)
+def cross_block(tile, near, far, own, raw):
+    rows = slice(16 * tile, 16 * tile + 16)
+    first = iota((16, 128), 1) == 0
+    for chunk in range(8):
+        group = real_group(chunk)
+        sums = [[None] * 3 for _ in range(16)]
+        for w in range(16):
+            side = near if w < 8 else far
+            re = side[w % 8, rows, 128 * group : 128 * group + 128].astype(F32)
+            im = side[w % 8, rows, 128 * group + 256 : 128 * group + 384].astype(F32)
+            both = re + (jnp.where(first, 0.0, im) if chunk == 1 else im)
+            for c in range(8):
+                at = pl.ds(c, 8, stride=0)
+                mine = [own[w, 3 * chunk + k, at, :] for k in range(3)]
+                for t in range(2):
+                    total = sums[2 * c + t]
+                    for k, picked in enumerate((both, im, re)):
+                        term = picked[8 * t : 8 * t + 8] * mine[k]
+                        total[k] = term if total[k] is None else total[k] + term
+        for index, (a, b, c) in enumerate(sums):
+            if chunk == 1:
+                edge = first[:8]
+                results = jnp.where(edge, a, a + b), jnp.where(edge, b, c - a)
+            else:
+                results = a + b, c - a
+            for k, part in enumerate(results):
+                raw[group + 2 * k, pl.ds(index % 2 * 64 + index // 2, 8, stride=8), :] = part
+
+
+def round_cross(raw, cross):
     for g in range(16):
-        cross[:, 128 * g : 128 * g + 128] = (raw[g] * (1.0 / 16.0)).astype(BF)
+        cross[:, 128 * g : 128 * g + 128] = raw[g].astype(BF)
+
+
+def cross_tiles(near, far, own, raw, cross):
+    for tile in range(2):
+        cross_block(tile, near, far, own, raw)
+        for g in range(16):
+            cross[128 * tile : 128 * tile + 128, 128 * g : 128 * g + 128] = raw[g].astype(BF)
+
+
+def lag_products(half, cross, lag_even, lag_odd, out, stage, sems):
+    copies = []
     width = 1024 // PIECES
-    copies = []
     for piece in range(PIECES):
         lower = slice(width * piece, width * piece + width)
         upper = slice(1024 + width * piece, 1024 + width * piece + width)
         evens = dot(cross[:, :1024], lag_even[:, lower])
         odds = dot(cross[:, 1024:], lag_odd[:, lower])
-        stage[:, :, lower] = (evens - odds).reshape(SOURCES, 8, width)
-        stage[:, :, upper] = (evens + odds).reshape(SOURCES, 8, width)
-        for lanes in (lower, upper):
+        stage[half, :, :, lower] = (evens - odds).reshape(32, 8, width)
+        stage[half, :, :, upper] = (evens + odds).reshape(32, 8, width)
+        for k, lanes in enumerate((lower, upper)):
             copy = pltpu.make_async_copy(
-                stage.at[:, :, lanes],
-                out.at[SOURCES * half : SOURCES * half + SOURCES, :, lanes],
-                sems.at[len(copies)],
+                stage.at[half, :, :, lanes],
+                out.at[32 * half : 32 * half + 32, :, lanes],
+                sems.at[half, 2 * piece + k],
             )
             copy.start()
             copies.append(copy)
+    return copies
+
+
+def first_cross_kernel(near, far, own, cross, raw):
+    cross_tiles(near, far, own, raw, cross)
+
+
+def first_cross(near, far, own):
+    return pl.pallas_call(
+        first_cross_kernel,
+        out_shape=jax.ShapeDtypeStruct((256, 2048), BF),
+        in_specs=[VMEM] * 3,
+        out_specs=VMEM,
+        scratch_shapes=[pltpu.VMEM((16, 128, 128), F32)],
+        compiler_params=PARAMS,
+        cost_estimate=cost(2**32, 9 * 2**20),
+    )(near, far, own)
+
+
+def last_kernel(near, far, own, lag_even, lag_odd, before, out, raw, cross, stage, sems):
+    copies = lag_products(0, before, lag_even, lag_odd, out, stage, sems)
+    cross_tiles(near, far, own, raw, cross)
+    copies += lag_products(1, cross, lag_even, lag_odd, out, stage, sems)
     for copy in copies:
         copy.wait()
 
 
-def correlate(half, near, far, own, lag, earlier=None):
-    operands = [near, far, own, *lag]
-    specs = [VMEM] * 5
-    aliases = {}
-    if earlier is not None:
-        aliases = {len(operands): 0}
-        operands.append(earlier)
-        specs.append(ANYWHERE)
-    return pl.pallas_call(
-        functools.partial(cross_kernel, half),
+def correlate(near, far, own, lag, before):
+    return pl.pallas_call(
+        last_kernel,
         out_shape=jax.ShapeDtypeStruct((64, 8, 2048), F32),
-        in_specs=specs,
+        in_specs=[VMEM] * 6,
         out_specs=ANYWHERE,
-        input_output_aliases=aliases,
         scratch_shapes=[
-            pltpu.VMEM((16, SOURCES * 8, 128), F32),
-            pltpu.VMEM((SOURCES * 8, 2048), BF),
-            pltpu.VMEM((SOURCES, 8, 2048), F32),
-            pltpu.SemaphoreType.DMA((2 * PIECES,)),
+            pltpu.VMEM((16, 128, 128), F32),
+            pltpu.VMEM((256, 2048), BF),
+            pltpu.VMEM((2, 32, 8, 2048), F32),
+            pltpu.SemaphoreType.DMA((2, 2 * PIECES)),
         ],
         compiler_params=PARAMS,
-        cost_estimate=pl.CostEstimate(
-            flops=3 * 2**30, bytes_accessed=9 * 2**20, transcendentals=0
-        ),
-    )(*operands)
+        cost_estimate=cost(2**33, 9 * 2**20),
+    )(near, far, own, *lag, before)
 
 
 def local(strain, sources):
@@ -378,7 +392,9 @@
     shared = share(strain, sources)
     everyone = [shared]
     for k in range(1, 8):
-        everyone.append(lax.ppermute(shared, "stack", [(j, j ^ k) for j in range(8)]))
+        turns = (k, 8 - k)
+        pairs = [(8 * i + j, 8 * i + (j ^ turns[i % 2])) for i in range(32) for j in range(8)]
+        everyone.append(lax.ppermute(shared, ("chan", "stack"), pairs))
     picked, blocks = pick(window_rows, everyone)
     rows = lax.all_to_all(picked, "stack", 0, 0, tiled=True)
     tables = [jnp.asarray(t) for t in (deinterleave(), *forward_tables())]
@@ -391,8 +407,7 @@
     held = [pltpu.VMEM((16, 128, 128), F32)]
     near_1, own = white_call(second_white_kernel, 384, [panel, mine], [*tables, rows, blocks], held)
     far_1 = swap(near_1)
-    result = correlate(0, near_0, far_0, own, lag)
-    return correlate(1, near_1, far_1, own, lag, result)
+    return correlate(near_1, far_1, own, lag, first_cross(near_0, far_0, own))
 
 
 def solution(mesh):

time: 75.1 us -> 72.2 us (0.961)
  Pallas kernels: 21.4 us -> 18.5 us
  blocking collectives: 20.4 us -> 17.7 us
  starting transfers between devices: 26.9 us -> 28.3 us
  waiting for transfers between devices: 5 us -> 6.24 us
    pallas_call x2, Pallas kernels: 14 us -> 11.1 us  [the longest x1 7.16 us: correlate(): pl.pallas_call(last_kernel, out_shape=jax.ShapeDtypeStruct((64, 8, 2048),...]
    all_to_all x1, blocking collectives: 20.4 us -> 17.7 us  [local(): rows = lax.all_to_all(picked, 'stack', 0, 0, tiled=True)]
    ppermute x7, waiting for transfers between devices: 4.24 us -> 6.23 us  [local(): everyone.append(lax.ppermute(shared, ('chan', 'stack'), pairs))]
    ppermute x7, starting transfers between devices: 11.5 us -> 12.9 us  [local(): everyone.append(lax.ppermute(shared, ('chan', 'stack'), pairs))]
    all_to_all x1, waiting for transfers between devices: 0.76 us -> 0.01 us  [local(): window_rows = lax.all_to_all(spread(strain), 'chan', 0, 0, tiled=True)]
  transfers between devices with their start and end apart: 10 -> 10, of which waited for: 4 -> 2; matrix products, arithmetic and copies ran while one was open for 0% -> 0% of each run, Pallas kernels for 14% -> 10%
where the time goes in v4:
time: 72.2 us; the launch traced here: 71.9 us
  starting transfers between devices  28.3 us (39%)
  Pallas kernels  18.5 us (26%)
  blocking collectives  17.7 us (25%)
  waiting for transfers between devices  6.24 us (9%)
  local copies, waits for them, and re-layouts  0.8 us (1%)
    all_to_all x1, blocking collectives, local(): rows = lax.all_to_all(picked, 'stack', 0, 0, tiled=True)  17.7 us
    ppermute x7, starting transfers between devices, local(): everyone.append(lax.ppermute(shared, ('chan', 'stack'), pairs))  12.9 us
    all_to_all x1, starting transfers between devices, local(): window_rows = lax.all_to_all(spread(strain), 'chan', 0, 0, tiled=True)  11.1 us
    pallas_call x1, Pallas kernels, correlate(): pl.pallas_call(last_kernel, out_shape=jax.ShapeDtypeStruct((64, 8, 2048),...  7.16 us
    ppermute x7, waiting for transfers between devices, local(): everyone.append(lax.ppermute(shared, ('chan', 'stack'), pairs))  6.23 us
    pallas_call x2, Pallas kernels, white_call(): pl.pallas_call(kernel, out_shape=shapes, in_specs=[VMEM] * len(operands),...  5.23 us
    ppermute x1, starting transfers between devices, local(): far_0 = swap(near_0)  4.04 us
    pallas_call x1, Pallas kernels, first_cross(): pl.pallas_call(first_cross_kernel, out_shape=jax.ShapeDtypeStruct((256, 2...  3.92 us
  transfers between devices with their start and end apart: 10, of which 2 were waited for; matrix products, arithmetic and copies ran while one was open for 0% of the time, Pallas kernels for 10%

profile of v4, /device:TPU:1, one launch (start us, length us, event | category | flops | bytes accessed | tf_op | source)
XLA Modules:
  0.0 71.9 jit_solution(15776185656180329881)
XLA Ops:
  0.0 0.8 %copy-done = bf16[16,8,128]{2,1,0:T(8,128)(2,1)S(1)} copy-done((bf16[16,8,128]{2,1,0:T(8,128)(2,1)S(1)}, bf16[16,8,128]{2,1,0:T(8,128)(2,1)}, u32[]{:S(2)}) %copy-start) | copy-done | bytes 32792
  0.8 1.1 %shard_map.91 = bf16[32,8,8,128]{3,2,1,0:T(8,128)(2,1)} custom-call(bf16[16,8,128]{2,1,0:T(8,128)(2,1)S(1)} %copy-done), custom_call_target="tpu_custom_call" | custom-call | flops 4294967296 | bytes 1048576 | tf_op jit(solution)/shard_map/pallas_call | solution.py:106
  1.8 11.1 %all-to-all-start = ((bf16[32,8,8,128]{3,2,1,0:T(8,128)(2,1)}), bf16[32,8,8,128]{3,2,1,0:T(8,128)(2,1)S(1)}, u32[]{:S(2)}, u32[]{:S(2)}) async-start(bf16[32,8,8,128]{3,2,1,0:T(8,128)(2,1)} %shard_map.91), calls=%async_computation | async-start | bytes 1048576 | tf_op jit(solution)/shard_map/all_to_all | solution.py:391
  12.9 0.1 shard_map.92.rest_0_
  13.0 1.3 %collective-permute-start.6 = (bf16[18,8,128]{2,1,0:T(8,128)(2,1)S(1)}, bf16[18,8,128]{2,1,0:T(8,128)(2,1)S(1)}, u32[]{:S(2)}, u32[]{:S(2)}) collective-permute-start(bf16[18,8,128]{2,1,0:T(8,128)(2,1)S(1)} %shard_map.92.rest_0_), channel_id=1, source_target_pairs={{0,7},{1,6},{2,5},{3,4},{4,3},{5,2},{6,1},{7,0},{8,9},{9,8},{10,11... | collective-permute-start | bytes 110600 | tf_op jit(solution)/shard_map/ppermute | solution.py:397
  14.3 2.6 %collective-permute-start.5 = (bf16[18,8,128]{2,1,0:T(8,128)(2,1)S(1)}, bf16[18,8,128]{2,1,0:T(8,128)(2,1)S(1)}, u32[]{:S(2)}, u32[]{:S(2)}) collective-permute-start(bf16[18,8,128]{2,1,0:T(8,128)(2,1)S(1)} %shard_map.92.rest_0_), channel_id=1, source_target_pairs={{0,6},{1,7},{2,4},{3,5},{4,2},{5,3},{6,0},{7,1},{8,10},{9,11},{10,... | collective-permute-start | bytes 110600 | tf_op jit(solution)/shard_map/ppermute | solution.py:397
  16.9 0.0 collective-permute-start.4
  17.0 2.5 %collective-permute-start.3 = (bf16[18,8,128]{2,1,0:T(8,128)(2,1)S(1)}, bf16[18,8,128]{2,1,0:T(8,128)(2,1)S(1)}, u32[]{:S(2)}, u32[]{:S(2)}) collective-permute-start(bf16[18,8,128]{2,1,0:T(8,128)(2,1)S(1)} %shard_map.92.rest_0_), channel_id=1, source_target_pairs={{0,4},{1,5},{2,6},{3,7},{4,0},{5,1},{6,2},{7,3},{8,12},{9,13},{10,... | collective-permute-start | bytes 110600 | tf_op jit(solution)/shard_map/ppermute | solution.py:397
  19.4 0.3 collective-permute-start.2
  19.7 0.0 collective-permute-done.6.rest_7_
  19.7 6.0 %collective-permute-start.1 = (bf16[18,8,128]{2,1,0:T(8,128)(2,1)S(1)}, bf16[18,8,128]{2,1,0:T(8,128)(2,1)S(1)}, u32[]{:S(2)}, u32[]{:S(2)}) collective-permute-start(bf16[18,8,128]{2,1,0:T(8,128)(2,1)S(1)} %shard_map.92.rest_0_), channel_id=1, source_target_pairs={{0,2},{1,3},{2,0},{3,1},{4,6},{5,7},{6,4},{7,5},{8,14},{9,15},{10,... | collective-permute-start | bytes 110600 | tf_op jit(solution)/shard_map/ppermute | solution.py:397
  25.7 0.2 collective-permute-start
  25.9 0.0 collective-permute-done.4.rest_5_
  25.9 0.0 collective-permute-done.3.rest_4_
  25.9 0.0 collective-permute-done.2.rest_3_
  25.9 3.6 %collective-permute-done.1.rest_2_ = bf16[18,8,128]{2,1,0:T(8,128)(2,1)S(1)} collective-permute-done((bf16[18,8,128]{2,1,0:T(8,128)(2,1)S(1)}, bf16[18,8,128]{2,1,0:T(8,128)(2,1)S(1)}, u32[]{:S(2)}, u32[]{:S(2)}) %collective-permute-start.1) | collective-permute-done | bytes 36896 | tf_op jit(solution)/shard_map/ppermute | solution.py:397
  29.5 2.6 %collective-permute-done.rest_1_ = bf16[18,8,128]{2,1,0:T(8,128)(2,1)S(1)} collective-permute-done((bf16[18,8,128]{2,1,0:T(8,128)(2,1)S(1)}, bf16[18,8,128]{2,1,0:T(8,128)(2,1)S(1)}, u32[]{:S(2)}, u32[]{:S(2)}) %collective-permute-start) | collective-permute-done | bytes 36896 | tf_op jit(solution)/shard_map/ppermute | solution.py:397
  32.1 0.0 all-to-all-done.window_rows
  32.2 1.1 %shard_map.93 = (bf16[8,512,128]{2,1,0:T(8,128)(2,1)S(1)}, bf16[8,16,8,128]{3,2,1,0:T(8,128)(2,1)S(1)}) custom-call(bf16[32,8,8,128]{3,2,1,0:T(8,128)(2,1)S(1)} %all-to-all-done.window_rows, bf16[18,8,128]{2,1,0:T(8,128)(2,1)S(1)} %shard_map.92.rest_0_, bf16[18,8,128]{2,1,0:T(8,128)(2,1)S(1)} %collective-permute-done.rest_1_, ...), custom_call_target="tpu_custom_call" | custom-call | flops 8589934592 | bytes 1048576 | tf_op jit(solution)/shard_map/pallas_call | solution.py:161
  33.3 0.0 copy-start.5
  33.3 0.0 copy-start.6
  33.3 17.7 %all_to_all.10.refs_4_ = bf16[8,512,128]{2,1,0:T(8,128)(2,1)S(1)} all-to-all(bf16[8,512,128]{2,1,0:T(8,128)(2,1)S(1)} %get-tuple-element.9), channel_id=1, replica_groups=mesh['chan'=32,'stack'=8] {'stack'}, dimensions={0} | all-to-all | bytes 2097152 | tf_op jit(solution)/shard_map/all_to_all | solution.py:399
  51.1 2.1 %shard_map.95.near = bf16[8,32,2048]{2,1,0:T(8,128)(2,1)S(1)} custom-call(bf16[256,256]{1,0:T(8,128)(2,1)S(1)} %copy-done.9, bf16[512,1024]{1,0:T(8,128)(2,1)S(1)} %copy-done.8, bf16[512,1024]{1,0:T(8,128)(2,1)S(1)} %copy-done.7, bf16[512,1024]{1,0:T(8,128)(2,1)S(1)} %copy-done.6, bf16[512,1024]{1,0:T(8,128)(2,1)S(1)} %copy-done.5, ...), custom_call_target="tpu_custom_call" | custom-call | flops 2147483648 | bytes 6291456 | tf_op jit(solution)/shard_map/pallas_call | solution.py:276
  53.1 4.0 %collective-permute-start.8 = (bf16[8,32,2048]{2,1,0:T(8,128)(2,1)S(1)}, bf16[8,32,2048]{2,1,0:T(8,128)(2,1)S(1)}, u32[]{:S(2)}, u32[]{:S(2)}) collective-permute-start(bf16[8,32,2048]{2,1,0:T(8,128)(2,1)S(1)} %shard_map.95.near), channel_id=1, source_target_pairs={{0,8},{8,0},{16,24},{24,16},{32,40},{40,32},{48,56},{56,48},{64,72... | collective-permute-start | bytes 3145736 | tf_op jit(solution)/shard_map/ppermute | solution.py:406
  57.2 3.2 %shard_map.94 = (bf16[8,32,2048]{2,1,0:T(8,128)(2,1)S(1)}, f32[16,24,8,128]{3,2,1,0:T(8,128)S(1)}) custom-call(bf16[256,256]{1,0:T(8,128)(2,1)S(1)} %copy-done.9, bf16[512,1024]{1,0:T(8,128)(2,1)S(1)} %copy-done.8, bf16[512,1024]{1,0:T(8,128)(2,1)S(1)} %copy-done.7, bf16[512,1024]{1,0:T(8,128)(2,1)S(1)} %copy-done.6, bf16[512,1024]{1,0:T(8,128)(2,1)S(1)} %copy-done.5, ...), custom_call_target="tpu_custom_call" | custom-call | flops 3221225472 | bytes 7340032 | tf_op jit(solution)/shard_map/pallas_call | solution.py:276
  60.4 0.3 collective-permute-start.7
  60.6 0.0 collective-permute-done.8.far
  60.6 0.0 copy-start.3
  60.7 0.0 copy-start.4
  60.7 3.9 %shard_map.96.before = bf16[256,2048]{1,0:T(8,128)(2,1)S(1)} custom-call(bf16[8,32,2048]{2,1,0:T(8,128)(2,1)S(1)} %shard_map.95.near, bf16[8,32,2048]{2,1,0:T(8,128)(2,1)S(1)} %collective-permute-done.8.far, f32[16,24,8,128]{3,2,1,0:T(8,128)S(1)} %get-tuple-element.12.own), custom_call_target="tpu_custom_call" | custom-call | flops 4294967296 | bytes 9437184 | tf_op jit(solution)/shard_map/pallas_call | solution.py:354
  64.6 0.0 collective-permute-done.7.far
  64.6 7.2 %shard_map.97 = f32[64,8,2048]{2,1,0:T(8,128)} custom-call(bf16[8,32,2048]{2,1,0:T(8,128)(2,1)S(1)} %get-tuple-element.11.near, bf16[8,32,2048]{2,1,0:T(8,128)(2,1)S(1)} %collective-permute-done.7.far, f32[16,24,8,128]{3,2,1,0:T(8,128)S(1)} %get-tuple-element.12.own, bf16[1024,1024]{1,0:T(8,128)(2,1)S(1)} %copy-done.4, bf16[1024,1024]{1,0:T(8,128)(2,1)S(1)} %copy-done.3, ...), custom_call_target="tpu_custom_call" | custom-call | flops 8589934592 | bytes 9437184 | tf_op jit(solution)/shard_map/pallas_call | solution.py:374
  (16 shorter events, 0.0 us)
Async XLA Ops:
  0.0 0.8 %copy-start = (bf16[16,8,128]{2,1,0:T(8,128)(2,1)S(1)}, bf16[16,8,128]{2,1,0:T(8,128)(2,1)}, u32[]{:S(2)}) copy-start(bf16[16,8,128]{2,1,0:T(8,128)(2,1)} %strain.3) | copy-start | bytes 98308
  0.8 12.1 %copy-start.1 = (bf16[16,8,128]{2,1,0:T(8,128)(2,1)S(1)}, bf16[16,8,128]{2,1,0:T(8,128)(2,1)}, u32[]{:S(2)}) copy-start(bf16[16,8,128]{2,1,0:T(8,128)(2,1)} %strain.3) | copy-start | bytes 98308
  0.8 12.1 %copy-start.2 = (s32[16,64]{1,0:T(8,128)S(1)}, s32[16,64]{1,0:T(8,128)}, u32[]{:S(2)}) copy-start(s32[16,64]{1,0:T(8,128)} %sources.1) | copy-start | bytes 12292
  1.8 30.3 %all-to-all-start = ((bf16[32,8,8,128]{3,2,1,0:T(8,128)(2,1)}), bf16[32,8,8,128]{3,2,1,0:T(8,128)(2,1)S(1)}, u32[]{:S(2)}, u32[]{:S(2)}) async-start(bf16[32,8,8,128]{3,2,1,0:T(8,128)(2,1)} %shard_map.91), calls=%async_computation | async-start | bytes 1048576 | tf_op jit(solution)/shard_map/all_to_all | solution.py:391
  13.0 6.7 %collective-permute-start.6 = (bf16[18,8,128]{2,1,0:T(8,128)(2,1)S(1)}, bf16[18,8,128]{2,1,0:T(8,128)(2,1)S(1)}, u32[]{:S(2)}, u32[]{:S(2)}) collective-permute-start(bf16[18,8,128]{2,1,0:T(8,128)(2,1)S(1)} %shard_map.92.rest_0_), channel_id=1, source_target_pairs={{0,7},{1,6},{2,5},{3,4},{4,3},{5,2},{6,1},{7,0},{8,9},{9,8},{10,11... | collective-permute-start | bytes 110600 | tf_op jit(solution)/shard_map/ppermute | solution.py:397
  14.3 11.3 %collective-permute-start.5 = (bf16[18,8,128]{2,1,0:T(8,128)(2,1)S(1)}, bf16[18,8,128]{2,1,0:T(8,128)(2,1)S(1)}, u32[]{:S(2)}, u32[]{:S(2)}) collective-permute-start(bf16[18,8,128]{2,1,0:T(8,128)(2,1)S(1)} %shard_map.92.rest_0_), channel_id=1, source_target_pairs={{0,6},{1,7},{2,4},{3,5},{4,2},{5,3},{6,0},{7,1},{8,10},{9,11},{10,... | collective-permute-start | bytes 110600 | tf_op jit(solution)/shard_map/ppermute | solution.py:397
  16.9 9.0 %collective-permute-start.4 = (bf16[18,8,128]{2,1,0:T(8,128)(2,1)S(1)}, bf16[18,8,128]{2,1,0:T(8,128)(2,1)S(1)}, u32[]{:S(2)}, u32[]{:S(2)}) collective-permute-start(bf16[18,8,128]{2,1,0:T(8,128)(2,1)S(1)} %shard_map.92.rest_0_), channel_id=1, source_target_pairs={{0,5},{1,4},{2,7},{3,6},{4,1},{5,0},{6,3},{7,2},{8,11},{9,10},{10,... | collective-permute-start | bytes 110600 | tf_op jit(solution)/shard_map/ppermute | solution.py:397
  17.0 9.0 %collective-permute-start.3 = (bf16[18,8,128]{2,1,0:T(8,128)(2,1)S(1)}, bf16[18,8,128]{2,1,0:T(8,128)(2,1)S(1)}, u32[]{:S(2)}, u32[]{:S(2)}) collective-permute-start(bf16[18,8,128]{2,1,0:T(8,128)(2,1)S(1)} %shard_map.92.rest_0_), channel_id=1, source_target_pairs={{0,4},{1,5},{2,6},{3,7},{4,0},{5,1},{6,2},{7,3},{8,12},{9,13},{10,... | collective-permute-start | bytes 110600 | tf_op jit(solution)/shard_map/ppermute | solution.py:397
  19.4 6.5 %collective-permute-start.2 = (bf16[18,8,128]{2,1,0:T(8,128)(2,1)S(1)}, bf16[18,8,128]{2,1,0:T(8,128)(2,1)S(1)}, u32[]{:S(2)}, u32[]{:S(2)}) collective-permute-start(bf16[18,8,128]{2,1,0:T(8,128)(2,1)S(1)} %shard_map.92.rest_0_), channel_id=1, source_target_pairs={{0,3},{1,2},{2,1},{3,0},{4,7},{5,6},{6,5},{7,4},{8,13},{9,12},{10,... | collective-permute-start | bytes 110600 | tf_op jit(solution)/shard_map/ppermute | solution.py:397
  19.7 9.9 %collective-permute-start.1 = (bf16[18,8,128]{2,1,0:T(8,128)(2,1)S(1)}, bf16[18,8,128]{2,1,0:T(8,128)(2,1)S(1)}, u32[]{:S(2)}, u32[]{:S(2)}) collective-permute-start(bf16[18,8,128]{2,1,0:T(8,128)(2,1)S(1)} %shard_map.92.rest_0_), channel_id=1, source_target_pairs={{0,2},{1,3},{2,0},{3,1},{4,6},{5,7},{6,4},{7,5},{8,14},{9,15},{10,... | collective-permute-start | bytes 110600 | tf_op jit(solution)/shard_map/ppermute | solution.py:397
  25.7 6.5 %collective-permute-start = (bf16[18,8,128]{2,1,0:T(8,128)(2,1)S(1)}, bf16[18,8,128]{2,1,0:T(8,128)(2,1)S(1)}, u32[]{:S(2)}, u32[]{:S(2)}) collective-permute-start(bf16[18,8,128]{2,1,0:T(8,128)(2,1)S(1)} %shard_map.92.rest_0_), channel_id=1, source_target_pairs={{0,1},{1,0},{2,3},{3,2},{4,5},{5,4},{6,7},{7,6},{8,15},{9,14},{10,... | collective-permute-start | bytes 110600 | tf_op jit(solution)/shard_map/ppermute | solution.py:397
  32.1 18.9 %copy-start.7 = (bf16[512,1024]{1,0:T(8,128)(2,1)S(1)}, bf16[512,1024]{1,0:T(8,128)(2,1)}, u32[]{:S(2)}) copy-start(bf16[512,1024]{1,0:T(8,128)(2,1)} %constant.16.clone.refs_1_) | copy-start | bytes 3145732
  32.1 18.9 %copy-start.8 = (bf16[512,1024]{1,0:T(8,128)(2,1)S(1)}, bf16[512,1024]{1,0:T(8,128)(2,1)}, u32[]{:S(2)}) copy-start(bf16[512,1024]{1,0:T(8,128)(2,1)} %constant.15.clone.refs_0_) | copy-start | bytes 3145732
  32.1 18.9 %copy-start.9 = (bf16[256,256]{1,0:T(8,128)(2,1)S(1)}, bf16[256,256]{1,0:T(8,128)(2,1)}, u32[]{:S(2)}) copy-start(bf16[256,256]{1,0:T(8,128)(2,1)} %constant.14.clone.perm) | copy-start | bytes 393220
  33.3 17.8 %copy-start.5 = (bf16[512,1024]{1,0:T(8,128)(2,1)S(1)}, bf16[512,1024]{1,0:T(8,128)(2,1)}, u32[]{:S(2)}) copy-start(bf16[512,1024]{1,0:T(8,128)(2,1)} %constant.18.clone.refs_3_) | copy-start | bytes 3145732
  33.3 17.8 %copy-start.6 = (bf16[512,1024]{1,0:T(8,128)(2,1)S(1)}, bf16[512,1024]{1,0:T(8,128)(2,1)}, u32[]{:S(2)}) copy-start(bf16[512,1024]{1,0:T(8,128)(2,1)} %constant.17.clone.refs_2_) | copy-start | bytes 3145732
  53.1 7.5 %collective-permute-start.8 = (bf16[8,32,2048]{2,1,0:T(8,128)(2,1)S(1)}, bf16[8,32,2048]{2,1,0:T(8,128)(2,1)S(1)}, u32[]{:S(2)}, u32[]{:S(2)}) collective-permute-start(bf16[8,32,2048]{2,1,0:T(8,128)(2,1)S(1)} %shard_map.95.near), channel_id=1, source_target_pairs={{0,8},{8,0},{16,24},{24,16},{32,40},{40,32},{48,56},{56,48},{64,72... | collective-permute-start | bytes 3145736 | tf_op jit(solution)/shard_map/ppermute | solution.py:406
  60.4 4.2 %collective-permute-start.7 = (bf16[8,32,2048]{2,1,0:T(8,128)(2,1)S(1)}, bf16[8,32,2048]{2,1,0:T(8,128)(2,1)S(1)}, u32[]{:S(2)}, u32[]{:S(2)}) collective-permute-start(bf16[8,32,2048]{2,1,0:T(8,128)(2,1)S(1)} %get-tuple-element.11.near), channel_id=1, source_target_pairs={{0,8},{8,0},{16,24},{24,16},{32,40},{40,32},{48,56},{56,48},{64,72... | collective-permute-start | bytes 3145736 | tf_op jit(solution)/shard_map/ppermute | solution.py:409
  60.6 4.0 %copy-start.3 = (bf16[1024,1024]{1,0:T(8,128)(2,1)S(1)}, bf16[1024,1024]{1,0:T(8,128)(2,1)}, u32[]{:S(2)}) copy-start(bf16[1024,1024]{1,0:T(8,128)(2,1)} %constant.20.clone.lag_odd) | copy-start | bytes 6291460
  60.7 4.0 %copy-start.4 = (bf16[1024,1024]{1,0:T(8,128)(2,1)S(1)}, bf16[1024,1024]{1,0:T(8,128)(2,1)}, u32[]{:S(2)}) copy-start(bf16[1024,1024]{1,0:T(8,128)(2,1)} %constant.19.clone.lag_even) | copy-start | bytes 6291460

commit v5 on v4

--- a/solution.py
+++ b/solution.py
@@ -91,27 +91,30 @@
     return pl.CostEstimate(flops=flops, bytes_accessed=moved, transcendentals=special)
 
 
-def spread_kernel(strain, sends, sems):
+def spread_kernel(strain, theirs, sends, sems):
+    core, _ = place()
+    windows = pl.ds(8 * core, 8)
     copies = []
-    for other in range(32):
-        windows = strain.at[8 * (other % 2) : 8 * (other % 2) + 8]
-        copies.append(pltpu.make_async_copy(windows, sends.at[other], sems.at[other]))
+    for other in range(16):
+        for k, (side, rows) in enumerate(((core, strain), (1 - core, theirs))):
+            sem = sems.at[2 * other + k]
+            copies.append(pltpu.make_async_copy(rows.at[windows], sends.at[other, side], sem))
     for copy in copies:
         copy.start()
     for copy in copies:
         copy.wait()
 
 
-def spread(strain):
+def spread(strain, theirs):
     return pl.pallas_call(
         spread_kernel,
-        out_shape=jax.ShapeDtypeStruct((32, 8, 8, 128), BF),
-        in_specs=[ANYWHERE],
+        out_shape=jax.ShapeDtypeStruct((16, 2, 8, 8, 128), BF),
+        in_specs=[ANYWHERE, ANYWHERE],
         out_specs=ANYWHERE,
         scratch_shapes=[pltpu.SemaphoreType.DMA((32,))],
         compiler_params=PARAMS,
         cost_estimate=cost(2**32),
-    )(strain)
+    )(strain, theirs)
 
 
 def share_kernel(strain, sources, shared):
@@ -134,13 +137,31 @@
     )(strain, sources)
 
 
+def join_kernel(first, second, out):
+    out[:18] = first[...]
+    out[18:] = second[...]
+
+
+def join(first, second):
+    return pl.pallas_call(
+        join_kernel,
+        out_shape=jax.ShapeDtypeStruct((36, 8, 128), BF),
+        in_specs=[VMEM, VMEM],
+        out_specs=VMEM,
+        compiler_params=PARAMS,
+        cost_estimate=cost(2**28),
+    )(first, second)
+
+
 def pick_kernel(window_rows, *rest):
-    shared, (out, blocks, picks) = rest[:8], rest[-3:]
+    shared, (out, blocks, picks) = rest[:4], rest[-3:]
     core, group = place()
-    for k in range(8):
-        sender = group ^ (k + core * (8 - 2 * k) if k else 0)
-        picks[sender] = shared[k][16:].astype(F32).reshape(16, 128)
-        blocks[sender] = shared[k][:16]
+    for k in range(4):
+        nearest = group ^ (k + core * (4 - 2 * k) if k else 0)
+        for side in range(2):
+            sender, held = nearest ^ (4 * side), shared[k][18 * side : 18 * side + 18]
+            picks[sender] = held[16:].astype(F32).reshape(16, 128)
+            blocks[sender] = held[:16]
     chosen = iota((16, 8), 0) == 8 * core + iota((16, 8), 1)
     chosen = chosen.astype(F32).astype(BF)
     columns = []
@@ -151,7 +172,7 @@
     channel = iota((512, 256), 1).astype(F32)
     for w in range(8):
         hits = (column[:, w : w + 1] == channel).astype(F32).astype(BF)
-        rows = window_rows[:, w].astype(F32).reshape(256, 128).astype(BF)
+        rows = window_rows[:, :, w].astype(F32).reshape(256, 128).astype(BF)
         found = dot(hits, rows).astype(BF)
         for other in range(8):
             out[other, 64 * w : 64 * w + 64] = found[64 * other : 64 * other + 64]
@@ -164,7 +185,7 @@
             jax.ShapeDtypeStruct((8, 512, 128), BF),
             jax.ShapeDtypeStruct((8, 16, 8, 128), BF),
         ),
-        in_specs=[VMEM] * 9,
+        in_specs=[VMEM] * 5,
         out_specs=(VMEM, VMEM),
         scratch_shapes=[pltpu.VMEM((8, 16, 128), F32)],
         compiler_params=PARAMS,
@@ -388,11 +409,16 @@
 
 
 def local(strain, sources):
-    window_rows = lax.all_to_all(spread(strain), "chan", 0, 0, tiled=True)
+    swap = functools.partial(lax.ppermute, axis_name="chan", perm=[(i, i ^ 1) for i in range(32)])
+    groups = [list(range(core, 32, 2)) for core in range(MESH_CORES)]
+    window_rows = lax.all_to_all(
+        spread(strain, swap(strain)), "chan", 0, 0, tiled=True, axis_index_groups=groups
+    )
     shared = share(strain, sources)
+    shared = join(shared, lax.ppermute(shared, "stack", [(j, j ^ 4) for j in range(8)]))
     everyone = [shared]
-    for k in range(1, 8):
-        turns = (k, 8 - k)
+    for k in range(1, 4):
+        turns = (k, 4 - k)
         pairs = [(8 * i + j, 8 * i + (j ^ turns[i % 2])) for i in range(32) for j in range(8)]
         everyone.append(lax.ppermute(shared, ("chan", "stack"), pairs))
     picked, blocks = pick(window_rows, everyone)
@@ -401,7 +427,6 @@
     lag = [jnp.asarray(t) for t in lag_tables()]
     panel = jax.ShapeDtypeStruct((8, 32, 2048), BF)
     mine = jax.ShapeDtypeStruct((16, 24, 8, 128), F32)
-    swap = functools.partial(lax.ppermute, axis_name="chan", perm=[(i, i ^ 1) for i in range(32)])
     (near_0,) = white_call(first_white_kernel, 256, [panel], [*tables, rows])
     far_0 = swap(near_0)
     held = [pltpu.VMEM((16, 128, 128), F32)]

time: 72.2 us -> 70 us (0.970)
  starting transfers between devices: 28.3 us -> 22.4 us
  waiting for transfers between devices: 6.24 us -> 8.18 us
  blocking collectives: 17.7 us -> 19.5 us
    ppermute x7 -> x3, starting transfers between devices: 12.9 us -> 3.92 us  [local(): everyone.append(lax.ppermute(shared, ('chan', 'stack'), pairs))]
    ppermute x0 -> x2, starting transfers between devices: none -> 5.73 us  [the longest x1 3.24 us: local(): swap(strain)]
    all_to_all x1, starting transfers between devices: 11.1 us -> 7.49 us  [local(): lax.all_to_all(spread(strain, swap(strain)), 'chan', 0, 0, tiled=True, ax...]
    ppermute x0 -> x2, waiting for transfers between devices: none -> 3.06 us  [the longest x1 1.99 us: local(): lax.ppermute(shared, 'stack', [(j, j ^ 4) for j in range(8)])]
    all_to_all x1, blocking collectives: 17.7 us -> 19.5 us  [local(): rows = lax.all_to_all(picked, 'stack', 0, 0, tiled=True)]
    ppermute x7 -> x3, waiting for transfers between devices: 6.23 us -> 4.7 us  [local(): everyone.append(lax.ppermute(shared, ('chan', 'stack'), pairs))]
    ppermute x1, starting transfers between devices: 4.04 us -> 5.01 us  [local(): far_0 = swap(near_0)]
  transfers between devices with their start and end apart: 10 -> 8, of which waited for: 2 -> 5; matrix products, arithmetic and copies ran while one was open for 0% -> 0% of each run, Pallas kernels for 10% -> 10%
where the time goes in v5:
time: 70 us; the launch traced here: 69.7 us
  starting transfers between devices  22.4 us (32%)
  blocking collectives  19.5 us (28%)
  Pallas kernels  18.5 us (26%)
  waiting for transfers between devices  8.18 us (12%)
  local copies, waits for them, and re-layouts  0.8 us (1%)
    all_to_all x1, blocking collectives, local(): rows = lax.all_to_all(picked, 'stack', 0, 0, tiled=True)  19.5 us
    all_to_all x1, starting transfers between devices, local(): lax.all_to_all(spread(strain, swap(strain)), 'chan', 0, 0, tiled=True, ax...  7.49 us
    pallas_call x1, Pallas kernels, correlate(): pl.pallas_call(last_kernel, out_shape=jax.ShapeDtypeStruct((64, 8, 2048),...  7.16 us
    pallas_call x2, Pallas kernels, white_call(): pl.pallas_call(kernel, out_shape=shapes, in_specs=[VMEM] * len(operands),...  5.23 us
    ppermute x1, starting transfers between devices, local(): far_0 = swap(near_0)  5.01 us
    ppermute x3, waiting for transfers between devices, local(): everyone.append(lax.ppermute(shared, ('chan', 'stack'), pairs))  4.7 us
    pallas_call x1, Pallas kernels, first_cross(): pl.pallas_call(first_cross_kernel, out_shape=jax.ShapeDtypeStruct((256, 2...  3.92 us
    ppermute x3, starting transfers between devices, local(): everyone.append(lax.ppermute(shared, ('chan', 'stack'), pairs))  3.92 us
  transfers between devices with their start and end apart: 8, of which 5 were waited for; matrix products, arithmetic and copies ran while one was open for 0% of the time, Pallas kernels for 10%

profile of v5, /device:TPU:1, one launch (start us, length us, event | category | flops | bytes accessed | tf_op | source)
XLA Modules:
  0.0 69.7 jit_solution(5679219098142706420)
XLA Ops:
  0.0 3.2 %collective-permute-start = (bf16[16,8,128]{2,1,0:T(8,128)(2,1)}, bf16[16,8,128]{2,1,0:T(8,128)(2,1)S(1)}, u32[]{:S(2)}, u32[]{:S(2)}) collective-permute-start(bf16[16,8,128]{2,1,0:T(8,128)(2,1)} %strain.3), channel_id=1, source_target_pairs={{0,8},{8,0},{16,24},{24,16},{32,40},{40,32},{48,56},{56,48},{64,72... | collective-permute-start | bytes 98312 | tf_op jit(solution)/shard_map/ppermute | solution.py:415
  3.2 1.1 %collective-permute-done.theirs = bf16[16,8,128]{2,1,0:T(8,128)(2,1)S(1)} collective-permute-done((bf16[16,8,128]{2,1,0:T(8,128)(2,1)}, bf16[16,8,128]{2,1,0:T(8,128)(2,1)S(1)}, u32[]{:S(2)}, u32[]{:S(2)}) %collective-permute-start) | collective-permute-done | bytes 32800 | tf_op jit(solution)/shard_map/ppermute | solution.py:415
  4.3 0.8 %copy-done = bf16[16,8,128]{2,1,0:T(8,128)(2,1)S(1)} copy-done((bf16[16,8,128]{2,1,0:T(8,128)(2,1)S(1)}, bf16[16,8,128]{2,1,0:T(8,128)(2,1)}, u32[]{:S(2)}) %copy-start) | copy-done | bytes 32792
  5.1 1.1 %shard_map.91 = bf16[16,2,8,8,128]{4,3,2,1,0:T(8,128)(2,1)} custom-call(bf16[16,8,128]{2,1,0:T(8,128)(2,1)S(1)} %copy-done, bf16[16,8,128]{2,1,0:T(8,128)(2,1)S(1)} %collective-permute-done.theirs), custom_call_target="tpu_custom_call" | custom-call | flops 4294967296 | bytes 1048576 | tf_op jit(solution)/shard_map/pallas_call | solution.py:109
  6.1 7.5 %all-to-all-start = ((bf16[16,2,8,8,128]{4,3,2,1,0:T(8,128)(2,1)}), bf16[16,2,8,8,128]{4,3,2,1,0:T(8,128)(2,1)S(1)}, u32[]{:S(2)}, u32[]{:S(2)}) async-start(bf16[16,2,8,8,128]{4,3,2,1,0:T(8,128)(2,1)} %shard_map.91), calls=%async_computation | async-start | bytes 1048576 | tf_op jit(solution)/shard_map/all_to_all | solution.py:414
  13.7 0.1 shard_map.92.first
  13.7 2.5 %collective-permute-start.1 = (bf16[18,8,128]{2,1,0:T(8,128)(2,1)S(1)}, bf16[18,8,128]{2,1,0:T(8,128)(2,1)S(1)}, u32[]{:S(2)}, u32[]{:S(2)}) collective-permute-start(bf16[18,8,128]{2,1,0:T(8,128)(2,1)S(1)} %shard_map.92.first), channel_id=1, source_target_pairs={{0,4},{1,5},{2,6},{3,7},{4,0},{5,1},{6,2},{7,3},{8,12},{9,13},{10,... | collective-permute-start | bytes 110600 | tf_op jit(solution)/shard_map/ppermute | solution.py:418
  16.2 2.0 %collective-permute-done.1.second = bf16[18,8,128]{2,1,0:T(8,128)(2,1)S(1)} collective-permute-done((bf16[18,8,128]{2,1,0:T(8,128)(2,1)S(1)}, bf16[18,8,128]{2,1,0:T(8,128)(2,1)S(1)}, u32[]{:S(2)}, u32[]{:S(2)}) %collective-permute-start.1) | collective-permute-done | bytes 36896 | tf_op jit(solution)/shard_map/ppermute | solution.py:418
  18.2 1.3 %collective-permute-start.4 = (bf16[36,8,128]{2,1,0:T(8,128)(2,1)S(1)}, bf16[36,8,128]{2,1,0:T(8,128)(2,1)S(1)}, u32[]{:S(2)}, u32[]{:S(2)}) collective-permute-start(bf16[36,8,128]{2,1,0:T(8,128)(2,1)S(1)} %shard_map.93.rest_0_), channel_id=1, source_target_pairs={{0,3},{1,2},{2,1},{3,0},{4,7},{5,6},{6,5},{7,4},{8,9},{9,8},{10,11... | collective-permute-start | bytes 221192 | tf_op jit(solution)/shard_map/ppermute | solution.py:423
  19.5 2.6 %collective-permute-start.3 = (bf16[36,8,128]{2,1,0:T(8,128)(2,1)S(1)}, bf16[36,8,128]{2,1,0:T(8,128)(2,1)S(1)}, u32[]{:S(2)}, u32[]{:S(2)}) collective-permute-start(bf16[36,8,128]{2,1,0:T(8,128)(2,1)S(1)} %shard_map.93.rest_0_), channel_id=1, source_target_pairs={{0,2},{1,3},{2,0},{3,1},{4,6},{5,7},{6,4},{7,5},{8,10},{9,11},{10,... | collective-permute-start | bytes 221192 | tf_op jit(solution)/shard_map/ppermute | solution.py:423
  22.1 0.0 collective-permute-start.2
  22.1 0.0 collective-permute-done.4.rest_3_
  22.1 2.8 %collective-permute-done.3.rest_2_ = bf16[36,8,128]{2,1,0:T(8,128)(2,1)S(1)} collective-permute-done((bf16[36,8,128]{2,1,0:T(8,128)(2,1)S(1)}, bf16[36,8,128]{2,1,0:T(8,128)(2,1)S(1)}, u32[]{:S(2)}, u32[]{:S(2)}) %collective-permute-start.3) | collective-permute-done | bytes 73760 | tf_op jit(solution)/shard_map/ppermute | solution.py:423
  25.0 1.9 %collective-permute-done.2.rest_1_ = bf16[36,8,128]{2,1,0:T(8,128)(2,1)S(1)} collective-permute-done((bf16[36,8,128]{2,1,0:T(8,128)(2,1)S(1)}, bf16[36,8,128]{2,1,0:T(8,128)(2,1)S(1)}, u32[]{:S(2)}, u32[]{:S(2)}) %collective-permute-start.2) | collective-permute-done | bytes 73760 | tf_op jit(solution)/shard_map/ppermute | solution.py:423
  26.8 0.4 all-to-all-done.window_rows
  27.3 1.1 %shard_map.94 = (bf16[8,512,128]{2,1,0:T(8,128)(2,1)S(1)}, bf16[8,16,8,128]{3,2,1,0:T(8,128)(2,1)S(1)}) custom-call(bf16[16,2,8,8,128]{4,3,2,1,0:T(8,128)(2,1)S(1)} %all-to-all-done.window_rows, bf16[36,8,128]{2,1,0:T(8,128)(2,1)S(1)} %shard_map.93.rest_0_, bf16[36,8,128]{2,1,0:T(8,128)(2,1)S(1)} %collective-permute-done.2.rest_1_, ...), custom_call_target="tpu_custom_call" | custom-call | flops 8589934592 | bytes 1048576 | tf_op jit(solution)/shard_map/pallas_call | solution.py:182
  28.4 0.0 copy-start.5
  28.4 0.0 copy-start.6
  28.4 19.5 %all_to_all.10.refs_4_ = bf16[8,512,128]{2,1,0:T(8,128)(2,1)S(1)} all-to-all(bf16[8,512,128]{2,1,0:T(8,128)(2,1)S(1)} %get-tuple-element.9), channel_id=1, replica_groups=mesh['chan'=32,'stack'=8] {'stack'}, dimensions={0} | all-to-all | bytes 2097152 | tf_op jit(solution)/shard_map/all_to_all | solution.py:425
  47.9 0.0 copy-done.5
  47.9 0.0 copy-done.6
  47.9 2.1 %shard_map.96.near = bf16[8,32,2048]{2,1,0:T(8,128)(2,1)S(1)} custom-call(bf16[256,256]{1,0:T(8,128)(2,1)S(1)} %copy-done.9, bf16[512,1024]{1,0:T(8,128)(2,1)S(1)} %copy-done.8, bf16[512,1024]{1,0:T(8,128)(2,1)S(1)} %copy-done.7, bf16[512,1024]{1,0:T(8,128)(2,1)S(1)} %copy-done.6, bf16[512,1024]{1,0:T(8,128)(2,1)S(1)} %copy-done.5, ...), custom_call_target="tpu_custom_call" | custom-call | flops 2147483648 | bytes 6291456 | tf_op jit(solution)/shard_map/pallas_call | solution.py:297
  49.9 5.0 %collective-permute-start.6 = (bf16[8,32,2048]{2,1,0:T(8,128)(2,1)S(1)}, bf16[8,32,2048]{2,1,0:T(8,128)(2,1)S(1)}, u32[]{:S(2)}, u32[]{:S(2)}) collective-permute-start(bf16[8,32,2048]{2,1,0:T(8,128)(2,1)S(1)} %shard_map.96.near), channel_id=1, source_target_pairs={{0,8},{8,0},{16,24},{24,16},{32,40},{40,32},{48,56},{56,48},{64,72... | collective-permute-start | bytes 3145736 | tf_op jit(solution)/shard_map/ppermute | solution.py:431
  55.0 3.2 %shard_map.95 = (bf16[8,32,2048]{2,1,0:T(8,128)(2,1)S(1)}, f32[16,24,8,128]{3,2,1,0:T(8,128)S(1)}) custom-call(bf16[256,256]{1,0:T(8,128)(2,1)S(1)} %copy-done.9, bf16[512,1024]{1,0:T(8,128)(2,1)S(1)} %copy-done.8, bf16[512,1024]{1,0:T(8,128)(2,1)S(1)} %copy-done.7, bf16[512,1024]{1,0:T(8,128)(2,1)S(1)} %copy-done.6, bf16[512,1024]{1,0:T(8,128)(2,1)S(1)} %copy-done.5, ...), custom_call_target="tpu_custom_call" | custom-call | flops 3221225472 | bytes 7340032 | tf_op jit(solution)/shard_map/pallas_call | solution.py:297
  58.1 0.3 collective-permute-start.5
  58.4 0.0 collective-permute-done.6.far
  58.4 0.0 copy-start.3
  58.4 0.0 copy-start.4
  58.5 3.9 %shard_map.97.before = bf16[256,2048]{1,0:T(8,128)(2,1)S(1)} custom-call(bf16[8,32,2048]{2,1,0:T(8,128)(2,1)S(1)} %shard_map.96.near, bf16[8,32,2048]{2,1,0:T(8,128)(2,1)S(1)} %collective-permute-done.6.far, f32[16,24,8,128]{3,2,1,0:T(8,128)S(1)} %get-tuple-element.12.own), custom_call_target="tpu_custom_call" | custom-call | flops 4294967296 | bytes 9437184 | tf_op jit(solution)/shard_map/pallas_call | solution.py:375
  62.4 0.0 collective-permute-done.5.far
  62.4 0.0 copy-done.3
  62.4 7.2 %shard_map.98 = f32[64,8,2048]{2,1,0:T(8,128)} custom-call(bf16[8,32,2048]{2,1,0:T(8,128)(2,1)S(1)} %get-tuple-element.11.near, bf16[8,32,2048]{2,1,0:T(8,128)(2,1)S(1)} %collective-permute-done.5.far, f32[16,24,8,128]{3,2,1,0:T(8,128)S(1)} %get-tuple-element.12.own, bf16[1024,1024]{1,0:T(8,128)(2,1)S(1)} %copy-done.4, bf16[1024,1024]{1,0:T(8,128)(2,1)S(1)} %copy-done.3, ...), custom_call_target="tpu_custom_call" | custom-call | flops 8589934592 | bytes 9437184 | tf_op jit(solution)/shard_map/pallas_call | solution.py:395
  (13 shorter events, 0.0 us)
Async XLA Ops:
  0.0 4.3 %collective-permute-start = (bf16[16,8,128]{2,1,0:T(8,128)(2,1)}, bf16[16,8,128]{2,1,0:T(8,128)(2,1)S(1)}, u32[]{:S(2)}, u32[]{:S(2)}) collective-permute-start(bf16[16,8,128]{2,1,0:T(8,128)(2,1)} %strain.3), channel_id=1, source_target_pairs={{0,8},{8,0},{16,24},{24,16},{32,40},{40,32},{48,56},{56,48},{64,72... | collective-permute-start | bytes 98312 | tf_op jit(solution)/shard_map/ppermute | solution.py:415
  4.3 0.8 %copy-start = (bf16[16,8,128]{2,1,0:T(8,128)(2,1)S(1)}, bf16[16,8,128]{2,1,0:T(8,128)(2,1)}, u32[]{:S(2)}) copy-start(bf16[16,8,128]{2,1,0:T(8,128)(2,1)} %strain.3) | copy-start | bytes 98308
  5.1 8.6 %copy-start.1 = (bf16[16,8,128]{2,1,0:T(8,128)(2,1)S(1)}, bf16[16,8,128]{2,1,0:T(8,128)(2,1)}, u32[]{:S(2)}) copy-start(bf16[16,8,128]{2,1,0:T(8,128)(2,1)} %strain.3) | copy-start | bytes 98308
  5.1 8.6 %copy-start.2 = (s32[16,64]{1,0:T(8,128)S(1)}, s32[16,64]{1,0:T(8,128)}, u32[]{:S(2)}) copy-start(s32[16,64]{1,0:T(8,128)} %sources.1) | copy-start | bytes 12292
  6.1 21.1 %all-to-all-start = ((bf16[16,2,8,8,128]{4,3,2,1,0:T(8,128)(2,1)}), bf16[16,2,8,8,128]{4,3,2,1,0:T(8,128)(2,1)S(1)}, u32[]{:S(2)}, u32[]{:S(2)}) async-start(bf16[16,2,8,8,128]{4,3,2,1,0:T(8,128)(2,1)} %shard_map.91), calls=%async_computation | async-start | bytes 1048576 | tf_op jit(solution)/shard_map/all_to_all | solution.py:414
  13.7 4.5 %collective-permute-start.1 = (bf16[18,8,128]{2,1,0:T(8,128)(2,1)S(1)}, bf16[18,8,128]{2,1,0:T(8,128)(2,1)S(1)}, u32[]{:S(2)}, u32[]{:S(2)}) collective-permute-start(bf16[18,8,128]{2,1,0:T(8,128)(2,1)S(1)} %shard_map.92.first), channel_id=1, source_target_pairs={{0,4},{1,5},{2,6},{3,7},{4,0},{5,1},{6,2},{7,3},{8,12},{9,13},{10,... | collective-permute-start | bytes 110600 | tf_op jit(solution)/shard_map/ppermute | solution.py:418
  18.2 3.9 %collective-permute-start.4 = (bf16[36,8,128]{2,1,0:T(8,128)(2,1)S(1)}, bf16[36,8,128]{2,1,0:T(8,128)(2,1)S(1)}, u32[]{:S(2)}, u32[]{:S(2)}) collective-permute-start(bf16[36,8,128]{2,1,0:T(8,128)(2,1)S(1)} %shard_map.93.rest_0_), channel_id=1, source_target_pairs={{0,3},{1,2},{2,1},{3,0},{4,7},{5,6},{6,5},{7,4},{8,9},{9,8},{10,11... | collective-permute-start | bytes 221192 | tf_op jit(solution)/shard_map/ppermute | solution.py:423
  19.5 5.4 %collective-permute-start.3 = (bf16[36,8,128]{2,1,0:T(8,128)(2,1)S(1)}, bf16[36,8,128]{2,1,0:T(8,128)(2,1)S(1)}, u32[]{:S(2)}, u32[]{:S(2)}) collective-permute-start(bf16[36,8,128]{2,1,0:T(8,128)(2,1)S(1)} %shard_map.93.rest_0_), channel_id=1, source_target_pairs={{0,2},{1,3},{2,0},{3,1},{4,6},{5,7},{6,4},{7,5},{8,10},{9,11},{10,... | collective-permute-start | bytes 221192 | tf_op jit(solution)/shard_map/ppermute | solution.py:423
  22.1 4.7 %collective-permute-start.2 = (bf16[36,8,128]{2,1,0:T(8,128)(2,1)S(1)}, bf16[36,8,128]{2,1,0:T(8,128)(2,1)S(1)}, u32[]{:S(2)}, u32[]{:S(2)}) collective-permute-start(bf16[36,8,128]{2,1,0:T(8,128)(2,1)S(1)} %shard_map.93.rest_0_), channel_id=1, source_target_pairs={{0,1},{1,0},{2,3},{3,2},{4,5},{5,4},{6,7},{7,6},{8,11},{9,10},{10,... | collective-permute-start | bytes 221192 | tf_op jit(solution)/shard_map/ppermute | solution.py:423
  27.3 20.6 %copy-start.7 = (bf16[512,1024]{1,0:T(8,128)(2,1)S(1)}, bf16[512,1024]{1,0:T(8,128)(2,1)}, u32[]{:S(2)}) copy-start(bf16[512,1024]{1,0:T(8,128)(2,1)} %constant.16.clone.refs_1_) | copy-start | bytes 3145732
  27.3 20.6 %copy-start.8 = (bf16[512,1024]{1,0:T(8,128)(2,1)S(1)}, bf16[512,1024]{1,0:T(8,128)(2,1)}, u32[]{:S(2)}) copy-start(bf16[512,1024]{1,0:T(8,128)(2,1)} %constant.15.clone.refs_0_) | copy-start | bytes 3145732
  27.3 20.6 %copy-start.9 = (bf16[256,256]{1,0:T(8,128)(2,1)S(1)}, bf16[256,256]{1,0:T(8,128)(2,1)}, u32[]{:S(2)}) copy-start(bf16[256,256]{1,0:T(8,128)(2,1)} %constant.14.clone.perm) | copy-start | bytes 393220
  28.4 19.5 %copy-start.5 = (bf16[512,1024]{1,0:T(8,128)(2,1)S(1)}, bf16[512,1024]{1,0:T(8,128)(2,1)}, u32[]{:S(2)}) copy-start(bf16[512,1024]{1,0:T(8,128)(2,1)} %constant.18.clone.refs_3_) | copy-start | bytes 3145732
  28.4 19.5 %copy-start.6 = (bf16[512,1024]{1,0:T(8,128)(2,1)S(1)}, bf16[512,1024]{1,0:T(8,128)(2,1)}, u32[]{:S(2)}) copy-start(bf16[512,1024]{1,0:T(8,128)(2,1)} %constant.17.clone.refs_2_) | copy-start | bytes 3145732
  49.9 8.5 %collective-permute-start.6 = (bf16[8,32,2048]{2,1,0:T(8,128)(2,1)S(1)}, bf16[8,32,2048]{2,1,0:T(8,128)(2,1)S(1)}, u32[]{:S(2)}, u32[]{:S(2)}) collective-permute-start(bf16[8,32,2048]{2,1,0:T(8,128)(2,1)S(1)} %shard_map.96.near), channel_id=1, source_target_pairs={{0,8},{8,0},{16,24},{24,16},{32,40},{40,32},{48,56},{56,48},{64,72... | collective-permute-start | bytes 3145736 | tf_op jit(solution)/shard_map/ppermute | solution.py:431
  58.1 4.2 %collective-permute-start.5 = (bf16[8,32,2048]{2,1,0:T(8,128)(2,1)S(1)}, bf16[8,32,2048]{2,1,0:T(8,128)(2,1)S(1)}, u32[]{:S(2)}, u32[]{:S(2)}) collective-permute-start(bf16[8,32,2048]{2,1,0:T(8,128)(2,1)S(1)} %get-tuple-element.11.near), channel_id=1, source_target_pairs={{0,8},{8,0},{16,24},{24,16},{32,40},{40,32},{48,56},{56,48},{64,72... | collective-permute-start | bytes 3145736 | tf_op jit(solution)/shard_map/ppermute | solution.py:434
  58.4 4.0 %copy-start.3 = (bf16[1024,1024]{1,0:T(8,128)(2,1)S(1)}, bf16[1024,1024]{1,0:T(8,128)(2,1)}, u32[]{:S(2)}) copy-start(bf16[1024,1024]{1,0:T(8,128)(2,1)} %constant.20.clone.lag_odd) | copy-start | bytes 6291460
  58.4 4.0 %copy-start.4 = (bf16[1024,1024]{1,0:T(8,128)(2,1)S(1)}, bf16[1024,1024]{1,0:T(8,128)(2,1)}, u32[]{:S(2)}) copy-start(bf16[1024,1024]{1,0:T(8,128)(2,1)} %constant.19.clone.lag_even) | copy-start | bytes 6291460

commit v6 on v5

--- a/solution.py
+++ b/solution.py
@@ -280,9 +280,10 @@
         for chunk in range(8):
             re = held[real_group(chunk), at] * (1.0 / 16.0)
             im = held[real_group(chunk) + 2, at] * (1.0 / 16.0)
-            own[window, 3 * chunk] = re
-            own[window, 3 * chunk + 1] = jnp.where(first, im, im - re) if chunk == 1 else im - re
-            own[window, 3 * chunk + 2] = im + re
+            own[window, 3 * chunk, :8] = re
+            less = jnp.where(first, im, im - re) if chunk == 1 else im - re
+            own[window, 3 * chunk + 1, :8] = less
+            own[window, 3 * chunk + 2, :8] = im + re
         return carry
 
     lax.fori_loop(0, 16, arrange, 0, unroll=2)
@@ -336,14 +337,14 @@
 
 def round_cross(raw, cross):
     for g in range(16):
-        cross[:, 128 * g : 128 * g + 128] = raw[g].astype(BF)
+        cross[:, 128 * g : 128 * g + 128] = raw[g, :128].astype(BF)
 
 
 def cross_tiles(near, far, own, raw, cross):
     for tile in range(2):
         cross_block(tile, near, far, own, raw)
         for g in range(16):
-            cross[128 * tile : 128 * tile + 128, 128 * g : 128 * g + 128] = raw[g].astype(BF)
+            cross[128 * tile : 128 * tile + 128, 128 * g : 128 * g + 128] = raw[g, :128].astype(BF)
 
 
 def lag_products(half, cross, lag_even, lag_odd, out, stage, sems):
@@ -377,7 +378,7 @@
         out_shape=jax.ShapeDtypeStruct((256, 2048), BF),
         in_specs=[VMEM] * 3,
         out_specs=VMEM,
-        scratch_shapes=[pltpu.VMEM((16, 128, 128), F32)],
+        scratch_shapes=[pltpu.VMEM((16, 136, 128), F32)],
         compiler_params=PARAMS,
         cost_estimate=cost(2**32, 9 * 2**20),
     )(near, far, own)
@@ -398,7 +399,7 @@
         in_specs=[VMEM] * 6,
         out_specs=ANYWHERE,
         scratch_shapes=[
-            pltpu.VMEM((16, 128, 128), F32),
+            pltpu.VMEM((16, 136, 128), F32),
             pltpu.VMEM((256, 2048), BF),
             pltpu.VMEM((2, 32, 8, 2048), F32),
             pltpu.SemaphoreType.DMA((2, 2 * PIECES)),
@@ -426,7 +427,7 @@
     tables = [jnp.asarray(t) for t in (deinterleave(), *forward_tables())]
     lag = [jnp.asarray(t) for t in lag_tables()]
     panel = jax.ShapeDtypeStruct((8, 32, 2048), BF)
-    mine = jax.ShapeDtypeStruct((16, 24, 8, 128), F32)
+    mine = jax.ShapeDtypeStruct((16, 24, 16, 128), F32)
     (near_0,) = white_call(first_white_kernel, 256, [panel], [*tables, rows])
     far_0 = swap(near_0)
     held = [pltpu.VMEM((16, 128, 128), F32)]

time: 70 us -> 69.9 us (level)
  no operation moved by 1% of the time
where the time goes in v6:
time: 69.9 us; the launch traced here: 69.6 us
  starting transfers between devices  22.5 us (32%)
  blocking collectives  19.3 us (28%)
  Pallas kernels  18.5 us (26%)
  waiting for transfers between devices  8.07 us (12%)
  local copies, waits for them, and re-layouts  0.8 us (1%)
    all_to_all x1, blocking collectives, local(): rows = lax.all_to_all(picked, 'stack', 0, 0, tiled=True)  19.3 us
    all_to_all x1, starting transfers between devices, local(): lax.all_to_all(spread(strain, swap(strain)), 'chan', 0, 0, tiled=True, ax...  7.49 us
    pallas_call x1, Pallas kernels, correlate(): pl.pallas_call(last_kernel, out_shape=jax.ShapeDtypeStruct((64, 8, 2048),...  7.16 us
    pallas_call x2, Pallas kernels, white_call(): pl.pallas_call(kernel, out_shape=shapes, in_specs=[VMEM] * len(operands),...  5.23 us
    ppermute x1, starting transfers between devices, local(): far_0 = swap(near_0)  5.01 us
    ppermute x3, waiting for transfers between devices, local(): everyone.append(lax.ppermute(shared, ('chan', 'stack'), pairs))  4.7 us
    ppermute x3, starting transfers between devices, local(): everyone.append(lax.ppermute(shared, ('chan', 'stack'), pairs))  4.01 us
    pallas_call x1, Pallas kernels, first_cross(): pl.pallas_call(first_cross_kernel, out_shape=jax.ShapeDtypeStruct((256, 2...  3.93 us
  transfers between devices with their start and end apart: 8, of which 5 were waited for; matrix products, arithmetic and copies ran while one was open for 0% of the time, Pallas kernels for 10%

profile of v6, /device:TPU:1, one launch (start us, length us, event | category | flops | bytes accessed | tf_op | source)
XLA Modules:
  0.0 69.6 jit_solution(1339320074732808931)
XLA Ops:
  0.0 3.2 %collective-permute-start = (bf16[16,8,128]{2,1,0:T(8,128)(2,1)}, bf16[16,8,128]{2,1,0:T(8,128)(2,1)S(1)}, u32[]{:S(2)}, u32[]{:S(2)}) collective-permute-start(bf16[16,8,128]{2,1,0:T(8,128)(2,1)} %strain.3), channel_id=1, source_target_pairs={{0,8},{8,0},{16,24},{24,16},{32,40},{40,32},{48,56},{56,48},{64,72... | collective-permute-start | bytes 98312 | tf_op jit(solution)/shard_map/ppermute | solution.py:416
  3.2 1.1 %collective-permute-done.theirs = bf16[16,8,128]{2,1,0:T(8,128)(2,1)S(1)} collective-permute-done((bf16[16,8,128]{2,1,0:T(8,128)(2,1)}, bf16[16,8,128]{2,1,0:T(8,128)(2,1)S(1)}, u32[]{:S(2)}, u32[]{:S(2)}) %collective-permute-start) | collective-permute-done | bytes 32800 | tf_op jit(solution)/shard_map/ppermute | solution.py:416
  4.3 0.8 %copy-done = bf16[16,8,128]{2,1,0:T(8,128)(2,1)S(1)} copy-done((bf16[16,8,128]{2,1,0:T(8,128)(2,1)S(1)}, bf16[16,8,128]{2,1,0:T(8,128)(2,1)}, u32[]{:S(2)}) %copy-start) | copy-done | bytes 32792
  5.1 1.1 %shard_map.91 = bf16[16,2,8,8,128]{4,3,2,1,0:T(8,128)(2,1)} custom-call(bf16[16,8,128]{2,1,0:T(8,128)(2,1)S(1)} %copy-done, bf16[16,8,128]{2,1,0:T(8,128)(2,1)S(1)} %collective-permute-done.theirs), custom_call_target="tpu_custom_call" | custom-call | flops 4294967296 | bytes 1048576 | tf_op jit(solution)/shard_map/pallas_call | solution.py:109
  6.1 7.5 %all-to-all-start = ((bf16[16,2,8,8,128]{4,3,2,1,0:T(8,128)(2,1)}), bf16[16,2,8,8,128]{4,3,2,1,0:T(8,128)(2,1)S(1)}, u32[]{:S(2)}, u32[]{:S(2)}) async-start(bf16[16,2,8,8,128]{4,3,2,1,0:T(8,128)(2,1)} %shard_map.91), calls=%async_computation | async-start | bytes 1048576 | tf_op jit(solution)/shard_map/all_to_all | solution.py:415
  13.7 0.1 shard_map.92.first
  13.7 2.5 %collective-permute-start.1 = (bf16[18,8,128]{2,1,0:T(8,128)(2,1)S(1)}, bf16[18,8,128]{2,1,0:T(8,128)(2,1)S(1)}, u32[]{:S(2)}, u32[]{:S(2)}) collective-permute-start(bf16[18,8,128]{2,1,0:T(8,128)(2,1)S(1)} %shard_map.92.first), channel_id=1, source_target_pairs={{0,4},{1,5},{2,6},{3,7},{4,0},{5,1},{6,2},{7,3},{8,12},{9,13},{10,... | collective-permute-start | bytes 110600 | tf_op jit(solution)/shard_map/ppermute | solution.py:419
  16.2 2.0 %collective-permute-done.1.second = bf16[18,8,128]{2,1,0:T(8,128)(2,1)S(1)} collective-permute-done((bf16[18,8,128]{2,1,0:T(8,128)(2,1)S(1)}, bf16[18,8,128]{2,1,0:T(8,128)(2,1)S(1)}, u32[]{:S(2)}, u32[]{:S(2)}) %collective-permute-start.1) | collective-permute-done | bytes 36896 | tf_op jit(solution)/shard_map/ppermute | solution.py:419
  18.2 0.0 copy-start.6
  18.2 0.0 copy-start.9
  18.2 1.4 %collective-permute-start.4 = (bf16[36,8,128]{2,1,0:T(8,128)(2,1)S(1)}, bf16[36,8,128]{2,1,0:T(8,128)(2,1)S(1)}, u32[]{:S(2)}, u32[]{:S(2)}) collective-permute-start(bf16[36,8,128]{2,1,0:T(8,128)(2,1)S(1)} %shard_map.93.rest_0_), channel_id=1, source_target_pairs={{0,3},{1,2},{2,1},{3,0},{4,7},{5,6},{6,5},{7,4},{8,9},{9,8},{10,11... | collective-permute-start | bytes 221192 | tf_op jit(solution)/shard_map/ppermute | solution.py:424
  19.6 2.6 %collective-permute-start.3 = (bf16[36,8,128]{2,1,0:T(8,128)(2,1)S(1)}, bf16[36,8,128]{2,1,0:T(8,128)(2,1)S(1)}, u32[]{:S(2)}, u32[]{:S(2)}) collective-permute-start(bf16[36,8,128]{2,1,0:T(8,128)(2,1)S(1)} %shard_map.93.rest_0_), channel_id=1, source_target_pairs={{0,2},{1,3},{2,0},{3,1},{4,6},{5,7},{6,4},{7,5},{8,10},{9,11},{10,... | collective-permute-start | bytes 221192 | tf_op jit(solution)/shard_map/ppermute | solution.py:424
  22.3 0.0 collective-permute-start.2
  22.3 0.0 collective-permute-done.4.rest_3_
  22.3 2.8 %collective-permute-done.3.rest_2_ = bf16[36,8,128]{2,1,0:T(8,128)(2,1)S(1)} collective-permute-done((bf16[36,8,128]{2,1,0:T(8,128)(2,1)S(1)}, bf16[36,8,128]{2,1,0:T(8,128)(2,1)S(1)}, u32[]{:S(2)}, u32[]{:S(2)}) %collective-permute-start.3) | collective-permute-done | bytes 73760 | tf_op jit(solution)/shard_map/ppermute | solution.py:424
  25.1 1.9 %collective-permute-done.2.rest_1_ = bf16[36,8,128]{2,1,0:T(8,128)(2,1)S(1)} collective-permute-done((bf16[36,8,128]{2,1,0:T(8,128)(2,1)S(1)}, bf16[36,8,128]{2,1,0:T(8,128)(2,1)S(1)}, u32[]{:S(2)}, u32[]{:S(2)}) %collective-permute-start.2) | collective-permute-done | bytes 73760 | tf_op jit(solution)/shard_map/ppermute | solution.py:424
  27.0 0.3 all-to-all-done.window_rows
  27.3 1.1 %shard_map.94 = (bf16[8,512,128]{2,1,0:T(8,128)(2,1)S(1)}, bf16[8,16,8,128]{3,2,1,0:T(8,128)(2,1)S(1)}) custom-call(bf16[16,2,8,8,128]{4,3,2,1,0:T(8,128)(2,1)S(1)} %all-to-all-done.window_rows, bf16[36,8,128]{2,1,0:T(8,128)(2,1)S(1)} %shard_map.93.rest_0_, bf16[36,8,128]{2,1,0:T(8,128)(2,1)S(1)} %collective-permute-done.2.rest_1_, ...), custom_call_target="tpu_custom_call" | custom-call | flops 8589934592 | bytes 1048576 | tf_op jit(solution)/shard_map/pallas_call | solution.py:182
  28.4 19.3 %all_to_all.10.refs_4_ = bf16[8,512,128]{2,1,0:T(8,128)(2,1)S(1)} all-to-all(bf16[8,512,128]{2,1,0:T(8,128)(2,1)S(1)} %get-tuple-element.9), channel_id=1, replica_groups=mesh['chan'=32,'stack'=8] {'stack'}, dimensions={0} | all-to-all | bytes 2097152 | tf_op jit(solution)/shard_map/all_to_all | solution.py:426
  47.7 0.0 copy-done.6
  47.7 2.1 %shard_map.96.near = bf16[8,32,2048]{2,1,0:T(8,128)(2,1)S(1)} custom-call(bf16[256,256]{1,0:T(8,128)(2,1)S(1)} %copy-done.9, bf16[512,1024]{1,0:T(8,128)(2,1)S(1)} %copy-done.8, bf16[512,1024]{1,0:T(8,128)(2,1)S(1)} %copy-done.7, bf16[512,1024]{1,0:T(8,128)(2,1)S(1)} %copy-done.6, bf16[512,1024]{1,0:T(8,128)(2,1)S(1)} %copy-done.5, ...), custom_call_target="tpu_custom_call" | custom-call | flops 2147483648 | bytes 6291456 | tf_op jit(solution)/shard_map/pallas_call | solution.py:298
  49.8 5.0 %collective-permute-start.6 = (bf16[8,32,2048]{2,1,0:T(8,128)(2,1)S(1)}, bf16[8,32,2048]{2,1,0:T(8,128)(2,1)S(1)}, u32[]{:S(2)}, u32[]{:S(2)}) collective-permute-start(bf16[8,32,2048]{2,1,0:T(8,128)(2,1)S(1)} %shard_map.96.near), channel_id=1, source_target_pairs={{0,8},{8,0},{16,24},{24,16},{32,40},{40,32},{48,56},{56,48},{64,72... | collective-permute-start | bytes 3145736 | tf_op jit(solution)/shard_map/ppermute | solution.py:432
  54.8 3.2 %shard_map.95 = (bf16[8,32,2048]{2,1,0:T(8,128)(2,1)S(1)}, f32[16,24,16,128]{3,2,1,0:T(8,128)S(1)}) custom-call(bf16[256,256]{1,0:T(8,128)(2,1)S(1)} %copy-done.9, bf16[512,1024]{1,0:T(8,128)(2,1)S(1)} %copy-done.8, bf16[512,1024]{1,0:T(8,128)(2,1)S(1)} %copy-done.7, bf16[512,1024]{1,0:T(8,128)(2,1)S(1)} %copy-done.6, bf16[512,1024]{1,0:T(8,128)(2,1)S(1)} %copy-done.5, ...), custom_call_target="tpu_custom_call" | custom-call | flops 3221225472 | bytes 7340032 | tf_op jit(solution)/shard_map/pallas_call | solution.py:298
  58.0 0.3 collective-permute-start.5
  58.3 0.0 collective-permute-done.6.far
  58.3 0.0 copy-start.3
  58.3 0.0 copy-start.4
  58.3 3.9 %shard_map.97.before = bf16[256,2048]{1,0:T(8,128)(2,1)S(1)} custom-call(bf16[8,32,2048]{2,1,0:T(8,128)(2,1)S(1)} %shard_map.96.near, bf16[8,32,2048]{2,1,0:T(8,128)(2,1)S(1)} %collective-permute-done.6.far, f32[16,24,16,128]{3,2,1,0:T(8,128)S(1)} %get-tuple-element.12.own), custom_call_target="tpu_custom_call" | custom-call | flops 4294967296 | bytes 9437184 | tf_op jit(solution)/shard_map/pallas_call | solution.py:376
  62.2 0.0 collective-permute-done.5.far
  62.2 0.0 copy-done.3
  62.3 0.0 copy-done.4
  62.3 7.2 %shard_map.98 = f32[64,8,2048]{2,1,0:T(8,128)} custom-call(bf16[8,32,2048]{2,1,0:T(8,128)(2,1)S(1)} %get-tuple-element.11.near, bf16[8,32,2048]{2,1,0:T(8,128)(2,1)S(1)} %collective-permute-done.5.far, f32[16,24,16,128]{3,2,1,0:T(8,128)S(1)} %get-tuple-element.12.own, bf16[1024,1024]{1,0:T(8,128)(2,1)S(1)} %copy-done.4, bf16[1024,1024]{1,0:T(8,128)(2,1)S(1)} %copy-done.3, ...), custom_call_target="tpu_custom_call" | custom-call | flops 8589934592 | bytes 9437184 | tf_op jit(solution)/shard_map/pallas_call | solution.py:396
  (13 shorter events, 0.0 us)
Async XLA Ops:
  0.0 4.3 %collective-permute-start = (bf16[16,8,128]{2,1,0:T(8,128)(2,1)}, bf16[16,8,128]{2,1,0:T(8,128)(2,1)S(1)}, u32[]{:S(2)}, u32[]{:S(2)}) collective-permute-start(bf16[16,8,128]{2,1,0:T(8,128)(2,1)} %strain.3), channel_id=1, source_target_pairs={{0,8},{8,0},{16,24},{24,16},{32,40},{40,32},{48,56},{56,48},{64,72... | collective-permute-start | bytes 98312 | tf_op jit(solution)/shard_map/ppermute | solution.py:416
  4.3 0.8 %copy-start = (bf16[16,8,128]{2,1,0:T(8,128)(2,1)S(1)}, bf16[16,8,128]{2,1,0:T(8,128)(2,1)}, u32[]{:S(2)}) copy-start(bf16[16,8,128]{2,1,0:T(8,128)(2,1)} %strain.3) | copy-start | bytes 98308
  5.1 8.6 %copy-start.1 = (bf16[16,8,128]{2,1,0:T(8,128)(2,1)S(1)}, bf16[16,8,128]{2,1,0:T(8,128)(2,1)}, u32[]{:S(2)}) copy-start(bf16[16,8,128]{2,1,0:T(8,128)(2,1)} %strain.3) | copy-start | bytes 98308
  5.1 8.6 %copy-start.2 = (s32[16,64]{1,0:T(8,128)S(1)}, s32[16,64]{1,0:T(8,128)}, u32[]{:S(2)}) copy-start(s32[16,64]{1,0:T(8,128)} %sources.1) | copy-start | bytes 12292
  6.1 21.1 %all-to-all-start = ((bf16[16,2,8,8,128]{4,3,2,1,0:T(8,128)(2,1)}), bf16[16,2,8,8,128]{4,3,2,1,0:T(8,128)(2,1)S(1)}, u32[]{:S(2)}, u32[]{:S(2)}) async-start(bf16[16,2,8,8,128]{4,3,2,1,0:T(8,128)(2,1)} %shard_map.91), calls=%async_computation | async-start | bytes 1048576 | tf_op jit(solution)/shard_map/all_to_all | solution.py:415
  13.7 4.5 %collective-permute-start.1 = (bf16[18,8,128]{2,1,0:T(8,128)(2,1)S(1)}, bf16[18,8,128]{2,1,0:T(8,128)(2,1)S(1)}, u32[]{:S(2)}, u32[]{:S(2)}) collective-permute-start(bf16[18,8,128]{2,1,0:T(8,128)(2,1)S(1)} %shard_map.92.first), channel_id=1, source_target_pairs={{0,4},{1,5},{2,6},{3,7},{4,0},{5,1},{6,2},{7,3},{8,12},{9,13},{10,... | collective-permute-start | bytes 110600 | tf_op jit(solution)/shard_map/ppermute | solution.py:419
  18.2 29.5 %copy-start.5 = (bf16[512,1024]{1,0:T(8,128)(2,1)S(1)}, bf16[512,1024]{1,0:T(8,128)(2,1)}, u32[]{:S(2)}) copy-start(bf16[512,1024]{1,0:T(8,128)(2,1)} %constant.18.clone.refs_3_) | copy-start | bytes 3145732
  18.2 29.5 %copy-start.6 = (bf16[512,1024]{1,0:T(8,128)(2,1)S(1)}, bf16[512,1024]{1,0:T(8,128)(2,1)}, u32[]{:S(2)}) copy-start(bf16[512,1024]{1,0:T(8,128)(2,1)} %constant.17.clone.refs_2_) | copy-start | bytes 3145732
  18.2 29.5 %copy-start.9 = (bf16[256,256]{1,0:T(8,128)(2,1)S(1)}, bf16[256,256]{1,0:T(8,128)(2,1)}, u32[]{:S(2)}) copy-start(bf16[256,256]{1,0:T(8,128)(2,1)} %constant.14.clone.perm) | copy-start | bytes 393220
  18.2 4.0 %collective-permute-start.4 = (bf16[36,8,128]{2,1,0:T(8,128)(2,1)S(1)}, bf16[36,8,128]{2,1,0:T(8,128)(2,1)S(1)}, u32[]{:S(2)}, u32[]{:S(2)}) collective-permute-start(bf16[36,8,128]{2,1,0:T(8,128)(2,1)S(1)} %shard_map.93.rest_0_), channel_id=1, source_target_pairs={{0,3},{1,2},{2,1},{3,0},{4,7},{5,6},{6,5},{7,4},{8,9},{9,8},{10,11... | collective-permute-start | bytes 221192 | tf_op jit(solution)/shard_map/ppermute | solution.py:424
  19.6 5.4 %collective-permute-start.3 = (bf16[36,8,128]{2,1,0:T(8,128)(2,1)S(1)}, bf16[36,8,128]{2,1,0:T(8,128)(2,1)S(1)}, u32[]{:S(2)}, u32[]{:S(2)}) collective-permute-start(bf16[36,8,128]{2,1,0:T(8,128)(2,1)S(1)} %shard_map.93.rest_0_), channel_id=1, source_target_pairs={{0,2},{1,3},{2,0},{3,1},{4,6},{5,7},{6,4},{7,5},{8,10},{9,11},{10,... | collective-permute-start | bytes 221192 | tf_op jit(solution)/shard_map/ppermute | solution.py:424
  22.3 4.7 %collective-permute-start.2 = (bf16[36,8,128]{2,1,0:T(8,128)(2,1)S(1)}, bf16[36,8,128]{2,1,0:T(8,128)(2,1)S(1)}, u32[]{:S(2)}, u32[]{:S(2)}) collective-permute-start(bf16[36,8,128]{2,1,0:T(8,128)(2,1)S(1)} %shard_map.93.rest_0_), channel_id=1, source_target_pairs={{0,1},{1,0},{2,3},{3,2},{4,5},{5,4},{6,7},{7,6},{8,11},{9,10},{10,... | collective-permute-start | bytes 221192 | tf_op jit(solution)/shard_map/ppermute | solution.py:424
  27.3 20.5 %copy-start.7 = (bf16[512,1024]{1,0:T(8,128)(2,1)S(1)}, bf16[512,1024]{1,0:T(8,128)(2,1)}, u32[]{:S(2)}) copy-start(bf16[512,1024]{1,0:T(8,128)(2,1)} %constant.16.clone.refs_1_) | copy-start | bytes 3145732
  27.3 20.5 %copy-start.8 = (bf16[512,1024]{1,0:T(8,128)(2,1)S(1)}, bf16[512,1024]{1,0:T(8,128)(2,1)}, u32[]{:S(2)}) copy-start(bf16[512,1024]{1,0:T(8,128)(2,1)} %constant.15.clone.refs_0_) | copy-start | bytes 3145732
  49.8 8.5 %collective-permute-start.6 = (bf16[8,32,2048]{2,1,0:T(8,128)(2,1)S(1)}, bf16[8,32,2048]{2,1,0:T(8,128)(2,1)S(1)}, u32[]{:S(2)}, u32[]{:S(2)}) collective-permute-start(bf16[8,32,2048]{2,1,0:T(8,128)(2,1)S(1)} %shard_map.96.near), channel_id=1, source_target_pairs={{0,8},{8,0},{16,24},{24,16},{32,40},{40,32},{48,56},{56,48},{64,72... | collective-permute-start | bytes 3145736 | tf_op jit(solution)/shard_map/ppermute | solution.py:432
  58.0 4.3 %collective-permute-start.5 = (bf16[8,32,2048]{2,1,0:T(8,128)(2,1)S(1)}, bf16[8,32,2048]{2,1,0:T(8,128)(2,1)S(1)}, u32[]{:S(2)}, u32[]{:S(2)}) collective-permute-start(bf16[8,32,2048]{2,1,0:T(8,128)(2,1)S(1)} %get-tuple-element.11.near), channel_id=1, source_target_pairs={{0,8},{8,0},{16,24},{24,16},{32,40},{40,32},{48,56},{56,48},{64,72... | collective-permute-start | bytes 3145736 | tf_op jit(solution)/shard_map/ppermute | solution.py:435
  58.3 4.0 %copy-start.3 = (bf16[1024,1024]{1,0:T(8,128)(2,1)S(1)}, bf16[1024,1024]{1,0:T(8,128)(2,1)}, u32[]{:S(2)}) copy-start(bf16[1024,1024]{1,0:T(8,128)(2,1)} %constant.20.clone.lag_odd) | copy-start | bytes 6291460
  58.3 4.0 %copy-start.4 = (bf16[1024,1024]{1,0:T(8,128)(2,1)S(1)}, bf16[1024,1024]{1,0:T(8,128)(2,1)}, u32[]{:S(2)}) copy-start(bf16[1024,1024]{1,0:T(8,128)(2,1)} %constant.19.clone.lag_even) | copy-start | bytes 6291460
